TPU v7x, 512 devices: a whole 4x4x16 slice. The times are simulated.
512 devices in a mesh: seq: 32 (over x, y, core), key: 16 (over z).
Axes of the slice: x: 4, y: 4, z: 16, core: 2. Of those that a mesh axis runs over, the one named last changes fastest.
Arguments:
- query_rows: bfloat16 [8192, 16, 256], P('seq', None, 'key'), may hold values from -0.375 to 0.375
- key_rows: bfloat16 [8192, 16, 256], P('seq', None, 'key'), may hold values from -0.1875 to 0.1875
- value_rows: bfloat16 [8192, 16, 256], P('seq', 'key'), may hold values from -6 to 6
- out_grad: bfloat16 [8192, 16, 256], P('seq', 'key')
- log_gates: float32 [16, 8192], P('key', 'seq'), may hold values from -0.8 to 0, as said below
- write_rate: float32 [16, 8192], P('key', 'seq'), may hold values from 0.1 to 0.8
- group_inverse: bfloat16 [64, 16, 128, 128], P('seq', 'key'), as said below
- states: bfloat16 [64, 16, 256, 256], P('seq', None, 'key'), may hold values from -0.75 to 0.75
Outputs:
- grad_query: bfloat16 [8192, 16, 256], P('seq', None, 'key')
- grad_key: bfloat16 [8192, 16, 256], P('seq', None, 'key')
- grad_value: bfloat16 [8192, 16, 256], P('seq', 'key')
- grad_square: float32 [], replicated
Inputs may be any that keep to these rules, and one draw needn't show every extreme that they name: `group_inverse`: each group's matrix is unit lower triangular: ones on the diagonal, zeros above it. `log_gates`: every entry is the logarithm of a decay factor, never positive.
All inputs are finite; a program needn't handle non-finite values.
Results may differ from a plain program's by a relative error of at most 0.007.
Values may be sent and summed in bfloat16 or wider, within the bound.
No kernel may reach another device: no remote copies, remote signals or barrier semaphores. Data moves between devices by JAX's collectives and lax.ppermute only.
A program may use at most 128 MiB of HBM per device.

v0:
```python
import jax
import jax.numpy as jnp
from jax import lax
from jax.sharding import PartitionSpec as P

highest_mode = lax.Precision.HIGHEST


def from_behind(value, axis, steps):
    count = lax.axis_size(axis)
    first, last = (max(0, -steps), min(count, count - steps))
    return lax.ppermute(value, axis, [(source, source + steps) for source in range(first, last)])


def mixed_dot(form, left, right):
    return jnp.einsum(form, left, right, preferred_element_type=jnp.float32)


def precise_product(form, left, right):
    return jnp.einsum(form, left.astype(jnp.float32), right, precision=highest_mode)


def linear_part(state_in, write_block, key_block, decay_block):
    through = precise_product("thk,hkm->thm", key_block, state_in)
    return decay_block[:, None, None] * state_in - precise_product(
        "thk,thm->hkm", write_block, through
    )


def device_map(state_out, written_keys, key_result, end_decay, offset_term):

    def group_step(state_in, pieces):
        write_block, key_block, decay_block, offset_block = pieces
        return (linear_part(state_in, write_block, key_block, decay_block) + offset_block, state_in)

    return lax.scan(
        group_step, state_out, (written_keys, key_result, end_decay, offset_term), reverse=True
    )


def token_wise(factor):
    return jnp.transpose(factor, (0, 2, 1))[:, :, :, None]


def square_sum(array):
    return jnp.sum(jnp.square(array.astype(jnp.float32)))


def local(query_rows, key_rows, value_rows, out_grad, log_gates, write_rate, group_inverse, states):
    halfway_point = jnp.bfloat16
    query_heads, key_heads, state_heads = (
        lax.all_to_all(query_rows, "key", split_axis=1, concat_axis=2, tiled=True),
        lax.all_to_all(key_rows, "key", split_axis=1, concat_axis=2, tiled=True),
        lax.all_to_all(states, "key", split_axis=1, concat_axis=2, tiled=True),
    )
    group_count, head_local, group_len, _ = group_inverse.shape
    token_count, _, key_width = query_heads.shape
    value_width = value_rows.shape[2]
    query_blk = query_heads.reshape(group_count, group_len, head_local, key_width)
    key_blk = key_heads.reshape(group_count, group_len, head_local, key_width)
    value_blk = value_rows.reshape(group_count, group_len, head_local, value_width)
    grad_blk = out_grad.reshape(group_count, group_len, head_local, value_width)
    gate_blk = jnp.transpose(log_gates.reshape(head_local, group_count, group_len), (1, 0, 2))
    rate_blk = jnp.transpose(write_rate.reshape(head_local, group_count, group_len), (1, 0, 2))
    gamma = jnp.cumsum(gate_blk, axis=2)
    final_gamma_value = gamma[:, :, -1:]
    incoming_decay = jnp.exp(gamma)
    outgoing_decay = jnp.exp(final_gamma_value - gamma)
    row_ids = lax.broadcasted_iota(jnp.int32, (group_len, group_len), 0)
    col_ids = lax.broadcasted_iota(jnp.int32, (group_len, group_len), 1)
    lower = row_ids >= col_ids
    spread = gamma[:, :, :, None] - gamma[:, :, None, :]
    decay_mask = jnp.where(lower, jnp.exp(jnp.where(lower, spread, 0.0)), 0.0)
    key_scaled = (key_blk * token_wise(rate_blk * incoming_decay)).astype(halfway_point)
    written_keys = mixed_dot("nhts,nshk->nthk", group_inverse, key_scaled).astype(halfway_point)
    scaled_values = (value_blk * token_wise(rate_blk)).astype(halfway_point)
    fresh_values = (
        mixed_dot("nhts,nshv->nthv", group_inverse, scaled_values)
        - mixed_dot("nthk,nhkv->nthv", written_keys, state_heads)
    ).astype(halfway_point)
    score_mat = (mixed_dot("nthk,nshk->nhts", query_blk, key_blk) * decay_mask).astype(
        halfway_point
    )
    key_result = (key_blk * token_wise(outgoing_decay)).astype(halfway_point)
    incoming_query = (query_blk * token_wise(incoming_decay)).astype(halfway_point)
    inner_gradient = mixed_dot("nhts,nthv->nshv", score_mat, grad_blk)
    offset_term = mixed_dot("nthk,nthv->nhkv", incoming_query, grad_blk) - precise_product(
        "nthk,nthv->nhkv", written_keys, inner_gradient
    )
    end_decay = jnp.exp(final_gamma_value[:, :, 0])
    empty_state = jnp.zeros((head_local, key_width, value_width), jnp.float32)

    def relay_hop(hop_index, incoming):
        state_in, _ = device_map(incoming, written_keys, key_result, end_decay, offset_term)
        return from_behind(state_in, "seq", -1)

    state_out = lax.fori_loop(0, lax.axis_size("seq") - 1, relay_hop, empty_state)
    _, state_gradient = device_map(state_out, written_keys, key_result, end_decay, offset_term)
    value_rounding = (
        inner_gradient + precise_product("nthk,nhkv->nthv", key_result, state_gradient)
    ).astype(halfway_point)
    value_grad_blk = (
        token_wise(rate_blk) * mixed_dot("nhts,nthv->nshv", group_inverse, value_rounding)
    ).astype(halfway_point)
    score_gradient = (mixed_dot("nthv,nshv->nhts", grad_blk, fresh_values) * decay_mask).astype(
        halfway_point
    )
    write_gradient = (-mixed_dot("nthv,nhkv->nthk", value_rounding, state_heads)).astype(
        halfway_point
    )
    state_rounding = state_gradient.astype(halfway_point)
    query_grad_blk = (
        token_wise(incoming_decay) * mixed_dot("nthv,nhkv->nthk", grad_blk, state_heads)
        + mixed_dot("nhts,nshk->nthk", score_gradient, key_blk)
    ).astype(halfway_point)
    key_grad_blk = (
        mixed_dot("nhts,nthk->nshk", score_gradient, query_blk)
        + token_wise(outgoing_decay) * mixed_dot("nthv,nhkv->nthk", fresh_values, state_rounding)
        + token_wise(rate_blk * incoming_decay)
        * mixed_dot("nhts,nthk->nshk", group_inverse, write_gradient)
    ).astype(halfway_point)
    query_grad_heads = query_grad_blk.reshape(token_count, head_local, key_width)
    key_grad_heads = key_grad_blk.reshape(token_count, head_local, key_width)
    grad_value = value_grad_blk.reshape(token_count, head_local, value_width)
    grad_query, grad_key = (
        lax.all_to_all(query_grad_heads, "key", split_axis=2, concat_axis=1, tiled=True),
        lax.all_to_all(key_grad_heads, "key", split_axis=2, concat_axis=1, tiled=True),
    )
    value_square = square_sum(grad_value)
    partial_value = square_sum(grad_query) + square_sum(grad_key) + value_square
    summed = lax.psum(partial_value, ("seq", "key"))
    entries = (
        token_count * lax.axis_size("seq") * query_rows.shape[1] * (2 * key_width + value_width)
    )
    return (grad_query, grad_key, grad_value, summed / entries)


def solution(mesh):
    in_specs = (
        P("seq", None, "key"),
        P("seq", None, "key"),
        P("seq", "key", None),
        P("seq", "key", None),
        P("key", "seq"),
        P("key", "seq"),
        P("seq", "key", None, None),
        P("seq", None, "key", None),
    )
    out_specs = (P("seq", None, "key"), P("seq", None, "key"), P("seq", "key", None), P())
    return jax.shard_map(local, mesh=mesh, in_specs=in_specs, out_specs=out_specs, check_vma=False)
```

profile of v0, /device:TPU:1, one launch (start us, length us, event | category | flops | bytes accessed | tf_op | source)
XLA Modules:
  0.0 631.2 jit_solution(10819537718962490288)
XLA Ops:
  0.7 15.9 %all-to-all-start.1 = ((bf16[256,16,16]{0,2,1:T(8,128)(2,1)}), bf16[256,16,16]{0,2,1:T(8,128)(2,1)S(1)}, u32[]{:S(2)}, u32[]{:S(2)}) async-start(bf16[256,16,16]{0,2,1:T(8,128)(2,1)} %param.15), calls=%async_computation.1 | async-start | bytes 262144 | tf_op jit(solution)/shard_map/all_to_all | solution.py:53
  17.9 10.7 %all-to-all-done.1 = bf16[256,16,16]{0,2,1:T(8,128)(2,1)S(1)} async-done(((bf16[256,16,16]{0,2,1:T(8,128)(2,1)}), bf16[256,16,16]{0,2,1:T(8,128)(2,1)S(1)}, u32[]{:S(2)}, u32[]{:S(2)}) %all-to-all-start.1) | async-done | bytes 131104 | tf_op jit(solution)/shard_map/all_to_all | solution.py:53
  36.8 9.7 %all-to-all-done.3 = bf16[256,16,16]{0,2,1:T(8,128)(2,1)S(1)} async-done(((bf16[256,16,16]{0,2,1:T(8,128)(2,1)}), bf16[256,16,16]{0,2,1:T(8,128)(2,1)S(1)}, u32[]{:S(2)}, u32[]{:S(2)}) %all-to-all-start.3) | async-done | bytes 131104 | tf_op jit(solution)/shard_map/all_to_all | solution.py:52
  54.0 393.7 %while.57 = (s32[]{:T(128)}, f32[1,256,256]{2,1,0:T(8,128)S(1)}, f32[2,1]{0,1:T(1,128)S(1)}, bf16[2,128,1,256]{3,1,2,0:T(8,128)(2,1)S(1)}, bf16[2,128,1,256]{3,1...) while((s32[]{:T(128)}, f32[1,256,256]{2,1,0:T(8,128)S(1)}, ...), condition=%wide.region_4.5_spmd, body=%wide.region_1.4_spmd.sunk | while | flops 201523200 | bytes 3015986 | solution.py:97
  222.6 7.9 %collective-permute-done = f32[1,256,256]{2,1,0:T(8,128)S(1)} collective-permute-done((f32[1,256,256]{2,1,0:T(8,128)S(1)}, f32[1,256,256]{2,1,0:T(8,128)S(1)}, u32[]{:S(2)}, u32[]{:S(2)}) %collective-permute-start) | collective-permute-done | bytes 262176 | tf_op jit(solution)/shard_map/while/body/eval_jaxpr/ppermute | solution.py:12
  236.2 7.9 %collective-permute-done = f32[1,256,256]{2,1,0:T(8,128)S(1)} collective-permute-done((f32[1,256,256]{2,1,0:T(8,128)S(1)}, f32[1,256,256]{2,1,0:T(8,128)S(1)}, u32[]{:S(2)}, u32[]{:S(2)}) %collective-permute-start) | collective-permute-done | bytes 262176 | tf_op jit(solution)/shard_map/while/body/eval_jaxpr/ppermute | solution.py:12
  249.8 7.9 %collective-permute-done = f32[1,256,256]{2,1,0:T(8,128)S(1)} collective-permute-done((f32[1,256,256]{2,1,0:T(8,128)S(1)}, f32[1,256,256]{2,1,0:T(8,128)S(1)}, u32[]{:S(2)}, u32[]{:S(2)}) %collective-permute-start) | collective-permute-done | bytes 262176 | tf_op jit(solution)/shard_map/while/body/eval_jaxpr/ppermute | solution.py:12
  263.4 7.9 %collective-permute-done = f32[1,256,256]{2,1,0:T(8,128)S(1)} collective-permute-done((f32[1,256,256]{2,1,0:T(8,128)S(1)}, f32[1,256,256]{2,1,0:T(8,128)S(1)}, u32[]{:S(2)}, u32[]{:S(2)}) %collective-permute-start) | collective-permute-done | bytes 262176 | tf_op jit(solution)/shard_map/while/body/eval_jaxpr/ppermute | solution.py:12
  276.9 7.9 %collective-permute-done = f32[1,256,256]{2,1,0:T(8,128)S(1)} collective-permute-done((f32[1,256,256]{2,1,0:T(8,128)S(1)}, f32[1,256,256]{2,1,0:T(8,128)S(1)}, u32[]{:S(2)}, u32[]{:S(2)}) %collective-permute-start) | collective-permute-done | bytes 262176 | tf_op jit(solution)/shard_map/while/body/eval_jaxpr/ppermute | solution.py:12
  290.5 7.9 %collective-permute-done = f32[1,256,256]{2,1,0:T(8,128)S(1)} collective-permute-done((f32[1,256,256]{2,1,0:T(8,128)S(1)}, f32[1,256,256]{2,1,0:T(8,128)S(1)}, u32[]{:S(2)}, u32[]{:S(2)}) %collective-permute-start) | collective-permute-done | bytes 262176 | tf_op jit(solution)/shard_map/while/body/eval_jaxpr/ppermute | solution.py:12
  304.1 7.9 %collective-permute-done = f32[1,256,256]{2,1,0:T(8,128)S(1)} collective-permute-done((f32[1,256,256]{2,1,0:T(8,128)S(1)}, f32[1,256,256]{2,1,0:T(8,128)S(1)}, u32[]{:S(2)}, u32[]{:S(2)}) %collective-permute-start) | collective-permute-done | bytes 262176 | tf_op jit(solution)/shard_map/while/body/eval_jaxpr/ppermute | solution.py:12
  317.7 7.9 %collective-permute-done = f32[1,256,256]{2,1,0:T(8,128)S(1)} collective-permute-done((f32[1,256,256]{2,1,0:T(8,128)S(1)}, f32[1,256,256]{2,1,0:T(8,128)S(1)}, u32[]{:S(2)}, u32[]{:S(2)}) %collective-permute-start) | collective-permute-done | bytes 262176 | tf_op jit(solution)/shard_map/while/body/eval_jaxpr/ppermute | solution.py:12
  331.2 7.9 %collective-permute-done = f32[1,256,256]{2,1,0:T(8,128)S(1)} collective-permute-done((f32[1,256,256]{2,1,0:T(8,128)S(1)}, f32[1,256,256]{2,1,0:T(8,128)S(1)}, u32[]{:S(2)}, u32[]{:S(2)}) %collective-permute-start) | collective-permute-done | bytes 262176 | tf_op jit(solution)/shard_map/while/body/eval_jaxpr/ppermute | solution.py:12
  344.8 7.9 %collective-permute-done = f32[1,256,256]{2,1,0:T(8,128)S(1)} collective-permute-done((f32[1,256,256]{2,1,0:T(8,128)S(1)}, f32[1,256,256]{2,1,0:T(8,128)S(1)}, u32[]{:S(2)}, u32[]{:S(2)}) %collective-permute-start) | collective-permute-done | bytes 262176 | tf_op jit(solution)/shard_map/while/body/eval_jaxpr/ppermute | solution.py:12
  358.4 7.9 %collective-permute-done = f32[1,256,256]{2,1,0:T(8,128)S(1)} collective-permute-done((f32[1,256,256]{2,1,0:T(8,128)S(1)}, f32[1,256,256]{2,1,0:T(8,128)S(1)}, u32[]{:S(2)}, u32[]{:S(2)}) %collective-permute-start) | collective-permute-done | bytes 262176 | tf_op jit(solution)/shard_map/while/body/eval_jaxpr/ppermute | solution.py:12
  372.0 7.9 %collective-permute-done = f32[1,256,256]{2,1,0:T(8,128)S(1)} collective-permute-done((f32[1,256,256]{2,1,0:T(8,128)S(1)}, f32[1,256,256]{2,1,0:T(8,128)S(1)}, u32[]{:S(2)}, u32[]{:S(2)}) %collective-permute-start) | collective-permute-done | bytes 262176 | tf_op jit(solution)/shard_map/while/body/eval_jaxpr/ppermute | solution.py:12
  385.5 7.9 %collective-permute-done = f32[1,256,256]{2,1,0:T(8,128)S(1)} collective-permute-done((f32[1,256,256]{2,1,0:T(8,128)S(1)}, f32[1,256,256]{2,1,0:T(8,128)S(1)}, u32[]{:S(2)}, u32[]{:S(2)}) %collective-permute-start) | collective-permute-done | bytes 262176 | tf_op jit(solution)/shard_map/while/body/eval_jaxpr/ppermute | solution.py:12
  412.7 7.9 %collective-permute-done = f32[1,256,256]{2,1,0:T(8,128)S(1)} collective-permute-done((f32[1,256,256]{2,1,0:T(8,128)S(1)}, f32[1,256,256]{2,1,0:T(8,128)S(1)}, u32[]{:S(2)}, u32[]{:S(2)}) %collective-permute-start) | collective-permute-done | bytes 262176 | tf_op jit(solution)/shard_map/while/body/eval_jaxpr/ppermute | solution.py:12
  426.2 7.9 %collective-permute-done = f32[1,256,256]{2,1,0:T(8,128)S(1)} collective-permute-done((f32[1,256,256]{2,1,0:T(8,128)S(1)}, f32[1,256,256]{2,1,0:T(8,128)S(1)}, u32[]{:S(2)}, u32[]{:S(2)}) %collective-permute-start) | collective-permute-done | bytes 262176 | tf_op jit(solution)/shard_map/while/body/eval_jaxpr/ppermute | solution.py:12
  439.8 7.9 %collective-permute-done = f32[1,256,256]{2,1,0:T(8,128)S(1)} collective-permute-done((f32[1,256,256]{2,1,0:T(8,128)S(1)}, f32[1,256,256]{2,1,0:T(8,128)S(1)}, u32[]{:S(2)}, u32[]{:S(2)}) %collective-permute-start) | collective-permute-done | bytes 262176 | tf_op jit(solution)/shard_map/while/body/eval_jaxpr/ppermute | solution.py:12
  456.1 11.2 %all-to-all-start.4 = ((bf16[16,2,2048]{2,1,0:T(2,128)(2,1)}), bf16[16,2,2048]{2,1,0:T(2,128)(2,1)S(1)}, u32[]{:S(2)}, u32[]{:S(2)}) async-start(bf16[16,2,2048]{2,1,0:T(2,128)(2,1)} %reshape.369), calls=%async_computation.4 | async-start | bytes 262144 | tf_op jit(solution)/shard_map/all_to_all | solution.py:127
  470.0 9.2 %all-to-all-done.4 = bf16[16,2,2048]{2,1,0:T(2,128)(2,1)S(1)} async-done(((bf16[16,2,2048]{2,1,0:T(2,128)(2,1)}), bf16[16,2,2048]{2,1,0:T(2,128)(2,1)S(1)}, u32[]{:S(2)}, u32[]{:S(2)}) %all-to-all-start.4) | async-done | bytes 131104 | tf_op jit(solution)/shard_map/all_to_all | solution.py:127
  484.6 10.4 %all-to-all-done.2 = bf16[16,2,2048]{2,1,0:T(2,128)(2,1)S(1)} async-done(((bf16[16,2,2048]{2,1,0:T(2,128)(2,1)}), bf16[16,2,2048]{2,1,0:T(2,128)(2,1)S(1)}, u32[]{:S(2)}, u32[]{:S(2)}) %all-to-all-start.2) | async-done | bytes 131104 | tf_op jit(solution)/shard_map/all_to_all | solution.py:126
  498.3 129.8 %psum.7 = f32[]{:T(128)} all-reduce(f32[]{:T(128)S(6)} %add.89), channel_id=1, replica_groups=mesh['seq'=32,'key'=16] {'seq','key'}, use_global_device_ids=true, to_apply=%region_10.11 | all-reduce | flops 1 | bytes 8 | tf_op jit(solution)/shard_map/psum | solution.py:131
  (363 shorter events, 420.2 us)
Async XLA Ops:
  0.7 27.9 %all-to-all-start.1 = ((bf16[256,16,16]{0,2,1:T(8,128)(2,1)}), bf16[256,16,16]{0,2,1:T(8,128)(2,1)S(1)}, u32[]{:S(2)}, u32[]{:S(2)}) async-start(bf16[256,16,16]{0,2,1:T(8,128)(2,1)} %param.15), calls=%async_computation.1 | async-start | bytes 262144 | tf_op jit(solution)/shard_map/all_to_all | solution.py:53
  28.6 17.9 %all-to-all-start.3 = ((bf16[256,16,16]{0,2,1:T(8,128)(2,1)}), bf16[256,16,16]{0,2,1:T(8,128)(2,1)S(1)}, u32[]{:S(2)}, u32[]{:S(2)}) async-start(bf16[256,16,16]{0,2,1:T(8,128)(2,1)} %param.14), calls=%async_computation.3 | async-start | bytes 262144 | tf_op jit(solution)/shard_map/all_to_all | solution.py:52
  46.5 405.4 %all-to-all-start = ((bf16[2,16,16,256]{3,2,0,1:T(8,128)(2,1)}), bf16[2,16,16,256]{3,2,0,1:T(8,128)(2,1)S(1)}, u32[]{:S(2)}, u32[]{:S(2)}) async-start(bf16[2,16,16,256]{3,2,0,1:T(8,128)(2,1)} %copy.117), calls=%async_computation | async-start | bytes 524288 | tf_op jit(solution)/shard_map/all_to_all | solution.py:54
  57.7 9.4 %collective-permute-start = (f32[1,256,256]{2,1,0:T(8,128)S(1)}, f32[1,256,256]{2,1,0:T(8,128)S(1)}, u32[]{:S(2)}, u32[]{:S(2)}) collective-permute-start(f32[1,256,256]{2,1,0:T(8,128)S(1)} %get-tuple-element.637), channel_id=1, source_target_pairs={{16,0},{32,16},{48,32},{64,48},{80,64},{96,80},{112,96},{128,112},... | collective-permute-start | bytes 786440 | tf_op jit(solution)/shard_map/while/body/eval_jaxpr/ppermute | solution.py:12
  208.5 8.4 %collective-permute-start = (f32[1,256,256]{2,1,0:T(8,128)S(1)}, f32[1,256,256]{2,1,0:T(8,128)S(1)}, u32[]{:S(2)}, u32[]{:S(2)}) collective-permute-start(f32[1,256,256]{2,1,0:T(8,128)S(1)} %get-tuple-element.637), channel_id=1, source_target_pairs={{16,0},{32,16},{48,32},{64,48},{80,64},{96,80},{112,96},{128,112},... | collective-permute-start | bytes 786440 | tf_op jit(solution)/shard_map/while/body/eval_jaxpr/ppermute | solution.py:12
  220.7 9.8 %collective-permute-start = (f32[1,256,256]{2,1,0:T(8,128)S(1)}, f32[1,256,256]{2,1,0:T(8,128)S(1)}, u32[]{:S(2)}, u32[]{:S(2)}) collective-permute-start(f32[1,256,256]{2,1,0:T(8,128)S(1)} %get-tuple-element.637), channel_id=1, source_target_pairs={{16,0},{32,16},{48,32},{64,48},{80,64},{96,80},{112,96},{128,112},... | collective-permute-start | bytes 786440 | tf_op jit(solution)/shard_map/while/body/eval_jaxpr/ppermute | solution.py:12
  234.3 9.8 %collective-permute-start = (f32[1,256,256]{2,1,0:T(8,128)S(1)}, f32[1,256,256]{2,1,0:T(8,128)S(1)}, u32[]{:S(2)}, u32[]{:S(2)}) collective-permute-start(f32[1,256,256]{2,1,0:T(8,128)S(1)} %get-tuple-element.637), channel_id=1, source_target_pairs={{16,0},{32,16},{48,32},{64,48},{80,64},{96,80},{112,96},{128,112},... | collective-permute-start | bytes 786440 | tf_op jit(solution)/shard_map/while/body/eval_jaxpr/ppermute | solution.py:12
  247.9 9.8 %collective-permute-start = (f32[1,256,256]{2,1,0:T(8,128)S(1)}, f32[1,256,256]{2,1,0:T(8,128)S(1)}, u32[]{:S(2)}, u32[]{:S(2)}) collective-permute-start(f32[1,256,256]{2,1,0:T(8,128)S(1)} %get-tuple-element.637), channel_id=1, source_target_pairs={{16,0},{32,16},{48,32},{64,48},{80,64},{96,80},{112,96},{128,112},... | collective-permute-start | bytes 786440 | tf_op jit(solution)/shard_map/while/body/eval_jaxpr/ppermute | solution.py:12
  261.4 9.8 %collective-permute-start = (f32[1,256,256]{2,1,0:T(8,128)S(1)}, f32[1,256,256]{2,1,0:T(8,128)S(1)}, u32[]{:S(2)}, u32[]{:S(2)}) collective-permute-start(f32[1,256,256]{2,1,0:T(8,128)S(1)} %get-tuple-element.637), channel_id=1, source_target_pairs={{16,0},{32,16},{48,32},{64,48},{80,64},{96,80},{112,96},{128,112},... | collective-permute-start | bytes 786440 | tf_op jit(solution)/shard_map/while/body/eval_jaxpr/ppermute | solution.py:12
  275.0 9.8 %collective-permute-start = (f32[1,256,256]{2,1,0:T(8,128)S(1)}, f32[1,256,256]{2,1,0:T(8,128)S(1)}, u32[]{:S(2)}, u32[]{:S(2)}) collective-permute-start(f32[1,256,256]{2,1,0:T(8,128)S(1)} %get-tuple-element.637), channel_id=1, source_target_pairs={{16,0},{32,16},{48,32},{64,48},{80,64},{96,80},{112,96},{128,112},... | collective-permute-start | bytes 786440 | tf_op jit(solution)/shard_map/while/body/eval_jaxpr/ppermute | solution.py:12
  288.6 9.8 %collective-permute-start = (f32[1,256,256]{2,1,0:T(8,128)S(1)}, f32[1,256,256]{2,1,0:T(8,128)S(1)}, u32[]{:S(2)}, u32[]{:S(2)}) collective-permute-start(f32[1,256,256]{2,1,0:T(8,128)S(1)} %get-tuple-element.637), channel_id=1, source_target_pairs={{16,0},{32,16},{48,32},{64,48},{80,64},{96,80},{112,96},{128,112},... | collective-permute-start | bytes 786440 | tf_op jit(solution)/shard_map/while/body/eval_jaxpr/ppermute | solution.py:12
  302.2 9.8 %collective-permute-start = (f32[1,256,256]{2,1,0:T(8,128)S(1)}, f32[1,256,256]{2,1,0:T(8,128)S(1)}, u32[]{:S(2)}, u32[]{:S(2)}) collective-permute-start(f32[1,256,256]{2,1,0:T(8,128)S(1)} %get-tuple-element.637), channel_id=1, source_target_pairs={{16,0},{32,16},{48,32},{64,48},{80,64},{96,80},{112,96},{128,112},... | collective-permute-start | bytes 786440 | tf_op jit(solution)/shard_map/while/body/eval_jaxpr/ppermute | solution.py:12
  315.7 9.8 %collective-permute-start = (f32[1,256,256]{2,1,0:T(8,128)S(1)}, f32[1,256,256]{2,1,0:T(8,128)S(1)}, u32[]{:S(2)}, u32[]{:S(2)}) collective-permute-start(f32[1,256,256]{2,1,0:T(8,128)S(1)} %get-tuple-element.637), channel_id=1, source_target_pairs={{16,0},{32,16},{48,32},{64,48},{80,64},{96,80},{112,96},{128,112},... | collective-permute-start | bytes 786440 | tf_op jit(solution)/shard_map/while/body/eval_jaxpr/ppermute | solution.py:12
  329.3 9.8 %collective-permute-start = (f32[1,256,256]{2,1,0:T(8,128)S(1)}, f32[1,256,256]{2,1,0:T(8,128)S(1)}, u32[]{:S(2)}, u32[]{:S(2)}) collective-permute-start(f32[1,256,256]{2,1,0:T(8,128)S(1)} %get-tuple-element.637), channel_id=1, source_target_pairs={{16,0},{32,16},{48,32},{64,48},{80,64},{96,80},{112,96},{128,112},... | collective-permute-start | bytes 786440 | tf_op jit(solution)/shard_map/while/body/eval_jaxpr/ppermute | solution.py:12
  342.9 9.8 %collective-permute-start = (f32[1,256,256]{2,1,0:T(8,128)S(1)}, f32[1,256,256]{2,1,0:T(8,128)S(1)}, u32[]{:S(2)}, u32[]{:S(2)}) collective-permute-start(f32[1,256,256]{2,1,0:T(8,128)S(1)} %get-tuple-element.637), channel_id=1, source_target_pairs={{16,0},{32,16},{48,32},{64,48},{80,64},{96,80},{112,96},{128,112},... | collective-permute-start | bytes 786440 | tf_op jit(solution)/shard_map/while/body/eval_jaxpr/ppermute | solution.py:12
  356.5 9.8 %collective-permute-start = (f32[1,256,256]{2,1,0:T(8,128)S(1)}, f32[1,256,256]{2,1,0:T(8,128)S(1)}, u32[]{:S(2)}, u32[]{:S(2)}) collective-permute-start(f32[1,256,256]{2,1,0:T(8,128)S(1)} %get-tuple-element.637), channel_id=1, source_target_pairs={{16,0},{32,16},{48,32},{64,48},{80,64},{96,80},{112,96},{128,112},... | collective-permute-start | bytes 786440 | tf_op jit(solution)/shard_map/while/body/eval_jaxpr/ppermute | solution.py:12
  370.0 9.8 %collective-permute-start = (f32[1,256,256]{2,1,0:T(8,128)S(1)}, f32[1,256,256]{2,1,0:T(8,128)S(1)}, u32[]{:S(2)}, u32[]{:S(2)}) collective-permute-start(f32[1,256,256]{2,1,0:T(8,128)S(1)} %get-tuple-element.637), channel_id=1, source_target_pairs={{16,0},{32,16},{48,32},{64,48},{80,64},{96,80},{112,96},{128,112},... | collective-permute-start | bytes 786440 | tf_op jit(solution)/shard_map/while/body/eval_jaxpr/ppermute | solution.py:12
  383.6 9.8 %collective-permute-start = (f32[1,256,256]{2,1,0:T(8,128)S(1)}, f32[1,256,256]{2,1,0:T(8,128)S(1)}, u32[]{:S(2)}, u32[]{:S(2)}) collective-permute-start(f32[1,256,256]{2,1,0:T(8,128)S(1)} %get-tuple-element.637), channel_id=1, source_target_pairs={{16,0},{32,16},{48,32},{64,48},{80,64},{96,80},{112,96},{128,112},... | collective-permute-start | bytes 786440 | tf_op jit(solution)/shard_map/while/body/eval_jaxpr/ppermute | solution.py:12
  397.2 9.8 %collective-permute-start = (f32[1,256,256]{2,1,0:T(8,128)S(1)}, f32[1,256,256]{2,1,0:T(8,128)S(1)}, u32[]{:S(2)}, u32[]{:S(2)}) collective-permute-start(f32[1,256,256]{2,1,0:T(8,128)S(1)} %get-tuple-element.637), channel_id=1, source_target_pairs={{16,0},{32,16},{48,32},{64,48},{80,64},{96,80},{112,96},{128,112},... | collective-permute-start | bytes 786440 | tf_op jit(solution)/shard_map/while/body/eval_jaxpr/ppermute | solution.py:12
  410.7 9.8 %collective-permute-start = (f32[1,256,256]{2,1,0:T(8,128)S(1)}, f32[1,256,256]{2,1,0:T(8,128)S(1)}, u32[]{:S(2)}, u32[]{:S(2)}) collective-permute-start(f32[1,256,256]{2,1,0:T(8,128)S(1)} %get-tuple-element.637), channel_id=1, source_target_pairs={{16,0},{32,16},{48,32},{64,48},{80,64},{96,80},{112,96},{128,112},... | collective-permute-start | bytes 786440 | tf_op jit(solution)/shard_map/while/body/eval_jaxpr/ppermute | solution.py:12
  424.3 9.8 %collective-permute-start = (f32[1,256,256]{2,1,0:T(8,128)S(1)}, f32[1,256,256]{2,1,0:T(8,128)S(1)}, u32[]{:S(2)}, u32[]{:S(2)}) collective-permute-start(f32[1,256,256]{2,1,0:T(8,128)S(1)} %get-tuple-element.637), channel_id=1, source_target_pairs={{16,0},{32,16},{48,32},{64,48},{80,64},{96,80},{112,96},{128,112},... | collective-permute-start | bytes 786440 | tf_op jit(solution)/shard_map/while/body/eval_jaxpr/ppermute | solution.py:12
  437.9 9.8 %collective-permute-start = (f32[1,256,256]{2,1,0:T(8,128)S(1)}, f32[1,256,256]{2,1,0:T(8,128)S(1)}, u32[]{:S(2)}, u32[]{:S(2)}) collective-permute-start(f32[1,256,256]{2,1,0:T(8,128)S(1)} %get-tuple-element.637), channel_id=1, source_target_pairs={{16,0},{32,16},{48,32},{64,48},{80,64},{96,80},{112,96},{128,112},... | collective-permute-start | bytes 786440 | tf_op jit(solution)/shard_map/while/body/eval_jaxpr/ppermute | solution.py:12
  456.1 23.1 %all-to-all-start.4 = ((bf16[16,2,2048]{2,1,0:T(2,128)(2,1)}), bf16[16,2,2048]{2,1,0:T(2,128)(2,1)S(1)}, u32[]{:S(2)}, u32[]{:S(2)}) async-start(bf16[16,2,2048]{2,1,0:T(2,128)(2,1)} %reshape.369), calls=%async_computation.4 | async-start | bytes 262144 | tf_op jit(solution)/shard_map/all_to_all | solution.py:127
  479.2 15.8 %all-to-all-start.2 = ((bf16[16,2,2048]{2,1,0:T(2,128)(2,1)}), bf16[16,2,2048]{2,1,0:T(2,128)(2,1)S(1)}, u32[]{:S(2)}, u32[]{:S(2)}) async-start(bf16[16,2,2048]{2,1,0:T(2,128)(2,1)} %reshape.367), calls=%async_computation.2 | async-start | bytes 262144 | tf_op jit(solution)/shard_map/all_to_all | solution.py:126
  (18 other events, 181.4 us)
where the time goes:
time: 636 us; the launch traced here: 631 us
  waiting for transfers between devices  255 us (40%)
  blocking collectives  130 us (20%)
  starting transfers between devices  104 us (16%)
  matrix products  84.9 us (13%)
  local copies, waits for them, and re-layouts  45.3 us (7%)
    ppermute x31, waiting for transfers between devices, from_behind(): lax.ppermute(value, axis, [(source, source + steps) for source in range(f...  215 us
    psum x1, blocking collectives, local(): summed = lax.psum(partial_value, ('seq', 'key'))  130 us
    dot_general x130, matrix products, precise_product(): jnp.einsum(form, left.astype(jnp.float32), right, precision=highest_mode)  80.6 us
    ppermute x31, starting transfers between devices, from_behind(): lax.ppermute(value, axis, [(source, source + steps) for source in range(f...  61.5 us
    dynamic_slice x64, local copies, waits for them, and re-layouts, device_map(): lax.scan(group_step, state_out, (written_keys, key_result, end_decay, off...  37.6 us
    all_to_all x1, starting transfers between devices, local(): lax.all_to_all(key_rows, 'key', split_axis=1, concat_axis=2, tiled=True)  15.9 us
  transfers between devices with their start and end apart: 36, of which 35 were waited for; matrix products, arithmetic and copies ran while one was open for 20% of the time, Pallas kernels for 0%

commit v1 on v0

v1 whole, which is shorter than its diff:
```python
import jax
import jax.numpy as jnp
from jax import lax
from jax.experimental import pallas as pl
from jax.experimental.pallas import tpu as pltpu
from jax.sharding import Mesh, PartitionSpec as P

F32 = jnp.float32
BF16 = jnp.bfloat16
SEQ = ("x", "y", "c")
N = 128
K = 256
V = 256
W2 = K + V
PAD = 16


def nn(a, b):
    return lax.dot_general(a, b, (((1,), (0,)), ((), ())), preferred_element_type=F32)


def nt(a, b):
    return lax.dot_general(a, b, (((1,), (1,)), ((), ())), preferred_element_type=F32)


def tn(a, b):
    return lax.dot_general(a, b, (((0,), (0,)), ((), ())), preferred_element_type=F32)


def split(a):
    high = a.astype(BF16)
    return high, (a - high.astype(F32)).astype(BF16)


def nn2(a, b):
    high, low = split(b)
    return nn(a, high) + nn(a, low)


def tn2(a, b):
    high, low = split(b)
    return tn(a, high) + tn(a, low)


def gates_of(gate_row, rate_row):
    rows = lax.broadcasted_iota(jnp.int32, (N, N), 0)
    cols = lax.broadcasted_iota(jnp.int32, (N, N), 1)
    lower = cols <= rows
    eye = cols == rows
    gate_col = jnp.sum(jnp.where(eye, gate_row, 0.0), axis=1, keepdims=True)
    rate_col = jnp.sum(jnp.where(eye, rate_row, 0.0), axis=1, keepdims=True)
    gamma_col = jnp.sum(jnp.where(lower, gate_row, 0.0), axis=1, keepdims=True)
    gamma_row = jnp.sum(jnp.where(rows <= cols, gate_col, 0.0), axis=0, keepdims=True)
    gamma_end = jnp.sum(gate_row, axis=1, keepdims=True)
    spread = jnp.where(lower, gamma_col - gamma_row, 0.0)
    mask = jnp.where(lower, jnp.exp(spread), 0.0)
    return gamma_row, gamma_end, mask, rate_col


def compose(first, second):
    decay1, m1, b1 = first
    decay2, m2, b2 = second
    both = nn(m1.astype(BF16), jnp.concatenate([m2, b2], axis=1).astype(BF16))
    return decay1 * decay2, decay2 * m1 + decay1 * m2 - both[:, :K], decay1 * b2 + b1 - both[:, K:]


def decay_rows(decay):
    high = decay.astype(BF16).astype(F32)
    middle = (decay - high).astype(BF16).astype(F32)
    low = decay - high - middle
    rows = lax.broadcasted_iota(jnp.int32, (PAD, W2), 0)
    return jnp.where(rows == 0, high, jnp.where(rows == 1, middle, jnp.where(rows == 2, low, 0.0))).astype(BF16)


def decay_from(block):
    return jnp.sum(block.astype(F32), axis=0, keepdims=True)[:, :1]


def unpack(block):
    return decay_from(block[K:]), block[:K, :K].astype(F32), block[:K, K:].astype(F32)


def unpack_halves(low, high):
    body = jnp.concatenate([low[: K // 2], high[: K // 2]], axis=0)
    return decay_from(low[K // 2 :]), body[:, :K].astype(F32), body[:, K:].astype(F32)


def head_rows(kq_ref, which):
    return kq_ref[:, 16 * which : 16 * which + 16, :].reshape(K, 2 * N)


def local_map_kernel(kq_ref, grad_ref, gate_ref, rate_ref, inv_ref, map_ref, wt_ref, lg_ref):
    key_t = head_rows(kq_ref, 0)
    query_t = head_rows(kq_ref, 1)
    maps = []
    for g in range(2):
        span = slice(g * N, (g + 1) * N)
        rate = rate_ref[:, span]
        gamma, gamma_end, mask, _ = gates_of(gate_ref[:, span], rate)
        kt, qt = key_t[:, span], query_t[:, span]
        into = jnp.exp(gamma)
        scaled = (kt * (rate * into)).astype(BF16)
        wt = nt(scaled, inv_ref[g, 0]).astype(BF16)
        wt_ref[:, span] = wt
        score = (tn(qt, kt) * mask).astype(BF16)
        out_t = (kt * jnp.exp(gamma_end - gamma)).astype(BF16)
        in_t = (qt * into).astype(BF16)
        grad = grad_ref[span, :]
        lg = tn(score, grad)
        lg_ref[span, :] = lg
        offset = nn(in_t, grad) - nn2(wt, lg)
        maps.append((jnp.exp(gamma_end), nt(wt, out_t), offset))
    decay, m, b = compose(*maps)
    map_ref[:K, :K] = m.astype(BF16)
    map_ref[:K, K:] = b.astype(BF16)
    map_ref[K:, :] = decay_rows(decay)


def pair_kernel(place_ref, pair_ref, half_ref, full_ref):
    decay, m, b = compose(unpack(pair_ref[0]), unpack(pair_ref[1]))
    full_ref[:K, :K] = m.astype(BF16)
    full_ref[:K, K:] = b.astype(BF16)
    rows = decay_rows(decay)
    full_ref[K:, :] = rows
    half_ref[K // 2 :, :] = rows
    half_ref[: K // 2, :] = full_ref[pl.ds(pl.multiple_of(place_ref[1] * (K // 2), K // 2), K // 2), :]


def plane_kernel(place_ref, pair_ref, own_ref, halves_ref, half_ref, em_ref, eb_ref, slots, body, ends):
    y, c = place_ref[0], place_ref[1]
    slots[y] = own_ref[...]
    for d in range(1, 4):
        at = lax.rem(y + d, 4)
        slots[at, : K // 2, :] = halves_ref[0, d - 1, : K // 2, :]
        slots[at, K // 2 : K, :] = halves_ref[1, d - 1, : K // 2, :]
        slots[at, K:, :] = halves_ref[0, d - 1, K // 2 :, :]
    suffix = unpack(slots[3])
    end = (jnp.ones((1, 1), F32), jnp.zeros((K, K), F32), jnp.zeros((K, V), F32))
    for j in (2, 1, 0):
        here = y == j
        end = tuple(jnp.where(here, s, e) for s, e in zip(suffix, end))
        suffix = compose(unpack(slots[j]), suffix)
    decay, m, b = suffix
    body[:, :K] = m.astype(BF16)
    body[:, K:] = b.astype(BF16)
    half_ref[K // 2 :, :] = decay_rows(decay)
    half_ref[: K // 2, :] = body[pl.ds(pl.multiple_of(c * (K // 2), K // 2), K // 2), :]
    inner = compose(unpack(pair_ref[1]), end)
    decay, m, b = tuple(jnp.where(c == 0, i, e) for i, e in zip(inner, end))
    em_ref[...] = m.astype(BF16)
    eb_ref[:K, :] = b
    eb_ref[K:, :] = jnp.broadcast_to(decay, (8, V))


def ahead_kernel(kq_ref, grad_ref, gate_ref, rate_ref, inv_ref, wt_ref, value_ref, state_ref,
                 gq_ref, nv_ref, ct_ref, sum_ref):
    key_t = head_rows(kq_ref, 0)
    query_t = head_rows(kq_ref, 1)
    total = jnp.zeros((1, 1), F32)
    for g in range(2):
        span = slice(g * N, (g + 1) * N)
        gamma, _, mask, rate_col = gates_of(gate_ref[:, span], rate_ref[:, span])
        kt, qt = key_t[:, span], query_t[:, span]
        state = state_ref[:, g].reshape(K, V)
        grad = grad_ref[span, :]
        scaled = (value_ref[span, :] * rate_col).astype(BF16)
        fresh = (nn(inv_ref[g, 0], scaled) - tn(wt_ref[:, span], state)).astype(BF16)
        nv_ref[span, :] = fresh
        score = (nt(grad, fresh) * mask).astype(BF16)
        gq = (jnp.exp(gamma) * nt(state, grad) + nt(kt, score)).astype(BF16)
        gq_ref[:, :, span] = gq.reshape(16, 16, N)
        ct_ref[:, span] = nn(qt, score)
        total += jnp.sum(jnp.square(gq.astype(F32)), keepdims=True)
    sum_ref[...] = jnp.broadcast_to(total, (8, 128))


def final_kernel(halves_ref, em_ref, eb_ref, kq_ref, grad_ref, gate_ref, rate_ref, inv_ref, wt_ref, lg_ref,
                 state_ref, nv_ref, ct_ref, sum_ref, gk_ref, gv_ref):
    key_t = head_rows(kq_ref, 0)
    query_t = head_rows(kq_ref, 1)
    later = None
    for d in (2, 1, 0):
        decay, m, b = unpack_halves(halves_ref[0, d], halves_ref[1, d])
        later = b if later is None else decay * later + b - nn(m.astype(BF16), later.astype(BF16))
    state_grad = eb_ref[K : K + 1, :1] * later + eb_ref[:K, :] - nn(em_ref[...], later.astype(BF16))
    total = sum_ref[:1, :1]
    for g in (1, 0):
        span = slice(g * N, (g + 1) * N)
        rate = rate_ref[:, span]
        gamma, gamma_end, _, rate_col = gates_of(gate_ref[:, span], rate)
        into = jnp.exp(gamma)
        away = jnp.exp(gamma_end - gamma)
        inverse = inv_ref[g, 0]
        out_t = (key_t[:, span] * away).astype(BF16)
        high, low = split(state_grad)
        value_grad = lg_ref[span, :] + tn(out_t, high) + tn(out_t, low)
        rounded = value_grad.astype(BF16)
        gv = (rate_col * tn(inverse, rounded)).astype(BF16)
        gv_ref[span, :] = gv
        write_t = (-nt(state_ref[:, g].reshape(K, V), rounded)).astype(BF16)
        gk = (ct_ref[:, span] + away * nt(high, nv_ref[span, :]) + (rate * into) * nn(write_t, inverse)).astype(BF16)
        gk_ref[:, :, span] = gk.reshape(16, 16, N)
        total += jnp.sum(jnp.square(gk.astype(F32)), keepdims=True) + jnp.sum(
            jnp.square(gv.astype(F32)), keepdims=True
        )
        if g == 1:
            in_t = (query_t[:, span] * into).astype(BF16)
            state_grad = (
                jnp.exp(gamma_end) * state_grad
                + nn(in_t, grad_ref[span, :])
                - nn2(wt_ref[:, span], value_grad)
            )
    high = total.astype(BF16).astype(F32)
    middle = (total - high).astype(BF16).astype(F32)
    low = total - high - middle
    rows = lax.broadcasted_iota(jnp.int32, (16, 128), 0)
    pieces = jnp.where(rows == 0, high, jnp.where(rows == 1, middle, jnp.where(rows == 2, low, 0.0)))
    gk_ref[:, :, 2 * N :] = jnp.broadcast_to(pieces.astype(BF16)[None], (16, 16, 128))


def call(kernel, outs, args, flops, scratch=(), scalars=0):
    spec = pl.BlockSpec(memory_space=pltpu.VMEM)
    smem = pl.BlockSpec(memory_space=pltpu.SMEM)
    moved = sum(a.size * a.dtype.itemsize for a in args)
    return pl.pallas_call(
        kernel,
        out_shape=outs,
        in_specs=[smem] * scalars + [spec] * (len(args) - scalars),
        out_specs=[spec] * len(outs),
        scratch_shapes=list(scratch),
        cost_estimate=pl.CostEstimate(flops=flops, bytes_accessed=moved, transcendentals=0),
        compiler_params=pltpu.CompilerParams(vmem_limit_bytes=24 * 2**20),
    )(*args)


def shape(dims, dtype=BF16):
    return jax.ShapeDtypeStruct(dims, dtype)


def to_heads(array):
    return lax.all_to_all(array, "key", 0, 0, tiled=True)


def local(query_rows, key_rows, value_rows, out_grad, log_gates, write_rate, group_inverse, states):
    keys = jnp.transpose(key_rows, (1, 2, 0))
    queries = jnp.transpose(query_rows, (1, 2, 0))
    kq = to_heads(jnp.concatenate([keys, queries], axis=1))
    grad = out_grad.reshape(2 * N, V)
    values = value_rows.reshape(2 * N, V)
    place = jnp.stack([lax.axis_index("y"), lax.axis_index("c")]).astype(jnp.int32)
    half = shape((K // 2 + PAD, W2))
    full = shape((K + PAD, W2))
    square = shape((K, V), F32)
    basics = (kq, grad, log_gates, write_rate, group_inverse)

    device_map, written_t, local_grad = call(
        local_map_kernel, [full, shape((K, 2 * N)), square], basics, 10**8
    )
    pair = lax.all_gather(device_map, "c")
    pair_half, pair_full = call(pair_kernel, [half, full], (place, pair), 10**8, scalars=1)
    state_blocks = jnp.transpose(states, (1, 0, 2, 3))
    state_blocks, pair_half = lax.optimization_barrier((state_blocks, pair_half))
    state_heads = to_heads(state_blocks)
    around = [
        lax.ppermute(pair_half, "y", [(s, (s - d) % 4) for s in range(4)]) for d in (1, 2, 3)
    ]
    pair_halves = lax.all_gather(jnp.stack(around), "c")
    plane_half, end_m, end_b = call(
        plane_kernel,
        [half, shape((K, K)), shape((K + 8, V), F32)],
        (place, pair, pair_full, pair_halves),
        5 * 10**8,
        scratch=[pltpu.VMEM((4, K + PAD, W2), BF16), pltpu.VMEM((K, W2), BF16), pltpu.VMEM((8, 128), F32)],
        scalars=1,
    )
    later = [lax.ppermute(plane_half, "x", [(s, s - d) for s in range(d, 4)]) for d in (1, 2, 3)]
    plane_halves = lax.all_gather(jnp.stack(later), "c")

    gq, fresh, score_term, query_sum = call(
        ahead_kernel,
        [shape((16, 16, 2 * N)), shape((2 * N, V)), square, shape((8, 128), F32)],
        (*basics, written_t, values, state_heads),
        2 * 10**8,
    )
    grad_query = to_heads(gq)
    gk, grad_value = call(
        final_kernel,
        [shape((16, 16, 3 * N)), shape((2 * N, V))],
        (plane_halves, end_m, end_b, *basics, written_t, local_grad, state_heads, fresh, score_term, query_sum),
        4 * 10**8,
    )
    gk = to_heads(gk)
    part = jnp.sum(gk[:, :3, 2 * N].astype(F32))
    parts = lax.all_to_all(jnp.full((32, 1, 128), part), SEQ, 0, 0, tiled=True)
    grad_square = jnp.sum(parts[:, 0, 0]) / (8192 * 16 * (2 * K + V))
    grad_key = jnp.transpose(gk[:, :, : 2 * N], (2, 0, 1))
    return (
        jnp.transpose(grad_query, (2, 0, 1)),
        grad_key,
        grad_value.reshape(2 * N, 1, V),
        grad_square,
    )


def solution(mesh):
    grid = Mesh(mesh.devices.reshape(4, 4, 2, 16), ("x", "y", "c", "key"))
    in_specs = (
        P(SEQ, None, "key"),
        P(SEQ, None, "key"),
        P(SEQ, "key", None),
        P(SEQ, "key", None),
        P("key", SEQ),
        P("key", SEQ),
        P(SEQ, "key", None, None),
        P(SEQ, None, "key", None),
    )
    out_specs = (P(SEQ, None, "key"), P(SEQ, None, "key"), P(SEQ, "key", None), P())
    return jax.shard_map(local, mesh=grid, in_specs=in_specs, out_specs=out_specs, check_vma=False)
```

time: 636 us -> 140 us (0.22)
  waiting for transfers between devices: 255 us -> 41 us
  blocking collectives: 130 us -> 14.9 us
  matrix products: 84.9 us -> 0 us
  local copies, waits for them, and re-layouts: 45.3 us -> 3.33 us
  starting transfers between devices: 104 us -> 66.7 us
  Pallas kernels: 0 us -> 7.71 us
    ppermute x31 -> x6, waiting for transfers between devices: 215 us -> 3.2 us  [the longest x3 3.19 us: local(): lax.ppermute(pair_half, 'y', [(s, (s - d) % 4) for s in range(4)])]
    psum x1 -> x0, blocking collectives: 130 us -> none  [local(): summed = lax.psum(partial_value, ('seq', 'key'))]
    dot_general x142 -> x0, matrix products: 84.9 us -> none  [the longest x130 80.6 us: precise_product(): jnp.einsum(form, left.astype(jnp.float32), right, precision=highest_mode)]
    ppermute x31 -> x6, starting transfers between devices: 61.5 us -> 14.6 us  [the longest x3 10.7 us: local(): lax.ppermute(pair_half, 'y', [(s, (s - d) % 4) for s in range(4)])]
    dynamic_slice x64 -> x0, local copies, waits for them, and re-layouts: 37.6 us -> none  [device_map(): lax.scan(group_step, state_out, (written_keys, key_result, end_decay, off...]
    all_gather x0 -> x3, blocking collectives: none -> 14.9 us  [the longest x1 8.01 us: local(): pair = lax.all_gather(device_map, 'c')]
    all_to_all x5, starting transfers between devices: 42.2 us -> 52.1 us  [the longest x4 39.6 us: to_heads(): return lax.all_to_all(array, 'key', 0, 0, tiled=True)]
    pallas_call x0 -> x5, Pallas kernels: none -> 7.71 us  [call(): pl.pallas_call(kernel, out_shape=outs, in_specs=[smem] * scalars + [spec]...]
  transfers between devices with their start and end apart: 36 -> 11, of which waited for: 35 -> 6; matrix products, arithmetic and copies ran while one was open for 20% -> 1% of each run, Pallas kernels for 0% -> 4%
where the time goes in v1:
time: 140 us; the launch traced here: 139 us
  starting transfers between devices  66.7 us (48%)
  waiting for transfers between devices  41 us (29%)
  blocking collectives  14.9 us (11%)
  Pallas kernels  7.71 us (6%)
  local copies, waits for them, and re-layouts  3.33 us (2%)
  other arithmetic  3.12 us (2%)
  between operations  2.63 us (2%)
    all_to_all x4, starting transfers between devices, to_heads(): return lax.all_to_all(array, 'key', 0, 0, tiled=True)  39.6 us
    all_to_all x4, waiting for transfers between devices, to_heads(): return lax.all_to_all(array, 'key', 0, 0, tiled=True)  31.6 us
    all_to_all x1, starting transfers between devices, local(): parts = lax.all_to_all(jnp.full((32, 1, 128), part), SEQ, 0, 0, tiled=True)  12.5 us
    ppermute x3, starting transfers between devices, local(): lax.ppermute(pair_half, 'y', [(s, (s - d) % 4) for s in range(4)])  10.7 us
    all_gather x1, blocking collectives, local(): pair = lax.all_gather(device_map, 'c')  8.01 us
    pallas_call x5, Pallas kernels, call(): pl.pallas_call(kernel, out_shape=outs, in_specs=[smem] * scalars + [spec]...  7.71 us
    all_to_all x1, waiting for transfers between devices, local(): parts = lax.all_to_all(jnp.full((32, 1, 128), part), SEQ, 0, 0, tiled=True)  6.2 us
    all_gather x1, blocking collectives, local(): pair_halves = lax.all_gather(jnp.stack(around), 'c')  4.14 us
  transfers between devices with their start and end apart: 11, of which 6 were waited for; matrix products, arithmetic and copies ran while one was open for 1% of the time, Pallas kernels for 4%

profile of v1, /device:TPU:1, one launch (start us, length us, event | category | flops | bytes accessed | tf_op | source)
XLA Modules:
  0.0 139.4 jit_solution(17445913444675385841)
XLA Ops:
  0.6 1.7 %pad_maximum_fusion.2 = bf16[16,32,256]{2,1,0:T(8,128)(2,1)} fusion(bf16[16,16,256]{2,1,0:T(8,128)(2,1)} %bitcast.37, bf16[16,16,256]{2,1,0:T(8,128)(2,1)} %bitcast.38), kind=kLoop, calls=%fused_computation.2 | loop fusion | flops 524288 | bytes 524288 | tf_op jit(solution)/shard_map/concatenate | solution.py:247
  2.3 15.9 %all-to-all-start = ((bf16[16,32,256]{2,1,0:T(8,128)(2,1)}), bf16[16,32,256]{2,1,0:T(8,128)(2,1)S(1)}, u32[]{:S(2)}, u32[]{:S(2)}) async-start(bf16[16,32,256]{2,1,0:T(8,128)(2,1)} %pad_maximum_fusion.2), calls=%async_computation | async-start | bytes 524288 | tf_op jit(solution)/shard_map/all_to_all | solution.py:241
  19.0 12.3 %all-to-all-done.kq_ref = bf16[16,32,256]{2,1,0:T(8,128)(2,1)S(1)} async-done(((bf16[16,32,256]{2,1,0:T(8,128)(2,1)}), bf16[16,32,256]{2,1,0:T(8,128)(2,1)S(1)}, u32[]{:S(2)}, u32[]{:S(2)}) %all-to-all-start) | async-done | bytes 262176 | tf_op jit(solution)/shard_map/all_to_all | solution.py:241
  31.4 1.3 shard_map.111
  32.7 8.0 %all-gather = bf16[544,512]{1,0:T(8,128)(2,1)S(1)} all-gather(bf16[272,512]{1,0:T(8,128)(2,1)S(1)} %get-tuple-element.21), channel_id=2, replica_groups=mesh['x'=4,'y'=4,'c'=2,'key'=16] {'c'}, dimensions={0}, use_global_device_ids=true | all-gather | bytes 835584 | tf_op jit(solution)/shard_map/all_gather | solution.py:259
  41.5 5.5 %all-to-all-start.1 = ((bf16[16,2,16,256]{3,2,1,0:T(8,128)(2,1)}), bf16[16,2,16,256]{3,2,1,0:T(8,128)(2,1)S(1)}, u32[]{:S(2)}, u32[]{:S(2)}) async-start(bf16[16,2,16,256]{3,2,1,0:T(8,128)(2,1)} %bitcast.21), calls=%async_computation.1 | async-start | bytes 524288 | tf_op jit(solution)/shard_map/all_to_all | solution.py:241
  47.0 3.2 %collective-permute-start.2 = (bf16[144,512]{1,0:T(8,128)(2,1)S(1)}, bf16[144,512]{1,0:T(8,128)(2,1)S(1)}, u32[]{:S(2)}, u32[]{:S(2)}) collective-permute-start(bf16[144,512]{1,0:T(8,128)(2,1)S(1)} %get-tuple-element.26), channel_id=1, source_target_pairs={{0,32},{32,64},{64,96},{96,0},{1,33},{33,65},{65,97},{97,1},{2,34}... | collective-permute-start | bytes 442376 | tf_op jit(solution)/shard_map/ppermute | solution.py:265
  50.2 4.5 %collective-permute-start.1 = (bf16[144,512]{1,0:T(8,128)(2,1)S(1)}, bf16[144,512]{1,0:T(8,128)(2,1)S(1)}, u32[]{:S(2)}, u32[]{:S(2)}) collective-permute-start(bf16[144,512]{1,0:T(8,128)(2,1)S(1)} %get-tuple-element.26), channel_id=1, source_target_pairs={{0,64},{32,96},{64,0},{96,32},{1,65},{33,97},{65,1},{97,33},{2,66}... | collective-permute-start | bytes 442376 | tf_op jit(solution)/shard_map/ppermute | solution.py:265
  54.8 3.0 %collective-permute-start = (bf16[144,512]{1,0:T(8,128)(2,1)S(1)}, bf16[144,512]{1,0:T(8,128)(2,1)S(1)}, u32[]{:S(2)}, u32[]{:S(2)}) collective-permute-start(bf16[144,512]{1,0:T(8,128)(2,1)S(1)} %get-tuple-element.26), channel_id=1, source_target_pairs={{0,96},{32,0},{64,32},{96,64},{1,97},{33,1},{65,33},{97,65},{2,98}... | collective-permute-start | bytes 442376 | tf_op jit(solution)/shard_map/ppermute | solution.py:265
  57.8 1.8 %collective-permute-done.1 = bf16[144,512]{1,0:T(8,128)(2,1)S(1)} collective-permute-done((bf16[144,512]{1,0:T(8,128)(2,1)S(1)}, bf16[144,512]{1,0:T(8,128)(2,1)S(1)}, u32[]{:S(2)}, u32[]{:S(2)}) %collective-permute-start.1) | collective-permute-done | bytes 147488 | tf_op jit(solution)/shard_map/ppermute | solution.py:265
  59.5 1.4 %collective-permute-done = bf16[144,512]{1,0:T(8,128)(2,1)S(1)} collective-permute-done((bf16[144,512]{1,0:T(8,128)(2,1)S(1)}, bf16[144,512]{1,0:T(8,128)(2,1)S(1)}, u32[]{:S(2)}, u32[]{:S(2)}) %collective-permute-start) | collective-permute-done | bytes 147488 | tf_op jit(solution)/shard_map/ppermute | solution.py:265
  61.0 4.1 %all-gather.1 = bf16[6,144,512]{2,1,0:T(8,128)(2,1)S(1)} all-gather(bf16[3,144,512]{2,1,0:T(8,128)(2,1)S(1)} %pad_maximum_fusion), channel_id=3, replica_groups=mesh['x'=4,'y'=4,'c'=2,'key'=16] {'c'}, dimensions={0}, use_global_device_ids=true | all-gather | bytes 1327104 | tf_op jit(solution)/shard_map/all_gather | solution.py:267
  65.1 1.4 %shard_map.114 = (bf16[144,512]{1,0:T(8,128)(2,1)S(1)}, bf16[256,256]{1,0:T(8,128)(2,1)S(1)}, f32[264,256]{1,0:T(8,128)S(1)}) custom-call(s32[2]{0:T(128)S(1)} %pad_add_fusion.place_ref, bf16[2,272,512]{2,1,0:T(8,128)(2,1)S(1)} %bitcast.24, bf16[272,512]{1,0:T(8,128)(2,1)S(1)} %get-tuple-element.25.own_ref, bf16[2,3,144,512]{3,2,1,0:T(8,128)(2,1)S(1)} %bitcast.28), custom_call_target="tpu_custom_call" | custom-call | flops 500000000 | bytes 1720328 | tf_op jit(solution)/shard_map/pallas_call | solution.py:225
  66.6 1.3 collective-permute-start.5
  67.9 1.3 collective-permute-start.4
  70.5 1.6 %shard_map.113 = (bf16[16,16,256]{2,1,0:T(8,128)(2,1)}, bf16[256,256]{1,0:T(8,128)(2,1)S(1)}, f32[256,256]{1,0:T(8,128)S(1)}, f32[8,128]{1,0:T(8,128)S(1)}) custom-call(bf16[16,32,256]{2,1,0:T(8,128)(2,1)S(1)} %all-to-all-done.kq_ref, bf16[256,256]{1,0:T(8,128)(2,1)S(1)} %bitcast.26, f32[1,256]{1,0:T(1,128)S(1)} %copy-done.3, f32[1,256]{1,0:T(1,128)S(1)} %copy-done.4, ...), custom_call_target="tpu_custom_call" | custom-call | flops 200000000 | bytes 985088 | tf_op jit(solution)/shard_map/pallas_call | solution.py:225
  72.1 11.7 %all-to-all-start.2 = ((bf16[16,16,256]{2,1,0:T(8,128)(2,1)}), bf16[16,16,256]{2,1,0:T(8,128)(2,1)S(1)}, u32[]{:S(2)}, u32[]{:S(2)}) async-start(bf16[16,16,256]{2,1,0:T(8,128)(2,1)} %get-tuple-element.24), calls=%async_computation.2 | async-start | bytes 262144 | tf_op jit(solution)/shard_map/all_to_all | solution.py:241
  83.9 2.7 %all-gather.2 = bf16[6,144,512]{2,1,0:T(8,128)(2,1)S(1)} all-gather(bf16[3,144,512]{2,1,0:T(8,128)(2,1)S(1)} %pad_maximum_fusion.1), channel_id=4, replica_groups=mesh['x'=4,'y'=4,'c'=2,'key'=16] {'c'}, dimensions={0}, use_global_device_ids=true | all-gather | bytes 1327104 | tf_op jit(solution)/shard_map/all_gather | solution.py:277
  86.7 2.6 %shard_map.115 = (bf16[16,16,384]{2,1,0:T(8,128)(2,1)}, bf16[256,256]{1,0:T(8,128)(2,1)}) custom-call(bf16[2,3,144,512]{3,2,1,0:T(8,128)(2,1)S(1)} %bitcast.22, bf16[256,256]{1,0:T(8,128)(2,1)S(1)} %get-tuple-element.28.em_ref, f32[264,256]{1,0:T(8,128)S(1)} %get-tuple-element.29.eb_ref, bf16[16,32,256]{2,1,0:T(8,128)(2,1)S(1)} %all-to-all-done.kq_ref, ...), custom_call_target="tpu_custom_call" | custom-call | flops 400000000 | bytes 2799616 | tf_op jit(solution)/shard_map/pallas_call | solution.py:225
  89.2 6.7 %all-to-all-done.2 = bf16[16,16,256]{2,1,0:T(8,128)(2,1)S(1)} async-done(((bf16[16,16,256]{2,1,0:T(8,128)(2,1)}), bf16[16,16,256]{2,1,0:T(8,128)(2,1)S(1)}, u32[]{:S(2)}, u32[]{:S(2)}) %all-to-all-start.2) | async-done | bytes 131104 | tf_op jit(solution)/shard_map/all_to_all | solution.py:241
  96.0 6.5 %all-to-all-start.3 = ((bf16[16,16,384]{2,1,0:T(8,128)(2,1)}), bf16[16,16,384]{2,1,0:T(8,128)(2,1)S(1)}, u32[]{:S(2)}, u32[]{:S(2)}) async-start(bf16[16,16,384]{2,1,0:T(8,128)(2,1)} %get-tuple-element.34), calls=%async_computation.3 | async-start | bytes 393216 | tf_op jit(solution)/shard_map/all_to_all | solution.py:241
  102.4 12.6 %all-to-all-done.3 = bf16[16,16,384]{2,1,0:T(8,128)(2,1)S(1)} async-done(((bf16[16,16,384]{2,1,0:T(8,128)(2,1)}), bf16[16,16,384]{2,1,0:T(8,128)(2,1)S(1)}, u32[]{:S(2)}, u32[]{:S(2)}) %all-to-all-start.3) | async-done | bytes 196640 | tf_op jit(solution)/shard_map/all_to_all | solution.py:241
  116.9 12.5 %all-to-all-start.4 = ((f32[32,1,128]{2,1,0:T(1,128)}), f32[32,1,128]{2,1,0:T(1,128)S(1)}, u32[]{:S(2)}, u32[]{:S(2)}) async-start(f32[32,1,128]{2,1,0:T(1,128)} %broadcast_in_dim.3), calls=%async_computation.4 | async-start | bytes 32768 | tf_op jit(solution)/shard_map/all_to_all | solution.py:294
  130.1 6.2 %all-to-all-done.4 = f32[32,1,128]{2,1,0:T(1,128)S(1)} async-done(((f32[32,1,128]{2,1,0:T(1,128)}), f32[32,1,128]{2,1,0:T(1,128)S(1)}, u32[]{:S(2)}, u32[]{:S(2)}) %all-to-all-start.4) | async-done | bytes 16416 | tf_op jit(solution)/shard_map/all_to_all | solution.py:294
  (28 shorter events, 6.8 us)
Async XLA Ops:
  2.3 15.9 %copy-start.5 = (bf16[2,16,16,256]{3,2,1,0:T(8,128)(2,1)S(1)}, bf16[2,16,16,256]{3,2,1,0:T(8,128)(2,1)}, u32[]{:S(2)}) copy-start(bf16[2,16,16,256]{3,2,1,0:T(8,128)(2,1)} %param.15) | copy-start | bytes 786436
  2.3 29.0 %all-to-all-start = ((bf16[16,32,256]{2,1,0:T(8,128)(2,1)}), bf16[16,32,256]{2,1,0:T(8,128)(2,1)S(1)}, u32[]{:S(2)}, u32[]{:S(2)}) async-start(bf16[16,32,256]{2,1,0:T(8,128)(2,1)} %pad_maximum_fusion.2), calls=%async_computation | async-start | bytes 524288 | tf_op jit(solution)/shard_map/all_to_all | solution.py:241
  18.2 13.1 %copy-start = (bf16[256,1,256]{2,0,1:T(8,128)(2,1)S(1)}, bf16[256,1,256]{2,0,1:T(8,128)(2,1)}, u32[]{:S(2)}) copy-start(bf16[256,1,256]{2,0,1:T(8,128)(2,1)} %param.11) | copy-start | bytes 393220
  18.2 13.1 %copy-start.1 = (bf16[2,1,128,128]{3,2,1,0:T(8,128)(2,1)S(1)}, bf16[2,1,128,128]{3,2,1,0:T(8,128)(2,1)}, u32[]{:S(2)}) copy-start(bf16[2,1,128,128]{3,2,1,0:T(8,128)(2,1)} %inv_ref.5) | copy-start | bytes 196612
  19.0 12.4 %copy-start.4 = (f32[1,256]{1,0:T(1,128)S(1)}, f32[1,256]{1,0:T(1,128)}, u32[]{:S(2)}) copy-start(f32[1,256]{1,0:T(1,128)} %rate_ref.5) | copy-start | bytes 3076
  19.0 12.3 %copy-start.3 = (f32[1,256]{1,0:T(1,128)S(1)}, f32[1,256]{1,0:T(1,128)}, u32[]{:S(2)}) copy-start(f32[1,256]{1,0:T(1,128)} %gate_ref.5) | copy-start | bytes 3076
  41.5 29.0 %all-to-all-start.1 = ((bf16[16,2,16,256]{3,2,1,0:T(8,128)(2,1)}), bf16[16,2,16,256]{3,2,1,0:T(8,128)(2,1)S(1)}, u32[]{:S(2)}, u32[]{:S(2)}) async-start(bf16[16,2,16,256]{3,2,1,0:T(8,128)(2,1)} %bitcast.21), calls=%async_computation.1 | async-start | bytes 524288 | tf_op jit(solution)/shard_map/all_to_all | solution.py:241
  47.0 10.7 %collective-permute-start.2 = (bf16[144,512]{1,0:T(8,128)(2,1)S(1)}, bf16[144,512]{1,0:T(8,128)(2,1)S(1)}, u32[]{:S(2)}, u32[]{:S(2)}) collective-permute-start(bf16[144,512]{1,0:T(8,128)(2,1)S(1)} %get-tuple-element.26), channel_id=1, source_target_pairs={{0,32},{32,64},{64,96},{96,0},{1,33},{33,65},{65,97},{97,1},{2,34}... | collective-permute-start | bytes 442376 | tf_op jit(solution)/shard_map/ppermute | solution.py:265
  50.2 9.3 %collective-permute-start.1 = (bf16[144,512]{1,0:T(8,128)(2,1)S(1)}, bf16[144,512]{1,0:T(8,128)(2,1)S(1)}, u32[]{:S(2)}, u32[]{:S(2)}) collective-permute-start(bf16[144,512]{1,0:T(8,128)(2,1)S(1)} %get-tuple-element.26), channel_id=1, source_target_pairs={{0,64},{32,96},{64,0},{96,32},{1,65},{33,97},{65,1},{97,33},{2,66}... | collective-permute-start | bytes 442376 | tf_op jit(solution)/shard_map/ppermute | solution.py:265
  54.8 6.2 %collective-permute-start = (bf16[144,512]{1,0:T(8,128)(2,1)S(1)}, bf16[144,512]{1,0:T(8,128)(2,1)S(1)}, u32[]{:S(2)}, u32[]{:S(2)}) collective-permute-start(bf16[144,512]{1,0:T(8,128)(2,1)S(1)} %get-tuple-element.26), channel_id=1, source_target_pairs={{0,96},{32,0},{64,32},{96,64},{1,97},{33,1},{65,33},{97,65},{2,98}... | collective-permute-start | bytes 442376 | tf_op jit(solution)/shard_map/ppermute | solution.py:265
  65.1 5.3 %copy-start.2 = (bf16[256,1,256]{2,0,1:T(8,128)(2,1)S(1)}, bf16[256,1,256]{2,0,1:T(8,128)(2,1)}, u32[]{:S(2)}) copy-start(bf16[256,1,256]{2,0,1:T(8,128)(2,1)} %param.10) | copy-start | bytes 393220
  66.6 17.3 %collective-permute-start.5 = (bf16[144,512]{1,0:T(8,128)(2,1)S(1)}, bf16[144,512]{1,0:T(8,128)(2,1)S(1)}, u32[]{:S(2)}, u32[]{:S(2)}) collective-permute-start(bf16[144,512]{1,0:T(8,128)(2,1)S(1)} %get-tuple-element.27), channel_id=1, source_target_pairs={{384,0},{385,1},{386,2},{387,3},{388,4},{389,5},{390,6},{391,7},{3... | collective-permute-start | bytes 442376 | tf_op jit(solution)/shard_map/ppermute | solution.py:276
  67.9 16.0 %collective-permute-start.4 = (bf16[144,512]{1,0:T(8,128)(2,1)S(1)}, bf16[144,512]{1,0:T(8,128)(2,1)S(1)}, u32[]{:S(2)}, u32[]{:S(2)}) collective-permute-start(bf16[144,512]{1,0:T(8,128)(2,1)S(1)} %get-tuple-element.27), channel_id=1, source_target_pairs={{256,0},{384,128},{257,1},{385,129},{258,2},{386,130},{259,3},{387... | collective-permute-start | bytes 442376 | tf_op jit(solution)/shard_map/ppermute | solution.py:276
  69.2 14.7 %collective-permute-start.3 = (bf16[144,512]{1,0:T(8,128)(2,1)S(1)}, bf16[144,512]{1,0:T(8,128)(2,1)S(1)}, u32[]{:S(2)}, u32[]{:S(2)}) collective-permute-start(bf16[144,512]{1,0:T(8,128)(2,1)S(1)} %get-tuple-element.27), channel_id=1, source_target_pairs={{128,0},{256,128},{384,256},{129,1},{257,129},{385,257},{130,2},{2... | collective-permute-start | bytes 442376 | tf_op jit(solution)/shard_map/ppermute | solution.py:276
  72.1 23.9 %all-to-all-start.2 = ((bf16[16,16,256]{2,1,0:T(8,128)(2,1)}), bf16[16,16,256]{2,1,0:T(8,128)(2,1)S(1)}, u32[]{:S(2)}, u32[]{:S(2)}) async-start(bf16[16,16,256]{2,1,0:T(8,128)(2,1)} %get-tuple-element.24), calls=%async_computation.2 | async-start | bytes 262144 | tf_op jit(solution)/shard_map/all_to_all | solution.py:241
  96.0 19.0 %all-to-all-start.3 = ((bf16[16,16,384]{2,1,0:T(8,128)(2,1)}), bf16[16,16,384]{2,1,0:T(8,128)(2,1)S(1)}, u32[]{:S(2)}, u32[]{:S(2)}) async-start(bf16[16,16,384]{2,1,0:T(8,128)(2,1)} %get-tuple-element.34), calls=%async_computation.3 | async-start | bytes 393216 | tf_op jit(solution)/shard_map/all_to_all | solution.py:241
  116.9 19.4 %all-to-all-start.4 = ((f32[32,1,128]{2,1,0:T(1,128)}), f32[32,1,128]{2,1,0:T(1,128)S(1)}, u32[]{:S(2)}, u32[]{:S(2)}) async-start(f32[32,1,128]{2,1,0:T(1,128)} %broadcast_in_dim.3), calls=%async_computation.4 | async-start | bytes 32768 | tf_op jit(solution)/shard_map/all_to_all | solution.py:294

commit v2 on v1

--- a/solution.py
+++ b/solution.py
@@ -175,7 +175,7 @@
 
 
 def final_kernel(halves_ref, em_ref, eb_ref, kq_ref, grad_ref, gate_ref, rate_ref, inv_ref, wt_ref, lg_ref,
-                 state_ref, nv_ref, ct_ref, sum_ref, gk_ref, gv_ref):
+                 state_ref, nv_ref, ct_ref, sum_ref, gq_ref, out_ref, gv_ref):
     key_t = head_rows(kq_ref, 0)
     query_t = head_rows(kq_ref, 1)
     later = None
@@ -184,6 +184,7 @@
         later = b if later is None else decay * later + b - nn(m.astype(BF16), later.astype(BF16))
     state_grad = eb_ref[K : K + 1, :1] * later + eb_ref[:K, :] - nn(em_ref[...], later.astype(BF16))
     total = sum_ref[:1, :1]
+    out_ref[:, :16, :] = gq_ref[...]
     for g in (1, 0):
         span = slice(g * N, (g + 1) * N)
         rate = rate_ref[:, span]
@@ -199,7 +200,7 @@
         gv_ref[span, :] = gv
         write_t = (-nt(state_ref[:, g].reshape(K, V), rounded)).astype(BF16)
         gk = (ct_ref[:, span] + away * nt(high, nv_ref[span, :]) + (rate * into) * nn(write_t, inverse)).astype(BF16)
-        gk_ref[:, :, span] = gk.reshape(16, 16, N)
+        out_ref[:, 16:32, span] = gk.reshape(16, 16, N)
         total += jnp.sum(jnp.square(gk.astype(F32)), keepdims=True) + jnp.sum(
             jnp.square(gv.astype(F32)), keepdims=True
         )
@@ -213,9 +214,20 @@
     high = total.astype(BF16).astype(F32)
     middle = (total - high).astype(BF16).astype(F32)
     low = total - high - middle
-    rows = lax.broadcasted_iota(jnp.int32, (16, 128), 0)
+    rows = lax.broadcasted_iota(jnp.int32, (8, 2 * N), 0)
     pieces = jnp.where(rows == 0, high, jnp.where(rows == 1, middle, jnp.where(rows == 2, low, 0.0)))
-    gk_ref[:, :, 2 * N :] = jnp.broadcast_to(pieces.astype(BF16)[None], (16, 16, 128))
+    out_ref[:, 32:, :] = jnp.broadcast_to(pieces.astype(BF16)[None], (16, 8, 2 * N))
+
+
+def join_kernel(key_ref, query_ref, out_ref):
+    out_ref[:, :16, :] = key_ref[...]
+    out_ref[:, 16:, :] = query_ref[...]
+
+
+def spread_kernel(back_ref, out_ref):
+    pieces = jnp.sum(back_ref[:, 32:, :].astype(F32), axis=0)[:, :128]
+    total = jnp.sum(pieces, axis=0, keepdims=True)
+    out_ref[...] = jnp.broadcast_to(total[None], (32, 1, 128))
 
 
 def call(kernel, outs, args, flops, scratch=(), scalars=0):
@@ -244,7 +256,8 @@
 def local(query_rows, key_rows, value_rows, out_grad, log_gates, write_rate, group_inverse, states):
     keys = jnp.transpose(key_rows, (1, 2, 0))
     queries = jnp.transpose(query_rows, (1, 2, 0))
-    kq = to_heads(jnp.concatenate([keys, queries], axis=1))
+    (joined,) = call(join_kernel, [shape((16, 32, 2 * N))], (keys, queries), 0)
+    kq = to_heads(joined)
     grad = out_grad.reshape(2 * N, V)
     values = value_rows.reshape(2 * N, V)
     place = jnp.stack([lax.axis_index("y"), lax.axis_index("c")]).astype(jnp.int32)
@@ -258,9 +271,8 @@
     )
     pair = lax.all_gather(device_map, "c")
     pair_half, pair_full = call(pair_kernel, [half, full], (place, pair), 10**8, scalars=1)
-    state_blocks = jnp.transpose(states, (1, 0, 2, 3))
-    state_blocks, pair_half = lax.optimization_barrier((state_blocks, pair_half))
-    state_heads = to_heads(state_blocks)
+    states, pair_half = lax.optimization_barrier((states, pair_half))
+    state_heads = to_heads(jnp.transpose(states, (1, 0, 2, 3)))
     around = [
         lax.ppermute(pair_half, "y", [(s, (s - d) % 4) for s in range(4)]) for d in (1, 2, 3)
     ]
@@ -269,34 +281,32 @@
         plane_kernel,
         [half, shape((K, K)), shape((K + 8, V), F32)],
         (place, pair, pair_full, pair_halves),
-        5 * 10**8,
+        6 * 10**10,
         scratch=[pltpu.VMEM((4, K + PAD, W2), BF16), pltpu.VMEM((K, W2), BF16), pltpu.VMEM((8, 128), F32)],
         scalars=1,
     )
     later = [lax.ppermute(plane_half, "x", [(s, s - d) for s in range(d, 4)]) for d in (1, 2, 3)]
-    plane_halves = lax.all_gather(jnp.stack(later), "c")
-
     gq, fresh, score_term, query_sum = call(
         ahead_kernel,
         [shape((16, 16, 2 * N)), shape((2 * N, V)), square, shape((8, 128), F32)],
         (*basics, written_t, values, state_heads),
         2 * 10**8,
     )
-    grad_query = to_heads(gq)
-    gk, grad_value = call(
+    later, gq = lax.optimization_barrier((later, gq))
+    plane_halves = lax.all_gather(jnp.stack(later), "c")
+    gathered, grad_value = call(
         final_kernel,
-        [shape((16, 16, 3 * N)), shape((2 * N, V))],
-        (plane_halves, end_m, end_b, *basics, written_t, local_grad, state_heads, fresh, score_term, query_sum),
+        [shape((16, 40, 2 * N)), shape((2 * N, V))],
+        (plane_halves, end_m, end_b, *basics, written_t, local_grad, state_heads, fresh, score_term, query_sum, gq),
         4 * 10**8,
     )
-    gk = to_heads(gk)
-    part = jnp.sum(gk[:, :3, 2 * N].astype(F32))
-    parts = lax.all_to_all(jnp.full((32, 1, 128), part), SEQ, 0, 0, tiled=True)
+    back = to_heads(gathered)
+    (spread,) = call(spread_kernel, [shape((32, 1, 128), F32)], (back,), 10**6)
+    parts = lax.all_to_all(spread, SEQ, 0, 0, tiled=True)
     grad_square = jnp.sum(parts[:, 0, 0]) / (8192 * 16 * (2 * K + V))
-    grad_key = jnp.transpose(gk[:, :, : 2 * N], (2, 0, 1))
     return (
-        jnp.transpose(grad_query, (2, 0, 1)),
-        grad_key,
+        jnp.transpose(back[:, :16], (2, 0, 1)),
+        jnp.transpose(back[:, 16:32], (2, 0, 1)),
         grad_value.reshape(2 * N, 1, V),
         grad_square,
     )

time: 140 us -> 130 us (0.929)
  blocking collectives: 14.9 us -> 41.8 us
  starting transfers between devices: 66.7 us -> 47.2 us
  waiting for transfers between devices: 41 us -> 25.6 us
  other arithmetic: 3.12 us -> 0.81 us
    all_to_all x0 -> x1, blocking collectives: none -> 23.6 us  [to_heads(): return lax.all_to_all(array, 'key', 0, 0, tiled=True)]
    all_to_all x4 -> x2, starting transfers between devices: 39.6 us -> 21.4 us  [to_heads(): return lax.all_to_all(array, 'key', 0, 0, tiled=True)]
    all_to_all x4 -> x2, waiting for transfers between devices: 31.6 us -> 16.8 us  [to_heads(): return lax.all_to_all(array, 'key', 0, 0, tiled=True)]
    all_gather x1, blocking collectives: 2.72 us -> 6.6 us  [local(): plane_halves = lax.all_gather(jnp.stack(later), 'c')]
    ppermute x3, waiting for transfers between devices: 3.19 us -> 0.01 us  [local(): lax.ppermute(pair_half, 'y', [(s, (s - d) % 4) for s in range(4)])]
    ppermute x3, waiting for transfers between devices: 0.01 us -> 2.53 us  [local(): lax.ppermute(plane_half, 'x', [(s, s - d) for s in range(d, 4)])]
    concatenate x1 -> x0, other arithmetic: 1.69 us -> none  [local(): kq = to_heads(jnp.concatenate([keys, queries], axis=1))]
    pallas_call x5 -> x7, Pallas kernels: 7.71 us -> 8.2 us  [call(): pl.pallas_call(kernel, out_shape=outs, in_specs=[smem] * scalars + [spec]...]
  transfers between devices with their start and end apart: 11 -> 9, of which waited for: 6 -> 4; matrix products, arithmetic and copies ran while one was open for 1% -> 1% of each run, Pallas kernels for 4% -> 2%
where the time goes in v2:
time: 130 us; the launch traced here: 129 us
  starting transfers between devices  47.2 us (36%)
  blocking collectives  41.8 us (32%)
  waiting for transfers between devices  25.6 us (20%)
  Pallas kernels  8.2 us (6%)
  local copies, waits for them, and re-layouts  3.27 us (3%)
  between operations  2.6 us (2%)
    all_to_all x1, blocking collectives, to_heads(): return lax.all_to_all(array, 'key', 0, 0, tiled=True)  23.6 us
    all_to_all x2, starting transfers between devices, to_heads(): return lax.all_to_all(array, 'key', 0, 0, tiled=True)  21.4 us
    all_to_all x2, waiting for transfers between devices, to_heads(): return lax.all_to_all(array, 'key', 0, 0, tiled=True)  16.8 us
    all_to_all x1, starting transfers between devices, local(): parts = lax.all_to_all(spread, SEQ, 0, 0, tiled=True)  11.2 us
    ppermute x3, starting transfers between devices, local(): lax.ppermute(pair_half, 'y', [(s, (s - d) % 4) for s in range(4)])  10.7 us
    pallas_call x7, Pallas kernels, call(): pl.pallas_call(kernel, out_shape=outs, in_specs=[smem] * scalars + [spec]...  8.2 us
    all_gather x1, blocking collectives, local(): pair = lax.all_gather(device_map, 'c')  8.01 us
    all_gather x1, blocking collectives, local(): plane_halves = lax.all_gather(jnp.stack(later), 'c')  6.6 us
  transfers between devices with their start and end apart: 9, of which 4 were waited for; matrix products, arithmetic and copies ran while one was open for 1% of the time, Pallas kernels for 2%

profile of v2, /device:TPU:1, one launch (start us, length us, event | category | flops | bytes accessed | tf_op | source)
XLA Modules:
  0.0 129.5 jit_solution(6663848090947921843)
XLA Ops:
  0.6 0.9 copy-done.3
  1.5 0.9 copy-done.4
  3.2 15.9 %all-to-all-start = ((bf16[16,32,256]{2,1,0:T(8,128)(2,1)}), bf16[16,32,256]{2,1,0:T(8,128)(2,1)S(1)}, u32[]{:S(2)}, u32[]{:S(2)}) async-start(bf16[16,32,256]{2,1,0:T(8,128)(2,1)} %shard_map.111), calls=%async_computation | async-start | bytes 524288 | tf_op jit(solution)/shard_map/all_to_all | solution.py:253
  19.1 13.0 %all-to-all-done.kq_ref = bf16[16,32,256]{2,1,0:T(8,128)(2,1)S(1)} async-done(((bf16[16,32,256]{2,1,0:T(8,128)(2,1)}), bf16[16,32,256]{2,1,0:T(8,128)(2,1)S(1)}, u32[]{:S(2)}, u32[]{:S(2)}) %all-to-all-start) | async-done | bytes 262176 | tf_op jit(solution)/shard_map/all_to_all | solution.py:253
  32.2 1.3 %shard_map.112 = (bf16[272,512]{1,0:T(8,128)(2,1)S(1)}, bf16[256,256]{1,0:T(8,128)(2,1)S(1)}, f32[256,256]{1,0:T(8,128)S(1)}) custom-call(bf16[16,32,256]{2,1,0:T(8,128)(2,1)S(1)} %all-to-all-done.kq_ref, bf16[256,256]{1,0:T(8,128)(2,1)S(1)} %bitcast.26, f32[1,256]{1,0:T(1,128)S(1)} %copy-done.5, f32[1,256]{1,0:T(1,128)S(1)} %copy-done.6, ...), custom_call_target="tpu_custom_call" | custom-call | flops 100000000 | bytes 460800 | tf_op jit(solution)/shard_map/pallas_call | solution.py:237
  33.5 8.0 %all-gather = bf16[544,512]{1,0:T(8,128)(2,1)S(1)} all-gather(bf16[272,512]{1,0:T(8,128)(2,1)S(1)} %get-tuple-element.24), channel_id=2, replica_groups=mesh['x'=4,'y'=4,'c'=2,'key'=16] {'c'}, dimensions={0}, use_global_device_ids=true | all-gather | bytes 835584 | tf_op jit(solution)/shard_map/all_gather | solution.py:272
  41.5 0.8 shard_map.113
  42.3 3.2 %collective-permute-start.2 = (bf16[144,512]{1,0:T(8,128)(2,1)S(1)}, bf16[144,512]{1,0:T(8,128)(2,1)S(1)}, u32[]{:S(2)}, u32[]{:S(2)}) collective-permute-start(bf16[144,512]{1,0:T(8,128)(2,1)S(1)} %get-tuple-element.27), channel_id=1, source_target_pairs={{0,32},{32,64},{64,96},{96,0},{1,33},{33,65},{65,97},{97,1},{2,34}... | collective-permute-start | bytes 442376 | tf_op jit(solution)/shard_map/ppermute | solution.py:277
  45.5 4.5 %collective-permute-start.1 = (bf16[144,512]{1,0:T(8,128)(2,1)S(1)}, bf16[144,512]{1,0:T(8,128)(2,1)S(1)}, u32[]{:S(2)}, u32[]{:S(2)}) collective-permute-start(bf16[144,512]{1,0:T(8,128)(2,1)S(1)} %get-tuple-element.27), channel_id=1, source_target_pairs={{0,64},{32,96},{64,0},{96,32},{1,65},{33,97},{65,1},{97,33},{2,66}... | collective-permute-start | bytes 442376 | tf_op jit(solution)/shard_map/ppermute | solution.py:277
  50.1 3.0 %collective-permute-start = (bf16[144,512]{1,0:T(8,128)(2,1)S(1)}, bf16[144,512]{1,0:T(8,128)(2,1)S(1)}, u32[]{:S(2)}, u32[]{:S(2)}) collective-permute-start(bf16[144,512]{1,0:T(8,128)(2,1)S(1)} %get-tuple-element.27), channel_id=1, source_target_pairs={{0,96},{32,0},{64,32},{96,64},{1,97},{33,1},{65,33},{97,65},{2,98}... | collective-permute-start | bytes 442376 | tf_op jit(solution)/shard_map/ppermute | solution.py:277
  53.8 5.5 %all-to-all-start.1 = ((bf16[16,2,16,256]{3,2,1,0:T(8,128)(2,1)}), bf16[16,2,16,256]{3,2,1,0:T(8,128)(2,1)S(1)}, u32[]{:S(2)}, u32[]{:S(2)}) async-start(bf16[16,2,16,256]{3,2,1,0:T(8,128)(2,1)} %bitcast.22), calls=%async_computation.1 | async-start | bytes 524288 | tf_op jit(solution)/shard_map/all_to_all | solution.py:253
  59.4 3.6 %all-gather.1 = bf16[6,144,512]{2,1,0:T(8,128)(2,1)S(1)} all-gather(bf16[3,144,512]{2,1,0:T(8,128)(2,1)S(1)} %pad_maximum_fusion), channel_id=3, replica_groups=mesh['x'=4,'y'=4,'c'=2,'key'=16] {'c'}, dimensions={0}, use_global_device_ids=true | all-gather | bytes 1327104 | tf_op jit(solution)/shard_map/all_gather | solution.py:279
  63.0 1.4 %shard_map.114 = (bf16[144,512]{1,0:T(8,128)(2,1)S(1)}, bf16[256,256]{1,0:T(8,128)(2,1)S(1)}, f32[264,256]{1,0:T(8,128)S(1)}) custom-call(s32[2]{0:T(128)S(1)} %pad_add_fusion.place_ref, bf16[2,272,512]{2,1,0:T(8,128)(2,1)S(1)} %bitcast.25, bf16[272,512]{1,0:T(8,128)(2,1)S(1)} %get-tuple-element.25.own_ref, bf16[2,3,144,512]{3,2,1,0:T(8,128)(2,1)S(1)} %bitcast.29), custom_call_target="tpu_custom_call" | custom-call | flops 60000002048 | bytes 1720328 | tf_op jit(solution)/shard_map/pallas_call | solution.py:237
  64.4 1.3 collective-permute-start.5
  65.7 1.3 collective-permute-start.4
  67.0 1.3 collective-permute-start.3
  68.3 3.8 %all-to-all-done.1.state_ref = bf16[16,2,16,256]{3,2,1,0:T(8,128)(2,1)S(1)} async-done(((bf16[16,2,16,256]{3,2,1,0:T(8,128)(2,1)}), bf16[16,2,16,256]{3,2,1,0:T(8,128)(2,1)S(1)}, u32[]{:S(2)}, u32[]{:S(2)}) %all-to-all-start.1) | async-done | bytes 262176 | tf_op jit(solution)/shard_map/all_to_all | solution.py:253
  72.1 1.1 shard_map.115
  73.2 2.5 %collective-permute-done.5 = bf16[144,512]{1,0:T(8,128)(2,1)S(1)} collective-permute-done((bf16[144,512]{1,0:T(8,128)(2,1)S(1)}, bf16[144,512]{1,0:T(8,128)(2,1)S(1)}, u32[]{:S(2)}, u32[]{:S(2)}) %collective-permute-start.5) | collective-permute-done | bytes 147488 | tf_op jit(solution)/shard_map/ppermute | solution.py:288
  75.8 6.6 %all-gather.2 = bf16[6,144,512]{2,1,0:T(8,128)(2,1)S(1)} all-gather(bf16[3,144,512]{2,1,0:T(8,128)(2,1)S(1)} %pad_maximum_fusion.1), channel_id=4, replica_groups=mesh['x'=4,'y'=4,'c'=2,'key'=16] {'c'}, dimensions={0}, use_global_device_ids=true | all-gather | bytes 1327104 | tf_op jit(solution)/shard_map/all_gather | solution.py:296
  82.4 2.2 %shard_map.116 = (bf16[16,40,256]{2,1,0:T(8,128)(2,1)S(1)}, bf16[256,256]{1,0:T(8,128)(2,1)}) custom-call(bf16[2,3,144,512]{3,2,1,0:T(8,128)(2,1)S(1)} %bitcast.23, bf16[256,256]{1,0:T(8,128)(2,1)S(1)} %get-tuple-element.35.em_ref, f32[264,256]{1,0:T(8,128)S(1)} %get-tuple-element.36.eb_ref, bf16[16,32,256]{2,1,0:T(8,128)(2,1)S(1)} %all-to-all-done.kq_ref, ...), custom_call_target="tpu_custom_call" | custom-call | flops 400000000 | bytes 2930688 | tf_op jit(solution)/shard_map/pallas_call | solution.py:237
  84.6 23.6 %all_to_all.20.back_ref = bf16[16,40,256]{2,1,0:T(8,128)(2,1)S(1)} all-to-all(bf16[16,40,256]{2,1,0:T(8,128)(2,1)S(1)} %get-tuple-element.42), channel_id=1, replica_groups=mesh['x'=4,'y'=4,'c'=2,'key'=16] {'key'}, dimensions={0} | all-to-all | bytes 655360 | tf_op jit(solution)/shard_map/all_to_all | solution.py:253
  108.9 11.2 %all-to-all-start.3 = ((f32[32,1,128]{2,1,0:T(1,128)}), f32[32,1,128]{2,1,0:T(1,128)S(1)}, u32[]{:S(2)}, u32[]{:S(2)}) async-start(f32[32,1,128]{2,1,0:T(1,128)} %shard_map.117), calls=%async_computation.3 | async-start | bytes 32768 | tf_op jit(solution)/shard_map/all_to_all | solution.py:305
  120.8 6.2 %all-to-all-done.3 = f32[32,1,128]{2,1,0:T(1,128)S(1)} async-done(((f32[32,1,128]{2,1,0:T(1,128)}), f32[32,1,128]{2,1,0:T(1,128)S(1)}, u32[]{:S(2)}, u32[]{:S(2)}) %all-to-all-start.3) | async-done | bytes 16416 | tf_op jit(solution)/shard_map/all_to_all | solution.py:305
  (27 shorter events, 3.6 us)
Async XLA Ops:
  0.6 0.9 copy-start.3
  1.5 0.9 copy-start.4
  3.2 29.0 %copy-start = (bf16[256,1,256]{2,0,1:T(8,128)(2,1)S(1)}, bf16[256,1,256]{2,0,1:T(8,128)(2,1)}, u32[]{:S(2)}) copy-start(bf16[256,1,256]{2,0,1:T(8,128)(2,1)} %param.11) | copy-start | bytes 393220
  3.2 29.0 %copy-start.1 = (bf16[2,1,128,128]{3,2,1,0:T(8,128)(2,1)S(1)}, bf16[2,1,128,128]{3,2,1,0:T(8,128)(2,1)}, u32[]{:S(2)}) copy-start(bf16[2,1,128,128]{3,2,1,0:T(8,128)(2,1)} %inv_ref.5) | copy-start | bytes 196612
  3.2 29.0 %all-to-all-start = ((bf16[16,32,256]{2,1,0:T(8,128)(2,1)}), bf16[16,32,256]{2,1,0:T(8,128)(2,1)S(1)}, u32[]{:S(2)}, u32[]{:S(2)}) async-start(bf16[16,32,256]{2,1,0:T(8,128)(2,1)} %shard_map.111), calls=%async_computation | async-start | bytes 524288 | tf_op jit(solution)/shard_map/all_to_all | solution.py:253
  19.0 13.1 %copy-start.6 = (f32[1,256]{1,0:T(1,128)S(1)}, f32[1,256]{1,0:T(1,128)}, u32[]{:S(2)}) copy-start(f32[1,256]{1,0:T(1,128)} %rate_ref.5) | copy-start | bytes 3076
  19.1 13.1 %copy-start.5 = (f32[1,256]{1,0:T(1,128)S(1)}, f32[1,256]{1,0:T(1,128)}, u32[]{:S(2)}) copy-start(f32[1,256]{1,0:T(1,128)} %gate_ref.5) | copy-start | bytes 3076
  41.5 11.5 %copy-start.7 = (bf16[2,16,16,256]{3,2,1,0:T(8,128)(2,1)S(1)}, bf16[2,16,16,256]{3,2,1,0:T(8,128)(2,1)}, u32[]{:S(2)}) copy-start(bf16[2,16,16,256]{3,2,1,0:T(8,128)(2,1)} %param.15) | copy-start | bytes 786436
  42.3 17.0 %collective-permute-start.2 = (bf16[144,512]{1,0:T(8,128)(2,1)S(1)}, bf16[144,512]{1,0:T(8,128)(2,1)S(1)}, u32[]{:S(2)}, u32[]{:S(2)}) collective-permute-start(bf16[144,512]{1,0:T(8,128)(2,1)S(1)} %get-tuple-element.27), channel_id=1, source_target_pairs={{0,32},{32,64},{64,96},{96,0},{1,33},{33,65},{65,97},{97,1},{2,34}... | collective-permute-start | bytes 442376 | tf_op jit(solution)/shard_map/ppermute | solution.py:277
  45.5 13.8 %collective-permute-start.1 = (bf16[144,512]{1,0:T(8,128)(2,1)S(1)}, bf16[144,512]{1,0:T(8,128)(2,1)S(1)}, u32[]{:S(2)}, u32[]{:S(2)}) collective-permute-start(bf16[144,512]{1,0:T(8,128)(2,1)S(1)} %get-tuple-element.27), channel_id=1, source_target_pairs={{0,64},{32,96},{64,0},{96,32},{1,65},{33,97},{65,1},{97,33},{2,66}... | collective-permute-start | bytes 442376 | tf_op jit(solution)/shard_map/ppermute | solution.py:277
  50.1 9.3 %collective-permute-start = (bf16[144,512]{1,0:T(8,128)(2,1)S(1)}, bf16[144,512]{1,0:T(8,128)(2,1)S(1)}, u32[]{:S(2)}, u32[]{:S(2)}) collective-permute-start(bf16[144,512]{1,0:T(8,128)(2,1)S(1)} %get-tuple-element.27), channel_id=1, source_target_pairs={{0,96},{32,0},{64,32},{96,64},{1,97},{33,1},{65,33},{97,65},{2,98}... | collective-permute-start | bytes 442376 | tf_op jit(solution)/shard_map/ppermute | solution.py:277
  53.8 18.3 %all-to-all-start.1 = ((bf16[16,2,16,256]{3,2,1,0:T(8,128)(2,1)}), bf16[16,2,16,256]{3,2,1,0:T(8,128)(2,1)S(1)}, u32[]{:S(2)}, u32[]{:S(2)}) async-start(bf16[16,2,16,256]{3,2,1,0:T(8,128)(2,1)} %bitcast.22), calls=%async_computation.1 | async-start | bytes 524288 | tf_op jit(solution)/shard_map/all_to_all | solution.py:253
  63.0 9.1 %copy-start.2 = (bf16[256,1,256]{2,0,1:T(8,128)(2,1)S(1)}, bf16[256,1,256]{2,0,1:T(8,128)(2,1)}, u32[]{:S(2)}) copy-start(bf16[256,1,256]{2,0,1:T(8,128)(2,1)} %param.10) | copy-start | bytes 393220
  64.4 11.3 %collective-permute-start.5 = (bf16[144,512]{1,0:T(8,128)(2,1)S(1)}, bf16[144,512]{1,0:T(8,128)(2,1)S(1)}, u32[]{:S(2)}, u32[]{:S(2)}) collective-permute-start(bf16[144,512]{1,0:T(8,128)(2,1)S(1)} %get-tuple-element.28), channel_id=1, source_target_pairs={{384,0},{385,1},{386,2},{387,3},{388,4},{389,5},{390,6},{391,7},{3... | collective-permute-start | bytes 442376 | tf_op jit(solution)/shard_map/ppermute | solution.py:288
  65.7 10.0 %collective-permute-start.4 = (bf16[144,512]{1,0:T(8,128)(2,1)S(1)}, bf16[144,512]{1,0:T(8,128)(2,1)S(1)}, u32[]{:S(2)}, u32[]{:S(2)}) collective-permute-start(bf16[144,512]{1,0:T(8,128)(2,1)S(1)} %get-tuple-element.28), channel_id=1, source_target_pairs={{256,0},{384,128},{257,1},{385,129},{258,2},{386,130},{259,3},{387... | collective-permute-start | bytes 442376 | tf_op jit(solution)/shard_map/ppermute | solution.py:288
  67.0 8.7 %collective-permute-start.3 = (bf16[144,512]{1,0:T(8,128)(2,1)S(1)}, bf16[144,512]{1,0:T(8,128)(2,1)S(1)}, u32[]{:S(2)}, u32[]{:S(2)}) collective-permute-start(bf16[144,512]{1,0:T(8,128)(2,1)S(1)} %get-tuple-element.28), channel_id=1, source_target_pairs={{128,0},{256,128},{384,256},{129,1},{257,129},{385,257},{130,2},{2... | collective-permute-start | bytes 442376 | tf_op jit(solution)/shard_map/ppermute | solution.py:288
  108.9 18.2 %all-to-all-start.3 = ((f32[32,1,128]{2,1,0:T(1,128)}), f32[32,1,128]{2,1,0:T(1,128)S(1)}, u32[]{:S(2)}, u32[]{:S(2)}) async-start(f32[32,1,128]{2,1,0:T(1,128)} %shard_map.117), calls=%async_computation.3 | async-start | bytes 32768 | tf_op jit(solution)/shard_map/all_to_all | solution.py:305

commit v3 on v1

--- a/solution.py
+++ b/solution.py
@@ -11,8 +11,11 @@
 N = 128
 K = 256
 V = 256
-W2 = K + V
+HALF = V // 2
 PAD = 16
+PAIRS = [(0, 1), (1, 0), (2, 3), (3, 2)]
+CROSS = [(0, 3), (3, 0), (1, 2), (2, 1)]
+HIDING = 6 * 10**10
 
 
 def nn(a, b):
@@ -64,11 +67,16 @@
     return decay1 * decay2, decay2 * m1 + decay1 * m2 - both[:, :K], decay1 * b2 + b1 - both[:, K:]
 
 
-def decay_rows(decay):
+def apply(first, state):
+    decay, m, b = first
+    return decay * state + b - nn(m.astype(BF16), state.astype(BF16))
+
+
+def decay_rows(decay, width):
     high = decay.astype(BF16).astype(F32)
     middle = (decay - high).astype(BF16).astype(F32)
     low = decay - high - middle
-    rows = lax.broadcasted_iota(jnp.int32, (PAD, W2), 0)
+    rows = lax.broadcasted_iota(jnp.int32, (PAD, width), 0)
     return jnp.where(rows == 0, high, jnp.where(rows == 1, middle, jnp.where(rows == 2, low, 0.0))).astype(BF16)
 
 
@@ -80,9 +88,26 @@
     return decay_from(block[K:]), block[:K, :K].astype(F32), block[:K, K:].astype(F32)
 
 
-def unpack_halves(low, high):
-    body = jnp.concatenate([low[: K // 2], high[: K // 2]], axis=0)
-    return decay_from(low[K // 2 :]), body[:, :K].astype(F32), body[:, K:].astype(F32)
+def pack(ref, decayed):
+    decay, m, b = decayed
+    ref[:K, :K] = m.astype(BF16)
+    ref[:K, K:] = b.astype(BF16)
+    ref[K:, :] = decay_rows(decay, ref.shape[1])
+
+
+def keep(ref, decayed):
+    decay, m, b = decayed
+    ref[:K, :K] = m
+    ref[:K, K:] = b
+    ref[K:, :] = jnp.broadcast_to(decay, (8, ref.shape[1]))
+
+
+def kept(ref):
+    return ref[K : K + 1, :1], ref[:K, :K], ref[:K, K:]
+
+
+def choose(flag, if_set, if_not):
+    return tuple(jnp.where(flag, p, q) for p, q in zip(if_set, if_not))
 
 
 def head_rows(kq_ref, which):
@@ -110,46 +135,44 @@
         lg_ref[span, :] = lg
         offset = nn(in_t, grad) - nn2(wt, lg)
         maps.append((jnp.exp(gamma_end), nt(wt, out_t), offset))
-    decay, m, b = compose(*maps)
-    map_ref[:K, :K] = m.astype(BF16)
-    map_ref[:K, K:] = b.astype(BF16)
-    map_ref[K:, :] = decay_rows(decay)
-
-
-def pair_kernel(place_ref, pair_ref, half_ref, full_ref):
-    decay, m, b = compose(unpack(pair_ref[0]), unpack(pair_ref[1]))
-    full_ref[:K, :K] = m.astype(BF16)
-    full_ref[:K, K:] = b.astype(BF16)
-    rows = decay_rows(decay)
-    full_ref[K:, :] = rows
-    half_ref[K // 2 :, :] = rows
-    half_ref[: K // 2, :] = full_ref[pl.ds(pl.multiple_of(place_ref[1] * (K // 2), K // 2), K // 2), :]
-
-
-def plane_kernel(place_ref, pair_ref, own_ref, halves_ref, half_ref, em_ref, eb_ref, slots, body, ends):
-    y, c = place_ref[0], place_ref[1]
-    slots[y] = own_ref[...]
-    for d in range(1, 4):
-        at = lax.rem(y + d, 4)
-        slots[at, : K // 2, :] = halves_ref[0, d - 1, : K // 2, :]
-        slots[at, K // 2 : K, :] = halves_ref[1, d - 1, : K // 2, :]
-        slots[at, K:, :] = halves_ref[0, d - 1, K // 2 :, :]
-    suffix = unpack(slots[3])
-    end = (jnp.ones((1, 1), F32), jnp.zeros((K, K), F32), jnp.zeros((K, V), F32))
-    for j in (2, 1, 0):
-        here = y == j
-        end = tuple(jnp.where(here, s, e) for s, e in zip(suffix, end))
-        suffix = compose(unpack(slots[j]), suffix)
-    decay, m, b = suffix
-    body[:, :K] = m.astype(BF16)
-    body[:, K:] = b.astype(BF16)
-    half_ref[K // 2 :, :] = decay_rows(decay)
-    half_ref[: K // 2, :] = body[pl.ds(pl.multiple_of(c * (K // 2), K // 2), K // 2), :]
-    inner = compose(unpack(pair_ref[1]), end)
-    decay, m, b = tuple(jnp.where(c == 0, i, e) for i, e in zip(inner, end))
-    em_ref[...] = m.astype(BF16)
-    eb_ref[:K, :] = b
-    eb_ref[K:, :] = jnp.broadcast_to(decay, (8, V))
+    pack(map_ref, compose(*maps))
+
+
+def pair_kernel(place_ref, own_ref, other_ref, map_ref):
+    upper = place_ref[0] == 1
+
+    def half(ref):
+        decay, m, b = unpack(ref[...])
+        return decay, m, jnp.where(upper, b[:, HALF:], b[:, :HALF])
+
+    own, other = half(own_ref), half(other_ref)
+    pack(map_ref, compose(choose(upper, other, own), choose(upper, own, other)))
+
+
+def first_round_kernel(place_ref, own_ref, other_ref, map_ref, end_ref):
+    upper = place_ref[1] == 1
+    own, other = unpack(own_ref[...]), unpack(other_ref[...])
+    pack(map_ref, compose(choose(upper, other, own), choose(upper, own, other)))
+    nothing = (jnp.ones((1, 1), F32), jnp.zeros((K, K), F32), jnp.zeros((K, HALF), F32))
+    keep(end_ref, choose(upper, nothing, other))
+
+
+def second_round_kernel(place_ref, own_ref, other_ref, end_ref, map_ref, new_end_ref):
+    upper = place_ref[2] == 1
+    own, other, end = unpack(own_ref[...]), unpack(other_ref[...]), kept(end_ref)
+    pack(map_ref, compose(choose(upper, other, own), choose(upper, own, other)))
+    keep(new_end_ref, choose(upper, end, compose(end, other)))
+
+
+def last_round_kernel(place_ref, own_ref, other_ref, end_ref, b_ref, new_end_ref):
+    upper = place_ref[3] == 1
+    own, other, end = unpack(own_ref[...]), unpack(other_ref[...]), kept(end_ref)
+    b_ref[...] = apply(choose(upper, other, own), jnp.where(upper, own[2], other[2])).astype(BF16)
+    keep(new_end_ref, choose(upper, end, compose(end, other)))
+
+
+def state_kernel(b_ref, end_ref, state_ref):
+    state_ref[...] = apply(kept(end_ref), b_ref[...].astype(F32))
 
 
 def ahead_kernel(kq_ref, grad_ref, gate_ref, rate_ref, inv_ref, wt_ref, value_ref, state_ref,
@@ -174,15 +197,12 @@
     sum_ref[...] = jnp.broadcast_to(total, (8, 128))
 
 
-def final_kernel(halves_ref, em_ref, eb_ref, kq_ref, grad_ref, gate_ref, rate_ref, inv_ref, wt_ref, lg_ref,
-                 state_ref, nv_ref, ct_ref, sum_ref, gk_ref, gv_ref):
+def final_kernel(place_ref, half_ref, other_ref, kq_ref, grad_ref, gate_ref, rate_ref, inv_ref, wt_ref, lg_ref,
+                 state_ref, nv_ref, ct_ref, sum_ref, gk_ref, gv_ref, total_ref):
     key_t = head_rows(kq_ref, 0)
     query_t = head_rows(kq_ref, 1)
-    later = None
-    for d in (2, 1, 0):
-        decay, m, b = unpack_halves(halves_ref[0, d], halves_ref[1, d])
-        later = b if later is None else decay * later + b - nn(m.astype(BF16), later.astype(BF16))
-    state_grad = eb_ref[K : K + 1, :1] * later + eb_ref[:K, :] - nn(em_ref[...], later.astype(BF16))
+    state_grad = jnp.concatenate([half_ref[0], half_ref[1]], axis=1)
+    state_grad = jnp.where(place_ref[0] == 0, apply(unpack(other_ref[...]), state_grad), state_grad)
     total = sum_ref[:1, :1]
     for g in (1, 0):
         span = slice(g * N, (g + 1) * N)
@@ -210,12 +230,34 @@
                 + nn(in_t, grad_ref[span, :])
                 - nn2(wt_ref[:, span], value_grad)
             )
+    total_ref[...] = jnp.broadcast_to(total[None], (32, 1, 128))
+
+
+def join_kernel(key_ref, query_ref, out_ref):
+    out_ref[:, :16, :] = key_ref[...]
+    out_ref[:, 16:, :] = query_ref[...]
+
+
+def send_kernel(gq_ref, gk_ref, parts_ref, out_ref):
+    total = jnp.sum(parts_ref[...], axis=0)
     high = total.astype(BF16).astype(F32)
     middle = (total - high).astype(BF16).astype(F32)
     low = total - high - middle
-    rows = lax.broadcasted_iota(jnp.int32, (16, 128), 0)
+    rows = lax.broadcasted_iota(jnp.int32, (16, N), 0)
     pieces = jnp.where(rows == 0, high, jnp.where(rows == 1, middle, jnp.where(rows == 2, low, 0.0)))
-    gk_ref[:, :, 2 * N :] = jnp.broadcast_to(pieces.astype(BF16)[None], (16, 16, 128))
+    for at, ref in ((0, gq_ref), (32, gk_ref)):
+        out_ref[:, at : at + 16, :] = ref[:, :, :N]
+        out_ref[:, at + 16 : at + 32, :] = ref[:, :, N:]
+    out_ref[:, 64:, :] = jnp.broadcast_to(pieces.astype(BF16)[None], (16, 16, N))
+
+
+def receive_kernel(back_ref, gq_ref, gk_ref, square_ref):
+    for at, ref in ((0, gq_ref), (32, gk_ref)):
+        ref[:, :, :N] = back_ref[:, at : at + 16, :]
+        ref[:, :, N:] = back_ref[:, at + 16 : at + 32, :]
+    pieces = jnp.sum(back_ref[:, 64:, :].astype(F32), axis=0)
+    total = jnp.sum(pieces, axis=0, keepdims=True)
+    square_ref[...] = total[:, :1] * (1.0 / (8192 * 16 * (2 * K + V)))
 
 
 def call(kernel, outs, args, flops, scratch=(), scalars=0):
@@ -244,37 +286,33 @@
 def local(query_rows, key_rows, value_rows, out_grad, log_gates, write_rate, group_inverse, states):
     keys = jnp.transpose(key_rows, (1, 2, 0))
     queries = jnp.transpose(query_rows, (1, 2, 0))
-    kq = to_heads(jnp.concatenate([keys, queries], axis=1))
+    (joined,) = call(join_kernel, [shape((16, 32, 2 * N))], (keys, queries), 0)
+    kq = to_heads(joined)
     grad = out_grad.reshape(2 * N, V)
     values = value_rows.reshape(2 * N, V)
-    place = jnp.stack([lax.axis_index("y"), lax.axis_index("c")]).astype(jnp.int32)
-    half = shape((K // 2 + PAD, W2))
-    full = shape((K + PAD, W2))
+    x, y, c = (lax.axis_index(name) for name in SEQ)
+    place = jnp.stack([c, y & 1, y >> 1, x & 1]).astype(jnp.int32)
+    chip_map = shape((K + PAD, K + HALF))
+    end_map = shape((K + 8, K + HALF), F32)
     square = shape((K, V), F32)
     basics = (kq, grad, log_gates, write_rate, group_inverse)
 
     device_map, written_t, local_grad = call(
-        local_map_kernel, [full, shape((K, 2 * N)), square], basics, 10**8
-    )
-    pair = lax.all_gather(device_map, "c")
-    pair_half, pair_full = call(pair_kernel, [half, full], (place, pair), 10**8, scalars=1)
-    state_blocks = jnp.transpose(states, (1, 0, 2, 3))
-    state_blocks, pair_half = lax.optimization_barrier((state_blocks, pair_half))
-    state_heads = to_heads(state_blocks)
-    around = [
-        lax.ppermute(pair_half, "y", [(s, (s - d) % 4) for s in range(4)]) for d in (1, 2, 3)
-    ]
-    pair_halves = lax.all_gather(jnp.stack(around), "c")
-    plane_half, end_m, end_b = call(
-        plane_kernel,
-        [half, shape((K, K)), shape((K + 8, V), F32)],
-        (place, pair, pair_full, pair_halves),
-        5 * 10**8,
-        scratch=[pltpu.VMEM((4, K + PAD, W2), BF16), pltpu.VMEM((K, W2), BF16), pltpu.VMEM((8, 128), F32)],
-        scalars=1,
-    )
-    later = [lax.ppermute(plane_half, "x", [(s, s - d) for s in range(d, 4)]) for d in (1, 2, 3)]
-    plane_halves = lax.all_gather(jnp.stack(later), "c")
+        local_map_kernel, [shape((K + PAD, K + V)), shape((K, 2 * N)), square], basics, 10**8
+    )
+    states, device_map = lax.optimization_barrier((states, device_map))
+    state_heads = to_heads(jnp.transpose(states, (1, 0, 2, 3)))
+    chip_other = lax.ppermute(device_map, "c", [(0, 1), (1, 0)])
+    (now,) = call(pair_kernel, [chip_map], (place, device_map, chip_other), HIDING, scalars=1)
+    other = lax.ppermute(now, "y", PAIRS)
+    now, end = call(first_round_kernel, [chip_map, end_map], (place, now, other), 10**8, scalars=1)
+    other = lax.ppermute(now, "y", CROSS)
+    now, end = call(second_round_kernel, [chip_map, end_map], (place, now, other, end), 10**8, scalars=1)
+    other = lax.ppermute(now, "x", PAIRS)
+    now, end = call(
+        last_round_kernel, [shape((K, HALF)), end_map], (place, now, other, end), 10**8, scalars=1
+    )
+    later = lax.ppermute(now, "x", [(2, 1), (3, 0)])
 
     gq, fresh, score_term, query_sum = call(
         ahead_kernel,
@@ -282,23 +320,29 @@
         (*basics, written_t, values, state_heads),
         2 * 10**8,
     )
-    grad_query = to_heads(gq)
-    gk, grad_value = call(
+    later, gq = lax.optimization_barrier((later, gq))
+    (state_half,) = call(state_kernel, [shape((K, HALF), F32)], (later, end), 10**8)
+    state_halves = lax.all_gather(state_half, "c")
+    gk, grad_value, total = call(
         final_kernel,
-        [shape((16, 16, 3 * N)), shape((2 * N, V))],
-        (plane_halves, end_m, end_b, *basics, written_t, local_grad, state_heads, fresh, score_term, query_sum),
+        [shape((16, 16, 2 * N)), shape((2 * N, V)), shape((32, 1, 128), F32)],
+        (place, state_halves, chip_other, *basics, written_t, local_grad, state_heads, fresh, score_term, query_sum),
         4 * 10**8,
-    )
-    gk = to_heads(gk)
-    part = jnp.sum(gk[:, :3, 2 * N].astype(F32))
-    parts = lax.all_to_all(jnp.full((32, 1, 128), part), SEQ, 0, 0, tiled=True)
-    grad_square = jnp.sum(parts[:, 0, 0]) / (8192 * 16 * (2 * K + V))
-    grad_key = jnp.transpose(gk[:, :, : 2 * N], (2, 0, 1))
+        scalars=1,
+    )
+    parts = lax.all_to_all(total, SEQ, 0, 0, tiled=True)
+    (sent,) = call(send_kernel, [shape((16, 80, N))], (gq, gk, parts), 10**6)
+    grad_query, grad_key, grad_square = call(
+        receive_kernel,
+        [shape((16, 16, 2 * N)), shape((16, 16, 2 * N)), shape((1, 1), F32)],
+        (to_heads(sent),),
+        10**6,
+    )
     return (
         jnp.transpose(grad_query, (2, 0, 1)),
-        grad_key,
+        jnp.transpose(grad_key, (2, 0, 1)),
         grad_value.reshape(2 * N, 1, V),
-        grad_square,
+        grad_square.reshape(()),
     )
 
 

time: 140 us -> 133 us (0.950)
  the two profiles are of different devices: /device:TPU:1 before, /device:TPU:64 now
where the time goes in v3:
time: 133 us
  blocking collectives  79.1 us (59%)
  starting transfers between devices  21 us (16%)
  waiting for transfers between devices  19 us (14%)
  Pallas kernels  9.21 us (7%)
  local copies, waits for them, and re-layouts  3.21 us (2%)
    all_to_all x2, blocking collectives, to_heads(): return lax.all_to_all(array, 'key', 0, 0, tiled=True)  65.4 us
    all_to_all x1, blocking collectives, local(): parts = lax.all_to_all(total, SEQ, 0, 0, tiled=True)  11.8 us
    pallas_call x11, Pallas kernels, call(): pl.pallas_call(kernel, out_shape=outs, in_specs=[smem] * scalars + [spec]...  9.21 us
    all_to_all x1, starting transfers between devices, to_heads(): return lax.all_to_all(array, 'key', 0, 0, tiled=True)  6 us
    ppermute x1, waiting for transfers between devices, local(): other = lax.ppermute(now, 'y', PAIRS)  5.41 us
    ppermute x1, waiting for transfers between devices, local(): later = lax.ppermute(now, 'x', [(2, 1), (3, 0)])  4.95 us
    ppermute x1, starting transfers between devices, local(): other = lax.ppermute(now, 'y', CROSS)  4.93 us
    ppermute x1, waiting for transfers between devices, local(): other = lax.ppermute(now, 'y', CROSS)  4.39 us
  transfers between devices with their start and end apart: 6, of which 4 were waited for; matrix products, arithmetic and copies ran while one was open for 1% of the time, Pallas kernels for 3%

profile of v3, /device:TPU:64, one launch (start us, length us, event | category | flops | bytes accessed | tf_op | source)
XLA Modules:
  0.0 132.5 jit_solution(11529509228850220767)
XLA Ops:
  0.6 0.9 copy-done.3
  1.5 0.9 copy-done.4
  2.5 32.8 %all_to_all.20.kq_ref = bf16[16,32,256]{2,1,0:T(8,128)(2,1)S(1)} all-to-all(bf16[16,32,256]{2,1,0:T(8,128)(2,1)S(1)} %shard_map.111), channel_id=1, replica_groups=mesh['x'=4,'y'=4,'c'=2,'key'=16] {'key'}, dimensions={0} | all-to-all | bytes 524288 | tf_op jit(solution)/shard_map/all_to_all | solution.py:283
  36.0 1.3 shard_map.112
  37.3 1.9 %collective-permute-start = (bf16[272,512]{1,0:T(8,128)(2,1)S(1)}, bf16[272,512]{1,0:T(8,128)(2,1)S(1)}, u32[]{:S(2)}, u32[]{:S(2)}) collective-permute-start(bf16[272,512]{1,0:T(8,128)(2,1)S(1)} %get-tuple-element.28.own_ref), channel_id=1, source_target_pairs={{0,16},{16,0},{1,17},{17,1},{2,18},{18,2},{3,19},{19,3},{4,20},{20... | collective-permute-start | bytes 835592 | tf_op jit(solution)/shard_map/ppermute | solution.py:305
  40.1 6.0 %all-to-all-start.1 = ((bf16[16,2,16,256]{3,2,1,0:T(8,128)(2,1)}), bf16[16,2,16,256]{3,2,1,0:T(8,128)(2,1)S(1)}, u32[]{:S(2)}, u32[]{:S(2)}) async-start(bf16[16,2,16,256]{3,2,1,0:T(8,128)(2,1)} %bitcast.15), calls=%async_computation.1 | async-start | bytes 524288 | tf_op jit(solution)/shard_map/all_to_all | solution.py:283
  46.1 0.8 shard_map.113.own_ref
  46.9 3.5 %collective-permute-start.1 = (bf16[272,384]{1,0:T(8,128)(2,1)S(1)}, bf16[272,384]{1,0:T(8,128)(2,1)S(1)}, u32[]{:S(2)}, u32[]{:S(2)}) collective-permute-start(bf16[272,384]{1,0:T(8,128)(2,1)S(1)} %shard_map.113.own_ref), channel_id=1, source_target_pairs={{0,32},{32,0},{64,96},{96,64},{1,33},{33,1},{65,97},{97,65},{2,34}... | collective-permute-start | bytes 626696 | tf_op jit(solution)/shard_map/ppermute | solution.py:307
  50.4 5.4 %collective-permute-done.1.other_ref = bf16[272,384]{1,0:T(8,128)(2,1)S(1)} collective-permute-done((bf16[272,384]{1,0:T(8,128)(2,1)S(1)}, bf16[272,384]{1,0:T(8,128)(2,1)S(1)}, u32[]{:S(2)}, u32[]{:S(2)}) %collective-permute-start.1) | collective-permute-done | bytes 208928 | tf_op jit(solution)/shard_map/ppermute | solution.py:307
  55.8 0.8 shard_map.114
  56.6 4.9 %collective-permute-start.2 = (bf16[272,384]{1,0:T(8,128)(2,1)S(1)}, bf16[272,384]{1,0:T(8,128)(2,1)S(1)}, u32[]{:S(2)}, u32[]{:S(2)}) collective-permute-start(bf16[272,384]{1,0:T(8,128)(2,1)S(1)} %get-tuple-element.29.own_ref), channel_id=1, source_target_pairs={{0,96},{96,0},{32,64},{64,32},{1,97},{97,1},{33,65},{65,33},{2,98}... | collective-permute-start | bytes 626696 | tf_op jit(solution)/shard_map/ppermute | solution.py:309
  61.6 4.4 %collective-permute-done.2.other_ref = bf16[272,384]{1,0:T(8,128)(2,1)S(1)} collective-permute-done((bf16[272,384]{1,0:T(8,128)(2,1)S(1)}, bf16[272,384]{1,0:T(8,128)(2,1)S(1)}, u32[]{:S(2)}, u32[]{:S(2)}) %collective-permute-start.2) | collective-permute-done | bytes 208928 | tf_op jit(solution)/shard_map/ppermute | solution.py:309
  66.0 0.9 shard_map.115
  66.8 3.4 %collective-permute-start.3 = (bf16[272,384]{1,0:T(8,128)(2,1)S(1)}, bf16[272,384]{1,0:T(8,128)(2,1)S(1)}, u32[]{:S(2)}, u32[]{:S(2)}) collective-permute-start(bf16[272,384]{1,0:T(8,128)(2,1)S(1)} %get-tuple-element.31.own_ref), channel_id=1, source_target_pairs={{0,128},{128,0},{256,384},{384,256},{1,129},{129,1},{257,385},{385... | collective-permute-start | bytes 626696 | tf_op jit(solution)/shard_map/ppermute | solution.py:311
  70.2 4.3 %collective-permute-done.3.other_ref = bf16[272,384]{1,0:T(8,128)(2,1)S(1)} collective-permute-done((bf16[272,384]{1,0:T(8,128)(2,1)S(1)}, bf16[272,384]{1,0:T(8,128)(2,1)S(1)}, u32[]{:S(2)}, u32[]{:S(2)}) %collective-permute-start.3) | collective-permute-done | bytes 208928 | tf_op jit(solution)/shard_map/ppermute | solution.py:311
  74.5 0.8 shard_map.116
  75.3 1.3 collective-permute-start.4
  76.7 1.1 shard_map.117
  77.8 4.9 %collective-permute-done.4.b_ref = bf16[256,128]{1,0:T(8,128)(2,1)S(1)} collective-permute-done((bf16[256,128]{1,0:T(8,128)(2,1)S(1)}, bf16[256,128]{1,0:T(8,128)(2,1)S(1)}, u32[]{:S(2)}, u32[]{:S(2)}) %collective-permute-start.4) | collective-permute-done | bytes 65568 | tf_op jit(solution)/shard_map/ppermute | solution.py:315
  82.9 2.0 %all-gather = f32[512,128]{1,0:T(8,128)S(1)} all-gather(f32[256,128]{1,0:T(8,128)S(1)} %shard_map.118), channel_id=2, replica_groups=mesh['x'=4,'y'=4,'c'=2,'key'=16] {'c'}, dimensions={0}, use_global_device_ids=true | all-gather | bytes 393216 | tf_op jit(solution)/shard_map/all_gather | solution.py:325
  84.9 2.5 %shard_map.119 = (bf16[16,16,256]{2,1,0:T(8,128)(2,1)S(1)}, bf16[256,256]{1,0:T(8,128)(2,1)}, f32[32,1,128]{2,1,0:T(1,128)S(1)}) custom-call(s32[4]{0:T(128)S(1)} %pad_add_fusion.place_ref, f32[2,256,128]{2,1,0:T(8,128)S(1)} %bitcast.19, bf16[272,512]{1,0:T(8,128)(2,1)S(1)} %collective-permute-done.other_ref, bf16[16,32,256]{2,1,0:T(8,128)(2,1)S(1)} %all_to_all.20.kq_ref, ...), custom_call_target="tpu_custom_call" | custom-call | flops 400000000 | bytes 2054160 | tf_op jit(solution)/shard_map/pallas_call | solution.py:267
  87.4 11.8 %all_to_all.21.parts_ref = f32[32,1,128]{2,1,0:T(1,128)S(1)} all-to-all(f32[32,1,128]{2,1,0:T(1,128)S(1)} %get-tuple-element.45), channel_id=1, replica_groups=mesh['x'=4,'y'=4,'c'=2,'key'=16] {'x','y','c'}, dimensions={0} | all-to-all | bytes 32768 | tf_op jit(solution)/shard_map/all_to_all | solution.py:333
  99.2 32.6 %all_to_all.22.back_ref = bf16[16,80,128]{2,1,0:T(8,128)(2,1)S(1)} all-to-all(bf16[16,80,128]{2,1,0:T(8,128)(2,1)S(1)} %shard_map.120), channel_id=1, replica_groups=mesh['x'=4,'y'=4,'c'=2,'key'=16] {'key'}, dimensions={0} | all-to-all | bytes 655360 | tf_op jit(solution)/shard_map/all_to_all | solution.py:283
  131.8 0.7 shard_map.121
  (21 shorter events, 1.8 us)
Async XLA Ops:
  0.6 0.9 copy-start.3
  1.5 0.9 copy-start.4
  2.5 32.9 %copy-start = (bf16[256,1,256]{2,0,1:T(8,128)(2,1)S(1)}, bf16[256,1,256]{2,0,1:T(8,128)(2,1)}, u32[]{:S(2)}) copy-start(bf16[256,1,256]{2,0,1:T(8,128)(2,1)} %param.11) | copy-start | bytes 393220
  2.5 32.9 %copy-start.1 = (bf16[2,1,128,128]{3,2,1,0:T(8,128)(2,1)S(1)}, bf16[2,1,128,128]{3,2,1,0:T(8,128)(2,1)}, u32[]{:S(2)}) copy-start(bf16[2,1,128,128]{3,2,1,0:T(8,128)(2,1)} %inv_ref.5) | copy-start | bytes 196612
  2.5 32.9 %copy-start.6 = (f32[1,256]{1,0:T(1,128)S(1)}, f32[1,256]{1,0:T(1,128)}, u32[]{:S(2)}) copy-start(f32[1,256]{1,0:T(1,128)} %rate_ref.5) | copy-start | bytes 3076
  35.3 0.7 copy-start.5
  35.3 4.0 %copy-start.7 = (bf16[2,16,16,256]{3,2,1,0:T(8,128)(2,1)S(1)}, bf16[2,16,16,256]{3,2,1,0:T(8,128)(2,1)}, u32[]{:S(2)}) copy-start(bf16[2,16,16,256]{3,2,1,0:T(8,128)(2,1)} %param.15) | copy-start | bytes 786436
  37.3 8.7 %collective-permute-start = (bf16[272,512]{1,0:T(8,128)(2,1)S(1)}, bf16[272,512]{1,0:T(8,128)(2,1)S(1)}, u32[]{:S(2)}, u32[]{:S(2)}) collective-permute-start(bf16[272,512]{1,0:T(8,128)(2,1)S(1)} %get-tuple-element.28.own_ref), channel_id=1, source_target_pairs={{0,16},{16,0},{1,17},{17,1},{2,18},{18,2},{3,19},{19,3},{4,20},{20... | collective-permute-start | bytes 835592 | tf_op jit(solution)/shard_map/ppermute | solution.py:305
  40.1 36.6 %all-to-all-start.1 = ((bf16[16,2,16,256]{3,2,1,0:T(8,128)(2,1)}), bf16[16,2,16,256]{3,2,1,0:T(8,128)(2,1)S(1)}, u32[]{:S(2)}, u32[]{:S(2)}) async-start(bf16[16,2,16,256]{3,2,1,0:T(8,128)(2,1)} %bitcast.15), calls=%async_computation.1 | async-start | bytes 524288 | tf_op jit(solution)/shard_map/all_to_all | solution.py:283
  46.9 8.9 %collective-permute-start.1 = (bf16[272,384]{1,0:T(8,128)(2,1)S(1)}, bf16[272,384]{1,0:T(8,128)(2,1)S(1)}, u32[]{:S(2)}, u32[]{:S(2)}) collective-permute-start(bf16[272,384]{1,0:T(8,128)(2,1)S(1)} %shard_map.113.own_ref), channel_id=1, source_target_pairs={{0,32},{32,0},{64,96},{96,64},{1,33},{33,1},{65,97},{97,65},{2,34}... | collective-permute-start | bytes 626696 | tf_op jit(solution)/shard_map/ppermute | solution.py:307
  56.6 9.3 %collective-permute-start.2 = (bf16[272,384]{1,0:T(8,128)(2,1)S(1)}, bf16[272,384]{1,0:T(8,128)(2,1)S(1)}, u32[]{:S(2)}, u32[]{:S(2)}) collective-permute-start(bf16[272,384]{1,0:T(8,128)(2,1)S(1)} %get-tuple-element.29.own_ref), channel_id=1, source_target_pairs={{0,96},{96,0},{32,64},{64,32},{1,97},{97,1},{33,65},{65,33},{2,98}... | collective-permute-start | bytes 626696 | tf_op jit(solution)/shard_map/ppermute | solution.py:309
  66.8 7.7 %collective-permute-start.3 = (bf16[272,384]{1,0:T(8,128)(2,1)S(1)}, bf16[272,384]{1,0:T(8,128)(2,1)S(1)}, u32[]{:S(2)}, u32[]{:S(2)}) collective-permute-start(bf16[272,384]{1,0:T(8,128)(2,1)S(1)} %get-tuple-element.31.own_ref), channel_id=1, source_target_pairs={{0,128},{128,0},{256,384},{384,256},{1,129},{129,1},{257,385},{385... | collective-permute-start | bytes 626696 | tf_op jit(solution)/shard_map/ppermute | solution.py:311
  74.5 2.1 %copy-start.2 = (bf16[256,1,256]{2,0,1:T(8,128)(2,1)S(1)}, bf16[256,1,256]{2,0,1:T(8,128)(2,1)}, u32[]{:S(2)}) copy-start(bf16[256,1,256]{2,0,1:T(8,128)(2,1)} %param.10) | copy-start | bytes 393220
  75.3 7.4 %collective-permute-start.4 = (bf16[256,128]{1,0:T(8,128)(2,1)S(1)}, bf16[256,128]{1,0:T(8,128)(2,1)S(1)}, u32[]{:S(2)}, u32[]{:S(2)}) collective-permute-start(bf16[256,128]{1,0:T(8,128)(2,1)S(1)} %get-tuple-element.33), channel_id=1, source_target_pairs={{256,128},{384,0},{257,129},{385,1},{258,130},{386,2},{259,131},{3... | collective-permute-start | bytes 196616 | tf_op jit(solution)/shard_map/ppermute | solution.py:315

commit v4 on v3

--- a/solution.py
+++ b/solution.py
@@ -13,8 +13,6 @@
 V = 256
 HALF = V // 2
 PAD = 16
-PAIRS = [(0, 1), (1, 0), (2, 3), (3, 2)]
-CROSS = [(0, 3), (3, 0), (1, 2), (2, 1)]
 HIDING = 6 * 10**10
 
 
@@ -149,30 +147,21 @@
     pack(map_ref, compose(choose(upper, other, own), choose(upper, own, other)))
 
 
-def first_round_kernel(place_ref, own_ref, other_ref, map_ref, end_ref):
-    upper = place_ref[1] == 1
-    own, other = unpack(own_ref[...]), unpack(other_ref[...])
-    pack(map_ref, compose(choose(upper, other, own), choose(upper, own, other)))
-    nothing = (jnp.ones((1, 1), F32), jnp.zeros((K, K), F32), jnp.zeros((K, HALF), F32))
-    keep(end_ref, choose(upper, nothing, other))
-
-
-def second_round_kernel(place_ref, own_ref, other_ref, end_ref, map_ref, new_end_ref):
-    upper = place_ref[2] == 1
-    own, other, end = unpack(own_ref[...]), unpack(other_ref[...]), kept(end_ref)
-    pack(map_ref, compose(choose(upper, other, own), choose(upper, own, other)))
-    keep(new_end_ref, choose(upper, end, compose(end, other)))
-
-
-def last_round_kernel(place_ref, own_ref, other_ref, end_ref, b_ref, new_end_ref):
-    upper = place_ref[3] == 1
-    own, other, end = unpack(own_ref[...]), unpack(other_ref[...]), kept(end_ref)
-    b_ref[...] = apply(choose(upper, other, own), jnp.where(upper, own[2], other[2])).astype(BF16)
-    keep(new_end_ref, choose(upper, end, compose(end, other)))
-
-
-def state_kernel(b_ref, end_ref, state_ref):
-    state_ref[...] = apply(kept(end_ref), b_ref[...].astype(F32))
+def plane_kernel(place_ref, chips_ref, map_ref, end_ref):
+    suffix = unpack(chips_ref[3])
+    end = (jnp.ones((1, 1), F32), jnp.zeros((K, K), F32), jnp.zeros((K, HALF), F32))
+    for j in (2, 1, 0):
+        end = choose(place_ref[1] == j, suffix, end)
+        suffix = compose(unpack(chips_ref[j]), suffix)
+    pack(map_ref, suffix)
+    keep(end_ref, end)
+
+
+def state_kernel(place_ref, planes_ref, end_ref, state_ref):
+    state = jnp.zeros((K, HALF), F32)
+    for j in (3, 2, 1):
+        state = jnp.where(place_ref[2] < j, apply(unpack(planes_ref[j]), state), state)
+    state_ref[...] = apply(kept(end_ref), state)
 
 
 def ahead_kernel(kq_ref, grad_ref, gate_ref, rate_ref, inv_ref, wt_ref, value_ref, state_ref,
@@ -291,7 +280,7 @@
     grad = out_grad.reshape(2 * N, V)
     values = value_rows.reshape(2 * N, V)
     x, y, c = (lax.axis_index(name) for name in SEQ)
-    place = jnp.stack([c, y & 1, y >> 1, x & 1]).astype(jnp.int32)
+    place = jnp.stack([c, y, x]).astype(jnp.int32)
     chip_map = shape((K + PAD, K + HALF))
     end_map = shape((K + 8, K + HALF), F32)
     square = shape((K, V), F32)
@@ -304,15 +293,8 @@
     state_heads = to_heads(jnp.transpose(states, (1, 0, 2, 3)))
     chip_other = lax.ppermute(device_map, "c", [(0, 1), (1, 0)])
     (now,) = call(pair_kernel, [chip_map], (place, device_map, chip_other), HIDING, scalars=1)
-    other = lax.ppermute(now, "y", PAIRS)
-    now, end = call(first_round_kernel, [chip_map, end_map], (place, now, other), 10**8, scalars=1)
-    other = lax.ppermute(now, "y", CROSS)
-    now, end = call(second_round_kernel, [chip_map, end_map], (place, now, other, end), 10**8, scalars=1)
-    other = lax.ppermute(now, "x", PAIRS)
-    now, end = call(
-        last_round_kernel, [shape((K, HALF)), end_map], (place, now, other, end), 10**8, scalars=1
-    )
-    later = lax.ppermute(now, "x", [(2, 1), (3, 0)])
+    now, end = call(plane_kernel, [chip_map, end_map], (place, lax.all_gather(now, "y")), 10**8, scalars=1)
+    planes = lax.all_gather(now, "x")
 
     gq, fresh, score_term, query_sum = call(
         ahead_kernel,
@@ -320,8 +302,7 @@
         (*basics, written_t, values, state_heads),
         2 * 10**8,
     )
-    later, gq = lax.optimization_barrier((later, gq))
-    (state_half,) = call(state_kernel, [shape((K, HALF), F32)], (later, end), 10**8)
+    (state_half,) = call(state_kernel, [shape((K, HALF), F32)], (place, planes, end), 10**8, scalars=1)
     state_halves = lax.all_gather(state_half, "c")
     gk, grad_value, total = call(
         final_kernel,

time: 133 us -> 131 us (0.985)
  blocking collectives: 79.1 us -> 109 us
  waiting for transfers between devices: 19 us -> 0.01 us
  starting transfers between devices: 21 us -> 7.92 us
    all_gather x0 -> x2, blocking collectives: none -> 28.6 us  [the longest x1 14.6 us: local(): planes = lax.all_gather(now, 'x')]
    ppermute x4 -> x0, waiting for transfers between devices: 19 us -> none  [the longest x1 5.41 us: local(): other = lax.ppermute(now, 'y', PAIRS)]
    ppermute x4 -> x0, starting transfers between devices: 13.1 us -> none  [the longest x1 4.93 us: local(): other = lax.ppermute(now, 'y', CROSS)]
    all_to_all x1, blocking collectives: 11.8 us -> 13.1 us  [local(): parts = lax.all_to_all(total, SEQ, 0, 0, tiled=True)]
    pallas_call x11 -> x9, Pallas kernels: 9.21 us -> 9 us  [call(): pl.pallas_call(kernel, out_shape=outs, in_specs=[smem] * scalars + [spec]...]
  transfers between devices with their start and end apart: 6 -> 2, of which waited for: 4 -> 0; matrix products, arithmetic and copies ran while one was open for 1% -> 1% of each run, Pallas kernels for 3% -> 2%
where the time goes in v4:
time: 131 us; the launch traced here: 130 us
  blocking collectives  109 us (83%)
  Pallas kernels  9 us (7%)
  starting transfers between devices  7.92 us (6%)
  local copies, waits for them, and re-layouts  3.22 us (2%)
    all_to_all x2, blocking collectives, to_heads(): return lax.all_to_all(array, 'key', 0, 0, tiled=True)  65.4 us
    all_gather x1, blocking collectives, local(): planes = lax.all_gather(now, 'x')  14.6 us
    all_gather x1, blocking collectives, local(): lax.all_gather(now, 'y')  14 us
    all_to_all x1, blocking collectives, local(): parts = lax.all_to_all(total, SEQ, 0, 0, tiled=True)  13.1 us
    pallas_call x9, Pallas kernels, call(): pl.pallas_call(kernel, out_shape=outs, in_specs=[smem] * scalars + [spec]...  9 us
    all_to_all x1, starting transfers between devices, to_heads(): return lax.all_to_all(array, 'key', 0, 0, tiled=True)  6 us
  transfers between devices with their start and end apart: 2, of which 0 were waited for; matrix products, arithmetic and copies ran while one was open for 1% of the time, Pallas kernels for 2%

profile of v4, /device:TPU:64, one launch (start us, length us, event | category | flops | bytes accessed | tf_op | source)
XLA Modules:
  0.0 130.2 jit_solution(14344069527791607962)
XLA Ops:
  0.6 0.9 copy-done.3
  1.5 0.9 copy-done.4
  2.5 0.0 copy-start
  2.5 0.0 copy-start.6
  2.5 32.8 %all_to_all.20.kq_ref = bf16[16,32,256]{2,1,0:T(8,128)(2,1)S(1)} all-to-all(bf16[16,32,256]{2,1,0:T(8,128)(2,1)S(1)} %shard_map.111), channel_id=1, replica_groups=mesh['x'=4,'y'=4,'c'=2,'key'=16] {'key'}, dimensions={0} | all-to-all | bytes 524288 | tf_op jit(solution)/shard_map/all_to_all | solution.py:272
  35.4 0.7 copy-done.5
  36.0 1.3 %shard_map.112 = (bf16[272,512]{1,0:T(8,128)(2,1)S(1)}, bf16[256,256]{1,0:T(8,128)(2,1)S(1)}, f32[256,256]{1,0:T(8,128)S(1)}) custom-call(bf16[16,32,256]{2,1,0:T(8,128)(2,1)S(1)} %all_to_all.20.kq_ref, bf16[256,256]{1,0:T(8,128)(2,1)S(1)} %bitcast.19, f32[1,256]{1,0:T(1,128)S(1)} %copy-done.5, f32[1,256]{1,0:T(1,128)S(1)} %copy-done.6, ...), custom_call_target="tpu_custom_call" | custom-call | flops 100000000 | bytes 460800 | tf_op jit(solution)/shard_map/pallas_call | solution.py:256
  37.3 1.9 %collective-permute-start = (bf16[272,512]{1,0:T(8,128)(2,1)S(1)}, bf16[272,512]{1,0:T(8,128)(2,1)S(1)}, u32[]{:S(2)}, u32[]{:S(2)}) collective-permute-start(bf16[272,512]{1,0:T(8,128)(2,1)S(1)} %get-tuple-element.25.own_ref), channel_id=1, source_target_pairs={{0,16},{16,0},{1,17},{17,1},{2,18},{18,2},{3,19},{19,3},{4,20},{20... | collective-permute-start | bytes 835592 | tf_op jit(solution)/shard_map/ppermute | solution.py:294
  39.3 0.1 pad_add_fusion.place_ref
  39.4 0.7 copy.14
  40.1 6.0 %all-to-all-start.1 = ((bf16[16,2,16,256]{3,2,1,0:T(8,128)(2,1)}), bf16[16,2,16,256]{3,2,1,0:T(8,128)(2,1)S(1)}, u32[]{:S(2)}, u32[]{:S(2)}) async-start(bf16[16,2,16,256]{3,2,1,0:T(8,128)(2,1)} %bitcast.16), calls=%async_computation.1 | async-start | bytes 524288 | tf_op jit(solution)/shard_map/all_to_all | solution.py:272
  46.1 0.8 shard_map.114
  46.9 14.0 %all-gather = bf16[1088,384]{1,0:T(8,128)(2,1)S(1)} all-gather(bf16[272,384]{1,0:T(8,128)(2,1)S(1)} %shard_map.114), channel_id=2, replica_groups=mesh['x'=4,'y'=4,'c'=2,'key'=16] {'y'}, dimensions={0}, use_global_device_ids=true | all-gather | bytes 1044480 | tf_op jit(solution)/shard_map/all_gather | solution.py:296
  60.9 1.2 shard_map.115
  62.1 14.6 %all-gather.1 = bf16[1088,384]{1,0:T(8,128)(2,1)S(1)} all-gather(bf16[272,384]{1,0:T(8,128)(2,1)S(1)} %get-tuple-element.26), channel_id=3, replica_groups=mesh['x'=4,'y'=4,'c'=2,'key'=16] {'x'}, dimensions={0}, use_global_device_ids=true | all-gather | bytes 1044480 | tf_op jit(solution)/shard_map/all_gather | solution.py:297
  76.6 1.3 shard_map.116
  77.9 0.0 copy-start.2
  77.9 2.1 %all-gather.2 = f32[512,128]{1,0:T(8,128)S(1)} all-gather(f32[256,128]{1,0:T(8,128)S(1)} %shard_map.116), channel_id=4, replica_groups=mesh['x'=4,'y'=4,'c'=2,'key'=16] {'c'}, dimensions={0}, use_global_device_ids=true | all-gather | bytes 393216 | tf_op jit(solution)/shard_map/all_gather | solution.py:306
  80.1 1.1 shard_map.113
  81.2 2.5 %shard_map.117 = (bf16[16,16,256]{2,1,0:T(8,128)(2,1)S(1)}, bf16[256,256]{1,0:T(8,128)(2,1)}, f32[32,1,128]{2,1,0:T(1,128)S(1)}) custom-call(s32[3]{0:T(128)S(1)} %pad_add_fusion.place_ref, f32[2,256,128]{2,1,0:T(8,128)S(1)} %bitcast.22, bf16[272,512]{1,0:T(8,128)(2,1)S(1)} %collective-permute-done.other_ref, bf16[16,32,256]{2,1,0:T(8,128)(2,1)S(1)} %all_to_all.20.kq_ref, ...), custom_call_target="tpu_custom_call" | custom-call | flops 400000000 | bytes 2054156 | tf_op jit(solution)/shard_map/pallas_call | solution.py:256
  83.7 13.1 %all_to_all.21.parts_ref = f32[32,1,128]{2,1,0:T(1,128)S(1)} all-to-all(f32[32,1,128]{2,1,0:T(1,128)S(1)} %get-tuple-element.33), channel_id=1, replica_groups=mesh['x'=4,'y'=4,'c'=2,'key'=16] {'x','y','c'}, dimensions={0} | all-to-all | bytes 32768 | tf_op jit(solution)/shard_map/all_to_all | solution.py:314
  96.8 0.1 shard_map.118
  96.9 32.6 %all_to_all.22.back_ref = bf16[16,80,128]{2,1,0:T(8,128)(2,1)S(1)} all-to-all(bf16[16,80,128]{2,1,0:T(8,128)(2,1)S(1)} %shard_map.118), channel_id=1, replica_groups=mesh['x'=4,'y'=4,'c'=2,'key'=16] {'key'}, dimensions={0} | all-to-all | bytes 655360 | tf_op jit(solution)/shard_map/all_to_all | solution.py:272
  129.4 0.7 shard_map.119
  (13 shorter events, 0.0 us)
Async XLA Ops:
  0.6 0.9 copy-start.3
  1.5 0.9 copy-start.4
  2.5 32.9 %copy-start = (bf16[256,1,256]{2,0,1:T(8,128)(2,1)S(1)}, bf16[256,1,256]{2,0,1:T(8,128)(2,1)}, u32[]{:S(2)}) copy-start(bf16[256,1,256]{2,0,1:T(8,128)(2,1)} %param.11) | copy-start | bytes 393220
  2.5 32.9 %copy-start.1 = (bf16[2,1,128,128]{3,2,1,0:T(8,128)(2,1)S(1)}, bf16[2,1,128,128]{3,2,1,0:T(8,128)(2,1)}, u32[]{:S(2)}) copy-start(bf16[2,1,128,128]{3,2,1,0:T(8,128)(2,1)} %inv_ref.5) | copy-start | bytes 196612
  2.5 32.9 %copy-start.6 = (f32[1,256]{1,0:T(1,128)S(1)}, f32[1,256]{1,0:T(1,128)}, u32[]{:S(2)}) copy-start(f32[1,256]{1,0:T(1,128)} %rate_ref.5) | copy-start | bytes 3076
  35.3 0.7 copy-start.5
  35.3 4.0 %copy-start.7 = (bf16[2,16,16,256]{3,2,1,0:T(8,128)(2,1)S(1)}, bf16[2,16,16,256]{3,2,1,0:T(8,128)(2,1)}, u32[]{:S(2)}) copy-start(bf16[2,16,16,256]{3,2,1,0:T(8,128)(2,1)} %param.15) | copy-start | bytes 786436
  37.3 8.8 %collective-permute-start = (bf16[272,512]{1,0:T(8,128)(2,1)S(1)}, bf16[272,512]{1,0:T(8,128)(2,1)S(1)}, u32[]{:S(2)}, u32[]{:S(2)}) collective-permute-start(bf16[272,512]{1,0:T(8,128)(2,1)S(1)} %get-tuple-element.25.own_ref), channel_id=1, source_target_pairs={{0,16},{16,0},{1,17},{17,1},{2,18},{18,2},{3,19},{19,3},{4,20},{20... | collective-permute-start | bytes 835592 | tf_op jit(solution)/shard_map/ppermute | solution.py:294
  40.1 40.0 %all-to-all-start.1 = ((bf16[16,2,16,256]{3,2,1,0:T(8,128)(2,1)}), bf16[16,2,16,256]{3,2,1,0:T(8,128)(2,1)S(1)}, u32[]{:S(2)}, u32[]{:S(2)}) async-start(bf16[16,2,16,256]{3,2,1,0:T(8,128)(2,1)} %bitcast.16), calls=%async_computation.1 | async-start | bytes 524288 | tf_op jit(solution)/shard_map/all_to_all | solution.py:272
  77.9 2.1 %copy-start.2 = (bf16[256,1,256]{2,0,1:T(8,128)(2,1)S(1)}, bf16[256,1,256]{2,0,1:T(8,128)(2,1)}, u32[]{:S(2)}) copy-start(bf16[256,1,256]{2,0,1:T(8,128)(2,1)} %param.10) | copy-start | bytes 393220

commit v5 on v4

--- a/solution.py
+++ b/solution.py
@@ -13,6 +13,7 @@
 V = 256
 HALF = V // 2
 PAD = 16
+ROWS = K + PAD
 HIDING = 6 * 10**10
 
 
@@ -91,17 +92,6 @@
     ref[:K, :K] = m.astype(BF16)
     ref[:K, K:] = b.astype(BF16)
     ref[K:, :] = decay_rows(decay, ref.shape[1])
-
-
-def keep(ref, decayed):
-    decay, m, b = decayed
-    ref[:K, :K] = m
-    ref[:K, K:] = b
-    ref[K:, :] = jnp.broadcast_to(decay, (8, ref.shape[1]))
-
-
-def kept(ref):
-    return ref[K : K + 1, :1], ref[:K, :K], ref[:K, K:]
 
 
 def choose(flag, if_set, if_not):
@@ -147,21 +137,21 @@
     pack(map_ref, compose(choose(upper, other, own), choose(upper, own, other)))
 
 
-def plane_kernel(place_ref, chips_ref, map_ref, end_ref):
+def plane_kernel(place_ref, chips_ref, send_ref, end_ref, end_b_ref):
     suffix = unpack(chips_ref[3])
     end = (jnp.ones((1, 1), F32), jnp.zeros((K, K), F32), jnp.zeros((K, HALF), F32))
     for j in (2, 1, 0):
         end = choose(place_ref[1] == j, suffix, end)
         suffix = compose(unpack(chips_ref[j]), suffix)
-    pack(map_ref, suffix)
-    keep(end_ref, end)
-
-
-def state_kernel(place_ref, planes_ref, end_ref, state_ref):
-    state = jnp.zeros((K, HALF), F32)
-    for j in (3, 2, 1):
-        state = jnp.where(place_ref[2] < j, apply(unpack(planes_ref[j]), state), state)
-    state_ref[...] = apply(kept(end_ref), state)
+    decay, m, b = suffix
+    m_half = jnp.where(place_ref[0] == 0, m[:, :HALF], m[:, HALF:])
+    send_ref[:K, :HALF] = m_half.astype(BF16)
+    send_ref[:K, HALF:] = b.astype(BF16)
+    send_ref[K:, :] = decay_rows(decay, 2 * HALF)
+    decay, m, b = end
+    end_ref[:K, :] = m
+    end_ref[K:, :] = jnp.broadcast_to(decay, (8, K))
+    end_b_ref[...] = b.astype(BF16)
 
 
 def ahead_kernel(kq_ref, grad_ref, gate_ref, rate_ref, inv_ref, wt_ref, value_ref, state_ref,
@@ -186,12 +176,24 @@
     sum_ref[...] = jnp.broadcast_to(total, (8, 128))
 
 
-def final_kernel(place_ref, half_ref, other_ref, kq_ref, grad_ref, gate_ref, rate_ref, inv_ref, wt_ref, lg_ref,
-                 state_ref, nv_ref, ct_ref, sum_ref, gk_ref, gv_ref, total_ref):
+def state_after(place_ref, halves_ref, end_ref, other_ref):
+    low, high = (halves_ref[i, 2 * ROWS :, :].astype(F32) for i in range(2))
+    state = jnp.concatenate([low[:, :HALF], high[:, :HALF]], axis=1)
+    end_b = jnp.concatenate([low[:, HALF:], high[:, HALF:]], axis=1)
+    for d in (1, 0):
+        low, high = (halves_ref[i, ROWS * d : ROWS * (d + 1), :] for i in range(2))
+        m = jnp.concatenate([low[:K, :HALF], high[:K, :HALF]], axis=1)
+        b = jnp.concatenate([low[:K, HALF:], high[:K, HALF:]], axis=1).astype(F32)
+        state = apply((decay_from(low[K:]), m, b), state)
+    state = apply((end_ref[K : K + 1, :1], end_ref[:K, :], end_b), state)
+    return jnp.where(place_ref[0] == 0, apply(unpack(other_ref[...]), state), state)
+
+
+def final_kernel(place_ref, halves_ref, end_ref, other_ref, kq_ref, grad_ref, gate_ref, rate_ref, inv_ref, wt_ref,
+                 lg_ref, state_ref, nv_ref, ct_ref, sum_ref, gk_ref, gv_ref, total_ref):
     key_t = head_rows(kq_ref, 0)
     query_t = head_rows(kq_ref, 1)
-    state_grad = jnp.concatenate([half_ref[0], half_ref[1]], axis=1)
-    state_grad = jnp.where(place_ref[0] == 0, apply(unpack(other_ref[...]), state_grad), state_grad)
+    state_grad = state_after(place_ref, halves_ref, end_ref, other_ref)
     total = sum_ref[:1, :1]
     for g in (1, 0):
         span = slice(g * N, (g + 1) * N)
@@ -219,7 +221,7 @@
                 + nn(in_t, grad_ref[span, :])
                 - nn2(wt_ref[:, span], value_grad)
             )
-    total_ref[...] = jnp.broadcast_to(total[None], (32, 1, 128))
+    total_ref[...] = jnp.broadcast_to(total, (8, 128))
 
 
 def join_kernel(key_ref, query_ref, out_ref):
@@ -227,24 +229,22 @@
     out_ref[:, 16:, :] = query_ref[...]
 
 
-def send_kernel(gq_ref, gk_ref, parts_ref, out_ref):
-    total = jnp.sum(parts_ref[...], axis=0)
+def send_kernel(gk_ref, total_ref, out_ref):
+    total = total_ref[:1, :]
     high = total.astype(BF16).astype(F32)
     middle = (total - high).astype(BF16).astype(F32)
     low = total - high - middle
     rows = lax.broadcasted_iota(jnp.int32, (16, N), 0)
     pieces = jnp.where(rows == 0, high, jnp.where(rows == 1, middle, jnp.where(rows == 2, low, 0.0)))
-    for at, ref in ((0, gq_ref), (32, gk_ref)):
-        out_ref[:, at : at + 16, :] = ref[:, :, :N]
-        out_ref[:, at + 16 : at + 32, :] = ref[:, :, N:]
-    out_ref[:, 64:, :] = jnp.broadcast_to(pieces.astype(BF16)[None], (16, 16, N))
-
-
-def receive_kernel(back_ref, gq_ref, gk_ref, square_ref):
-    for at, ref in ((0, gq_ref), (32, gk_ref)):
-        ref[:, :, :N] = back_ref[:, at : at + 16, :]
-        ref[:, :, N:] = back_ref[:, at + 16 : at + 32, :]
-    pieces = jnp.sum(back_ref[:, 64:, :].astype(F32), axis=0)
+    out_ref[:, :16, :] = gk_ref[:, :, :N]
+    out_ref[:, 16:32, :] = gk_ref[:, :, N:]
+    out_ref[:, 32:, :] = jnp.broadcast_to(pieces.astype(BF16)[None], (16, 16, N))
+
+
+def receive_kernel(back_ref, gk_ref, square_ref):
+    gk_ref[:, :, :N] = back_ref[:, :16, :]
+    gk_ref[:, :, N:] = back_ref[:, 16:32, :]
+    pieces = jnp.sum(back_ref[:, 32:, :].astype(F32), axis=0)
     total = jnp.sum(pieces, axis=0, keepdims=True)
     square_ref[...] = total[:, :1] * (1.0 / (8192 * 16 * (2 * K + V)))
 
@@ -282,7 +282,6 @@
     x, y, c = (lax.axis_index(name) for name in SEQ)
     place = jnp.stack([c, y, x]).astype(jnp.int32)
     chip_map = shape((K + PAD, K + HALF))
-    end_map = shape((K + 8, K + HALF), F32)
     square = shape((K, V), F32)
     basics = (kq, grad, log_gates, write_rate, group_inverse)
 
@@ -293,8 +292,14 @@
     state_heads = to_heads(jnp.transpose(states, (1, 0, 2, 3)))
     chip_other = lax.ppermute(device_map, "c", [(0, 1), (1, 0)])
     (now,) = call(pair_kernel, [chip_map], (place, device_map, chip_other), HIDING, scalars=1)
-    now, end = call(plane_kernel, [chip_map, end_map], (place, lax.all_gather(now, "y")), 10**8, scalars=1)
-    planes = lax.all_gather(now, "x")
+    plane_half, end, end_b = call(
+        plane_kernel,
+        [shape((ROWS, 2 * HALF)), shape((K + 8, K), F32), shape((K, HALF))],
+        (place, lax.all_gather(now, "y")),
+        10**8,
+        scalars=1,
+    )
+    later = [lax.ppermute(plane_half, "x", [(s, s - d) for s in range(d, 4)]) for d in (1, 2, 3)]
 
     gq, fresh, score_term, query_sum = call(
         ahead_kernel,
@@ -302,22 +307,25 @@
         (*basics, written_t, values, state_heads),
         2 * 10**8,
     )
-    (state_half,) = call(state_kernel, [shape((K, HALF), F32)], (place, planes, end), 10**8, scalars=1)
-    state_halves = lax.all_gather(state_half, "c")
+    grad_query = to_heads(gq)
+    later, fresh = lax.optimization_barrier((later, fresh))
+    last = jnp.concatenate([later[2][:K, HALF:], end_b], axis=1)
+    halves = lax.all_gather(jnp.concatenate([later[0], later[1], last], axis=0), "c")
     gk, grad_value, total = call(
         final_kernel,
-        [shape((16, 16, 2 * N)), shape((2 * N, V)), shape((32, 1, 128), F32)],
-        (place, state_halves, chip_other, *basics, written_t, local_grad, state_heads, fresh, score_term, query_sum),
+        [shape((16, 16, 2 * N)), shape((2 * N, V)), shape((8, 128), F32)],
+        (
+            place, halves, end, chip_other, *basics, written_t, local_grad, state_heads, fresh, score_term,
+            query_sum,
+        ),
         4 * 10**8,
         scalars=1,
     )
-    parts = lax.all_to_all(total, SEQ, 0, 0, tiled=True)
-    (sent,) = call(send_kernel, [shape((16, 80, N))], (gq, gk, parts), 10**6)
-    grad_query, grad_key, grad_square = call(
-        receive_kernel,
-        [shape((16, 16, 2 * N)), shape((16, 16, 2 * N)), shape((1, 1), F32)],
-        (to_heads(sent),),
-        10**6,
+    for axis in ("c", "y", "x"):
+        total = lax.optimization_barrier(lax.psum(total, axis))
+    (sent,) = call(send_kernel, [shape((16, 48, N))], (gk, total), 10**6)
+    grad_key, grad_square = call(
+        receive_kernel, [shape((16, 16, 2 * N)), shape((1, 1), F32)], (to_heads(sent),), 10**6
     )
     return (
         jnp.transpose(grad_query, (2, 0, 1)),

time: 131 us -> 140 us (1.069)
  the two profiles are of different devices: /device:TPU:64 before, /device:TPU:32 now
where the time goes in v5:
time: 140 us
  blocking collectives  75.7 us (54%)
  starting transfers between devices  36.1 us (26%)
  waiting for transfers between devices  13.5 us (10%)
  Pallas kernels  9.48 us (7%)
  local copies, waits for them, and re-layouts  3.88 us (3%)
    all_to_all x1, blocking collectives, to_heads(): return lax.all_to_all(array, 'key', 0, 0, tiled=True)  33 us
    all_to_all x3, starting transfers between devices, to_heads(): return lax.all_to_all(array, 'key', 0, 0, tiled=True)  30.3 us
    psum x3, blocking collectives, local(): total = lax.optimization_barrier(lax.psum(total, axis))  26.3 us
    all_gather x1, blocking collectives, local(): lax.all_gather(now, 'y')  14 us
    all_to_all x3, waiting for transfers between devices, to_heads(): return lax.all_to_all(array, 'key', 0, 0, tiled=True)  13.5 us
    pallas_call x8, Pallas kernels, call(): pl.pallas_call(kernel, out_shape=outs, in_specs=[smem] * scalars + [spec]...  9.48 us
    ppermute x3, starting transfers between devices, local(): lax.ppermute(plane_half, 'x', [(s, s - d) for s in range(d, 4)])  3.88 us
    unnamed x17, local copies, waits for them, and re-layouts  3.14 us
  transfers between devices with their start and end apart: 7, of which 1 were waited for; matrix products, arithmetic and copies ran while one was open for 1% of the time, Pallas kernels for 5%

profile of v5, /device:TPU:32, one launch (start us, length us, event | category | flops | bytes accessed | tf_op | source)
XLA Modules:
  0.0 139.6 jit_solution(7192668807197758309)
XLA Ops:
  0.6 0.9 copy-done.3
  1.5 0.9 copy-done.4
  2.5 33.0 %all_to_all.20.kq_ref = bf16[16,32,256]{2,1,0:T(8,128)(2,1)S(1)} all-to-all(bf16[16,32,256]{2,1,0:T(8,128)(2,1)S(1)} %shard_map.111), channel_id=1, replica_groups=mesh['x'=4,'y'=4,'c'=2,'key'=16] {'key'}, dimensions={0} | all-to-all | bytes 524288 | tf_op jit(solution)/shard_map/all_to_all | solution.py:272
  36.2 1.3 shard_map.112
  37.5 1.9 %collective-permute-start = (bf16[272,512]{1,0:T(8,128)(2,1)S(1)}, bf16[272,512]{1,0:T(8,128)(2,1)S(1)}, u32[]{:S(2)}, u32[]{:S(2)}) collective-permute-start(bf16[272,512]{1,0:T(8,128)(2,1)S(1)} %get-tuple-element.29.own_ref), channel_id=1, source_target_pairs={{0,16},{16,0},{1,17},{17,1},{2,18},{18,2},{3,19},{19,3},{4,20},{20... | collective-permute-start | bytes 835592 | tf_op jit(solution)/shard_map/ppermute | solution.py:293
  39.6 0.7 copy.14
  40.3 6.2 %all-to-all-start.1 = ((bf16[16,2,16,256]{3,2,1,0:T(8,128)(2,1)}), bf16[16,2,16,256]{3,2,1,0:T(8,128)(2,1)S(1)}, u32[]{:S(2)}, u32[]{:S(2)}) async-start(bf16[16,2,16,256]{3,2,1,0:T(8,128)(2,1)} %bitcast.15), calls=%async_computation.1 | async-start | bytes 524288 | tf_op jit(solution)/shard_map/all_to_all | solution.py:272
  46.6 0.8 shard_map.114
  47.4 14.0 %all-gather = bf16[1088,384]{1,0:T(8,128)(2,1)S(1)} all-gather(bf16[272,384]{1,0:T(8,128)(2,1)S(1)} %shard_map.114), channel_id=2, replica_groups=mesh['x'=4,'y'=4,'c'=2,'key'=16] {'y'}, dimensions={0}, use_global_device_ids=true | all-gather | bytes 1044480 | tf_op jit(solution)/shard_map/all_gather | solution.py:298
  61.4 1.2 shard_map.115
  62.6 1.3 collective-permute-start.3
  63.9 1.3 collective-permute-start.2
  65.2 1.3 collective-permute-start.1
  66.5 1.6 %shard_map.113 = (bf16[16,16,256]{2,1,0:T(8,128)(2,1)}, bf16[256,256]{1,0:T(8,128)(2,1)S(1)}, f32[256,256]{1,0:T(8,128)S(1)}, f32[8,128]{1,0:T(8,128)S(1)}) custom-call(bf16[16,32,256]{2,1,0:T(8,128)(2,1)S(1)} %all_to_all.20.kq_ref, bf16[256,256]{1,0:T(8,128)(2,1)S(1)} %bitcast.19, f32[1,256]{1,0:T(1,128)S(1)} %copy-done.5, f32[1,256]{1,0:T(1,128)S(1)} %copy-done.6, ...), custom_call_target="tpu_custom_call" | custom-call | flops 200000000 | bytes 985088 | tf_op jit(solution)/shard_map/pallas_call | solution.py:256
  68.1 12.0 %all-to-all-start.2 = ((bf16[16,16,256]{2,1,0:T(8,128)(2,1)}), bf16[16,16,256]{2,1,0:T(8,128)(2,1)S(1)}, u32[]{:S(2)}, u32[]{:S(2)}) async-start(bf16[16,16,256]{2,1,0:T(8,128)(2,1)} %get-tuple-element.28), calls=%async_computation.2 | async-start | bytes 262144 | tf_op jit(solution)/shard_map/all_to_all | solution.py:272
  80.2 2.4 %all-gather.1 = bf16[1600,256]{1,0:T(8,128)(2,1)S(1)} all-gather(bf16[800,256]{1,0:T(8,128)(2,1)S(1)} %maximum_maximum_fusion), channel_id=3, replica_groups=mesh['x'=4,'y'=4,'c'=2,'key'=16] {'c'}, dimensions={0}, use_global_device_ids=true | all-gather | bytes 1228800 | tf_op jit(solution)/shard_map/all_gather | solution.py:313
  82.6 3.2 %shard_map.116 = (bf16[16,16,256]{2,1,0:T(8,128)(2,1)S(1)}, bf16[256,256]{1,0:T(8,128)(2,1)}, f32[8,128]{1,0:T(8,128)S(1)}) custom-call(s32[3]{0:T(128)S(1)} %pad_add_fusion.place_ref, bf16[2,800,256]{2,1,0:T(8,128)(2,1)S(1)} %bitcast.17, f32[264,256]{1,0:T(8,128)S(1)} %get-tuple-element.36.end_ref, bf16[272,512]{1,0:T(8,128)(2,1)S(1)} %collective-permute-done.other_ref, ...), custom_call_target="tpu_custom_call" | custom-call | flops 400000000 | bytes 2881548 | tf_op jit(solution)/shard_map/pallas_call | solution.py:256
  85.8 2.4 %psum.21 = f32[8,128]{1,0:T(8,128)S(1)} all-reduce(f32[8,128]{1,0:T(8,128)S(1)} %get-tuple-element.42), channel_id=1, replica_groups=mesh['x'=4,'y'=4,'c'=2,'key'=16] {'c'}, use_global_device_ids=true, to_apply=%region_0.0 | all-reduce | flops 1024 | bytes 8192 | tf_op jit(solution)/shard_map/psum | solution.py:325
  88.2 10.8 %psum.22 = f32[8,128]{1,0:T(8,128)S(1)} all-reduce(f32[8,128]{1,0:T(8,128)S(1)} %psum.21), channel_id=1, replica_groups=mesh['x'=4,'y'=4,'c'=2,'key'=16] {'y'}, use_global_device_ids=true, to_apply=%region_1.0 | all-reduce | flops 1024 | bytes 8192 | tf_op jit(solution)/shard_map/psum | solution.py:325
  99.0 13.1 %psum.23.total_ref = f32[8,128]{1,0:T(8,128)S(1)} all-reduce(f32[8,128]{1,0:T(8,128)S(1)} %psum.22), channel_id=1, replica_groups=mesh['x'=4,'y'=4,'c'=2,'key'=16] {'x'}, use_global_device_ids=true, to_apply=%region_2.0 | all-reduce | flops 1024 | bytes 8192 | tf_op jit(solution)/shard_map/psum | solution.py:325
  112.0 0.7 shard_map.117
  112.8 12.0 %all-to-all-start.3 = ((bf16[16,48,128]{2,1,0:T(8,128)(2,1)}), bf16[16,48,128]{2,1,0:T(8,128)(2,1)S(1)}, u32[]{:S(2)}, u32[]{:S(2)}) async-start(bf16[16,48,128]{2,1,0:T(8,128)(2,1)} %shard_map.117), calls=%async_computation.3 | async-start | bytes 393216 | tf_op jit(solution)/shard_map/all_to_all | solution.py:272
  124.8 13.5 %all-to-all-done.3.back_ref = bf16[16,48,128]{2,1,0:T(8,128)(2,1)S(1)} async-done(((bf16[16,48,128]{2,1,0:T(8,128)(2,1)}), bf16[16,48,128]{2,1,0:T(8,128)(2,1)S(1)}, u32[]{:S(2)}, u32[]{:S(2)}) %all-to-all-start.3) | async-done | bytes 196640 | tf_op jit(solution)/shard_map/all_to_all | solution.py:272
  138.3 0.7 shard_map.118
  (25 shorter events, 1.5 us)
Async XLA Ops:
  0.6 0.9 copy-start.3
  1.5 0.9 copy-start.4
  2.5 33.1 %copy-start = (bf16[256,1,256]{2,0,1:T(8,128)(2,1)S(1)}, bf16[256,1,256]{2,0,1:T(8,128)(2,1)}, u32[]{:S(2)}) copy-start(bf16[256,1,256]{2,0,1:T(8,128)(2,1)} %param.11) | copy-start | bytes 393220
  2.5 33.1 %copy-start.1 = (bf16[2,1,128,128]{3,2,1,0:T(8,128)(2,1)S(1)}, bf16[2,1,128,128]{3,2,1,0:T(8,128)(2,1)}, u32[]{:S(2)}) copy-start(bf16[2,1,128,128]{3,2,1,0:T(8,128)(2,1)} %inv_ref.5) | copy-start | bytes 196612
  2.5 33.1 %copy-start.6 = (f32[1,256]{1,0:T(1,128)S(1)}, f32[1,256]{1,0:T(1,128)}, u32[]{:S(2)}) copy-start(f32[1,256]{1,0:T(1,128)} %rate_ref.5) | copy-start | bytes 3076
  35.5 0.7 copy-start.5
  35.5 4.0 %copy-start.7 = (bf16[2,16,16,256]{3,2,1,0:T(8,128)(2,1)S(1)}, bf16[2,16,16,256]{3,2,1,0:T(8,128)(2,1)}, u32[]{:S(2)}) copy-start(bf16[2,16,16,256]{3,2,1,0:T(8,128)(2,1)} %param.15) | copy-start | bytes 786436
  37.5 9.0 %collective-permute-start = (bf16[272,512]{1,0:T(8,128)(2,1)S(1)}, bf16[272,512]{1,0:T(8,128)(2,1)S(1)}, u32[]{:S(2)}, u32[]{:S(2)}) collective-permute-start(bf16[272,512]{1,0:T(8,128)(2,1)S(1)} %get-tuple-element.29.own_ref), channel_id=1, source_target_pairs={{0,16},{16,0},{1,17},{17,1},{2,18},{18,2},{3,19},{19,3},{4,20},{20... | collective-permute-start | bytes 835592 | tf_op jit(solution)/shard_map/ppermute | solution.py:293
  40.3 26.2 %all-to-all-start.1 = ((bf16[16,2,16,256]{3,2,1,0:T(8,128)(2,1)}), bf16[16,2,16,256]{3,2,1,0:T(8,128)(2,1)S(1)}, u32[]{:S(2)}, u32[]{:S(2)}) async-start(bf16[16,2,16,256]{3,2,1,0:T(8,128)(2,1)} %bitcast.15), calls=%async_computation.1 | async-start | bytes 524288 | tf_op jit(solution)/shard_map/all_to_all | solution.py:272
  61.4 5.1 %copy-start.2 = (bf16[256,1,256]{2,0,1:T(8,128)(2,1)S(1)}, bf16[256,1,256]{2,0,1:T(8,128)(2,1)}, u32[]{:S(2)}) copy-start(bf16[256,1,256]{2,0,1:T(8,128)(2,1)} %param.10) | copy-start | bytes 393220
  62.6 17.6 %collective-permute-start.3 = (bf16[272,256]{1,0:T(8,128)(2,1)S(1)}, bf16[272,256]{1,0:T(8,128)(2,1)S(1)}, u32[]{:S(2)}, u32[]{:S(2)}) collective-permute-start(bf16[272,256]{1,0:T(8,128)(2,1)S(1)} %get-tuple-element.30), channel_id=1, source_target_pairs={{384,0},{385,1},{386,2},{387,3},{388,4},{389,5},{390,6},{391,7},{3... | collective-permute-start | bytes 417800 | tf_op jit(solution)/shard_map/ppermute | solution.py:302
  63.9 16.3 %collective-permute-start.2 = (bf16[272,256]{1,0:T(8,128)(2,1)S(1)}, bf16[272,256]{1,0:T(8,128)(2,1)S(1)}, u32[]{:S(2)}, u32[]{:S(2)}) collective-permute-start(bf16[272,256]{1,0:T(8,128)(2,1)S(1)} %get-tuple-element.30), channel_id=1, source_target_pairs={{256,0},{384,128},{257,1},{385,129},{258,2},{386,130},{259,3},{387... | collective-permute-start | bytes 417800 | tf_op jit(solution)/shard_map/ppermute | solution.py:302
  65.2 15.0 %collective-permute-start.1 = (bf16[272,256]{1,0:T(8,128)(2,1)S(1)}, bf16[272,256]{1,0:T(8,128)(2,1)S(1)}, u32[]{:S(2)}, u32[]{:S(2)}) collective-permute-start(bf16[272,256]{1,0:T(8,128)(2,1)S(1)} %get-tuple-element.30), channel_id=1, source_target_pairs={{128,0},{256,128},{384,256},{129,1},{257,129},{385,257},{130,2},{2... | collective-permute-start | bytes 417800 | tf_op jit(solution)/shard_map/ppermute | solution.py:302
  68.1 44.7 %all-to-all-start.2 = ((bf16[16,16,256]{2,1,0:T(8,128)(2,1)}), bf16[16,16,256]{2,1,0:T(8,128)(2,1)S(1)}, u32[]{:S(2)}, u32[]{:S(2)}) async-start(bf16[16,16,256]{2,1,0:T(8,128)(2,1)} %get-tuple-element.28), calls=%async_computation.2 | async-start | bytes 262144 | tf_op jit(solution)/shard_map/all_to_all | solution.py:272
  112.8 25.6 %all-to-all-start.3 = ((bf16[16,48,128]{2,1,0:T(8,128)(2,1)}), bf16[16,48,128]{2,1,0:T(8,128)(2,1)S(1)}, u32[]{:S(2)}, u32[]{:S(2)}) async-start(bf16[16,48,128]{2,1,0:T(8,128)(2,1)} %shard_map.117), calls=%async_computation.3 | async-start | bytes 393216 | tf_op jit(solution)/shard_map/all_to_all | solution.py:272

commit v6 on v5

--- a/solution.py
+++ b/solution.py
@@ -221,30 +221,49 @@
                 + nn(in_t, grad_ref[span, :])
                 - nn2(wt_ref[:, span], value_grad)
             )
-    total_ref[...] = jnp.broadcast_to(total, (8, 128))
-
-
-def join_kernel(key_ref, query_ref, out_ref):
-    out_ref[:, :16, :] = key_ref[...]
-    out_ref[:, 16:, :] = query_ref[...]
-
-
-def send_kernel(gk_ref, total_ref, out_ref):
-    total = total_ref[:1, :]
+    total_ref[...] = jnp.broadcast_to(total[None], (32, 1, 128))
+
+
+def join_kernel(key_ref, query_ref, out_ref, done):
+    copies = [
+        pltpu.make_async_copy(ref, out_ref.at[:, pl.ds(16 * i, 16), :], done.at[i])
+        for i, ref in enumerate((key_ref, query_ref))
+    ]
+    for copy in copies:
+        copy.start()
+    for copy in copies:
+        copy.wait()
+
+
+def join(keys, queries):
+    spec = pl.BlockSpec(memory_space=pl.ANY)
+    return pl.pallas_call(
+        join_kernel,
+        out_shape=shape((16, 32, 2 * N)),
+        in_specs=[spec, spec],
+        out_specs=spec,
+        scratch_shapes=[pltpu.SemaphoreType.DMA((2,))],
+    )(keys, queries)
+
+
+def send_kernel(gq_ref, gk_ref, parts_ref, out_ref):
+    total = jnp.sum(parts_ref[...], axis=0)
     high = total.astype(BF16).astype(F32)
     middle = (total - high).astype(BF16).astype(F32)
     low = total - high - middle
     rows = lax.broadcasted_iota(jnp.int32, (16, N), 0)
     pieces = jnp.where(rows == 0, high, jnp.where(rows == 1, middle, jnp.where(rows == 2, low, 0.0)))
-    out_ref[:, :16, :] = gk_ref[:, :, :N]
-    out_ref[:, 16:32, :] = gk_ref[:, :, N:]
-    out_ref[:, 32:, :] = jnp.broadcast_to(pieces.astype(BF16)[None], (16, 16, N))
-
-
-def receive_kernel(back_ref, gk_ref, square_ref):
-    gk_ref[:, :, :N] = back_ref[:, :16, :]
-    gk_ref[:, :, N:] = back_ref[:, 16:32, :]
-    pieces = jnp.sum(back_ref[:, 32:, :].astype(F32), axis=0)
+    for at, ref in ((0, gq_ref), (32, gk_ref)):
+        out_ref[:, at : at + 16, :] = ref[:, :, :N]
+        out_ref[:, at + 16 : at + 32, :] = ref[:, :, N:]
+    out_ref[:, 64:, :] = jnp.broadcast_to(pieces.astype(BF16)[None], (16, 16, N))
+
+
+def receive_kernel(back_ref, gq_ref, gk_ref, square_ref):
+    for at, ref in ((0, gq_ref), (32, gk_ref)):
+        ref[:, :, :N] = back_ref[:, at : at + 16, :]
+        ref[:, :, N:] = back_ref[:, at + 16 : at + 32, :]
+    pieces = jnp.sum(back_ref[:, 64:, :].astype(F32), axis=0)
     total = jnp.sum(pieces, axis=0, keepdims=True)
     square_ref[...] = total[:, :1] * (1.0 / (8192 * 16 * (2 * K + V)))
 
@@ -275,8 +294,7 @@
 def local(query_rows, key_rows, value_rows, out_grad, log_gates, write_rate, group_inverse, states):
     keys = jnp.transpose(key_rows, (1, 2, 0))
     queries = jnp.transpose(query_rows, (1, 2, 0))
-    (joined,) = call(join_kernel, [shape((16, 32, 2 * N))], (keys, queries), 0)
-    kq = to_heads(joined)
+    kq = to_heads(join(keys, queries))
     grad = out_grad.reshape(2 * N, V)
     values = value_rows.reshape(2 * N, V)
     x, y, c = (lax.axis_index(name) for name in SEQ)
@@ -288,8 +306,8 @@
     device_map, written_t, local_grad = call(
         local_map_kernel, [shape((K + PAD, K + V)), shape((K, 2 * N)), square], basics, 10**8
     )
-    states, device_map = lax.optimization_barrier((states, device_map))
-    state_heads = to_heads(jnp.transpose(states, (1, 0, 2, 3)))
+    state_blocks, device_map = lax.optimization_barrier((jnp.transpose(states, (1, 0, 2, 3)), device_map))
+    state_heads = to_heads(state_blocks)
     chip_other = lax.ppermute(device_map, "c", [(0, 1), (1, 0)])
     (now,) = call(pair_kernel, [chip_map], (place, device_map, chip_other), HIDING, scalars=1)
     plane_half, end, end_b = call(
@@ -307,13 +325,12 @@
         (*basics, written_t, values, state_heads),
         2 * 10**8,
     )
-    grad_query = to_heads(gq)
     later, fresh = lax.optimization_barrier((later, fresh))
     last = jnp.concatenate([later[2][:K, HALF:], end_b], axis=1)
     halves = lax.all_gather(jnp.concatenate([later[0], later[1], last], axis=0), "c")
     gk, grad_value, total = call(
         final_kernel,
-        [shape((16, 16, 2 * N)), shape((2 * N, V)), shape((8, 128), F32)],
+        [shape((16, 16, 2 * N)), shape((2 * N, V)), shape((32, 1, 128), F32)],
         (
             place, halves, end, chip_other, *basics, written_t, local_grad, state_heads, fresh, score_term,
             query_sum,
@@ -321,11 +338,13 @@
         4 * 10**8,
         scalars=1,
     )
-    for axis in ("c", "y", "x"):
-        total = lax.optimization_barrier(lax.psum(total, axis))
-    (sent,) = call(send_kernel, [shape((16, 48, N))], (gk, total), 10**6)
-    grad_key, grad_square = call(
-        receive_kernel, [shape((16, 16, 2 * N)), shape((1, 1), F32)], (to_heads(sent),), 10**6
+    parts = lax.all_to_all(total, SEQ, 0, 0, tiled=True)
+    (sent,) = call(send_kernel, [shape((16, 80, N))], (gq, gk, parts), 10**6)
+    grad_query, grad_key, grad_square = call(
+        receive_kernel,
+        [shape((16, 16, 2 * N)), shape((16, 16, 2 * N)), shape((1, 1), F32)],
+        (to_heads(sent),),
+        10**6,
     )
     return (
         jnp.transpose(grad_query, (2, 0, 1)),

time: 140 us -> 133 us (0.950)
  the two profiles are of different devices: /device:TPU:32 before, /device:TPU:64 now
where the time goes in v6:
time: 133 us; the launch traced here: 132 us
  blocking collectives  63.5 us (48%)
  starting transfers between devices  26.7 us (20%)
  waiting for transfers between devices  22.8 us (17%)
  Pallas kernels  17.3 us (13%)
    all_to_all x1, blocking collectives, to_heads(): return lax.all_to_all(array, 'key', 0, 0, tiled=True)  32.6 us
    all_to_all x2, starting transfers between devices, to_heads(): return lax.all_to_all(array, 'key', 0, 0, tiled=True)  20.9 us
    all_to_all x2, waiting for transfers between devices, to_heads(): return lax.all_to_all(array, 'key', 0, 0, tiled=True)  17.4 us
    all_to_all x1, blocking collectives, local(): parts = lax.all_to_all(total, SEQ, 0, 0, tiled=True)  14.6 us
    all_gather x1, blocking collectives, local(): lax.all_gather(now, 'y')  14 us
    pallas_call x1, Pallas kernels, join(): pl.pallas_call(join_kernel, out_shape=shape((16, 32, 2 * N)), in_specs=[s...  9.06 us
    pallas_call x7, Pallas kernels, call(): pl.pallas_call(kernel, out_shape=outs, in_specs=[smem] * scalars + [spec]...  8.25 us
    ppermute x3, waiting for transfers between devices, local(): lax.ppermute(plane_half, 'x', [(s, s - d) for s in range(d, 4)])  5.42 us
  transfers between devices with their start and end apart: 6, of which 2 were waited for; matrix products, arithmetic and copies ran while one was open for 1% of the time, Pallas kernels for 2%

profile of v6, /device:TPU:64, one launch (start us, length us, event | category | flops | bytes accessed | tf_op | source)
XLA Modules:
  0.0 132.0 jit_solution(15137685884155426968)
XLA Ops:
  0.6 9.1 %shard_map.111 = bf16[16,32,256]{2,1,0:T(8,128)(2,1)} custom-call(bf16[16,16,256]{2,1,0:T(8,128)(2,1)} %bitcast.22, bf16[16,16,256]{2,1,0:T(8,128)(2,1)} %bitcast.23), custom_call_target="tpu_custom_call" | custom-call | tf_op jit(solution)/shard_map/pallas_call | solution.py:240
  9.7 0.0 copy-start.5
  9.7 14.9 %all-to-all-start = ((bf16[16,32,256]{2,1,0:T(8,128)(2,1)}), bf16[16,32,256]{2,1,0:T(8,128)(2,1)S(1)}, u32[]{:S(2)}, u32[]{:S(2)}) async-start(bf16[16,32,256]{2,1,0:T(8,128)(2,1)} %shard_map.111), calls=%async_computation | async-start | bytes 524288 | tf_op jit(solution)/shard_map/all_to_all | solution.py:291
  24.6 0.0 copy-start
  24.7 0.7 copy.14
  25.4 17.4 %all-to-all-done.kq_ref = bf16[16,32,256]{2,1,0:T(8,128)(2,1)S(1)} async-done(((bf16[16,32,256]{2,1,0:T(8,128)(2,1)}), bf16[16,32,256]{2,1,0:T(8,128)(2,1)S(1)}, u32[]{:S(2)}, u32[]{:S(2)}) %all-to-all-start) | async-done | bytes 262176 | tf_op jit(solution)/shard_map/all_to_all | solution.py:291
  42.8 1.3 shard_map.112
  44.1 1.9 %collective-permute-start = (bf16[272,512]{1,0:T(8,128)(2,1)S(1)}, bf16[272,512]{1,0:T(8,128)(2,1)S(1)}, u32[]{:S(2)}, u32[]{:S(2)}) collective-permute-start(bf16[272,512]{1,0:T(8,128)(2,1)S(1)} %get-tuple-element.30.own_ref), channel_id=1, source_target_pairs={{0,16},{16,0},{1,17},{17,1},{2,18},{18,2},{3,19},{19,3},{4,20},{20... | collective-permute-start | bytes 835592 | tf_op jit(solution)/shard_map/ppermute | solution.py:311
  46.0 0.1 pad_add_fusion.place_ref
  46.1 6.0 %all-to-all-start.1 = ((bf16[16,2,16,256]{3,2,1,0:T(8,128)(2,1)}), bf16[16,2,16,256]{3,2,1,0:T(8,128)(2,1)S(1)}, u32[]{:S(2)}, u32[]{:S(2)}) async-start(bf16[16,2,16,256]{3,2,1,0:T(8,128)(2,1)} %bitcast.15), calls=%async_computation.1 | async-start | bytes 524288 | tf_op jit(solution)/shard_map/all_to_all | solution.py:291
  52.1 0.8 shard_map.114
  52.9 14.0 %all-gather = bf16[1088,384]{1,0:T(8,128)(2,1)S(1)} all-gather(bf16[272,384]{1,0:T(8,128)(2,1)S(1)} %shard_map.114), channel_id=2, replica_groups=mesh['x'=4,'y'=4,'c'=2,'key'=16] {'y'}, dimensions={0}, use_global_device_ids=true | all-gather | bytes 1044480 | tf_op jit(solution)/shard_map/all_gather | solution.py:316
  67.0 1.2 shard_map.115
  68.1 1.3 collective-permute-start.3
  69.4 1.3 collective-permute-start.2
  70.7 1.3 collective-permute-start.1
  72.1 1.1 shard_map.113
  73.2 5.4 %collective-permute-done.3 = bf16[272,256]{1,0:T(8,128)(2,1)S(1)} collective-permute-done((bf16[272,256]{1,0:T(8,128)(2,1)S(1)}, bf16[272,256]{1,0:T(8,128)(2,1)S(1)}, u32[]{:S(2)}, u32[]{:S(2)}) %collective-permute-start.3) | collective-permute-done | bytes 139296 | tf_op jit(solution)/shard_map/ppermute | solution.py:320
  78.6 2.4 %all-gather.1 = bf16[1600,256]{1,0:T(8,128)(2,1)S(1)} all-gather(bf16[800,256]{1,0:T(8,128)(2,1)S(1)} %maximum_maximum_fusion), channel_id=3, replica_groups=mesh['x'=4,'y'=4,'c'=2,'key'=16] {'c'}, dimensions={0}, use_global_device_ids=true | all-gather | bytes 1228800 | tf_op jit(solution)/shard_map/all_gather | solution.py:330
  81.0 3.0 %shard_map.116 = (bf16[16,16,256]{2,1,0:T(8,128)(2,1)S(1)}, bf16[256,256]{1,0:T(8,128)(2,1)}, f32[32,1,128]{2,1,0:T(1,128)S(1)}) custom-call(s32[3]{0:T(128)S(1)} %pad_add_fusion.place_ref, bf16[2,800,256]{2,1,0:T(8,128)(2,1)S(1)} %bitcast.17, f32[264,256]{1,0:T(8,128)S(1)} %get-tuple-element.37.end_ref, ...), custom_call_target="tpu_custom_call" | custom-call | flops 400000000 | bytes 2881548 | tf_op jit(solution)/shard_map/pallas_call | solution.py:275
  84.1 14.6 %all_to_all.20.parts_ref = f32[32,1,128]{2,1,0:T(1,128)S(1)} all-to-all(f32[32,1,128]{2,1,0:T(1,128)S(1)} %get-tuple-element.43), channel_id=1, replica_groups=mesh['x'=4,'y'=4,'c'=2,'key'=16] {'x','y','c'}, dimensions={0} | all-to-all | bytes 32768 | tf_op jit(solution)/shard_map/all_to_all | solution.py:341
  98.6 0.1 shard_map.117
  98.7 32.6 %all_to_all.21.back_ref = bf16[16,80,128]{2,1,0:T(8,128)(2,1)S(1)} all-to-all(bf16[16,80,128]{2,1,0:T(8,128)(2,1)S(1)} %shard_map.117), channel_id=1, replica_groups=mesh['x'=4,'y'=4,'c'=2,'key'=16] {'key'}, dimensions={0} | all-to-all | bytes 655360 | tf_op jit(solution)/shard_map/all_to_all | solution.py:291
  131.3 0.7 shard_map.118
  (16 shorter events, 0.1 us)
Async XLA Ops:
  9.7 14.9 %copy-start.5 = (bf16[2,16,16,256]{3,2,1,0:T(8,128)(2,1)S(1)}, bf16[2,16,16,256]{3,2,1,0:T(8,128)(2,1)}, u32[]{:S(2)}) copy-start(bf16[2,16,16,256]{3,2,1,0:T(8,128)(2,1)} %param.15) | copy-start | bytes 786436
  9.7 33.1 %all-to-all-start = ((bf16[16,32,256]{2,1,0:T(8,128)(2,1)}), bf16[16,32,256]{2,1,0:T(8,128)(2,1)S(1)}, u32[]{:S(2)}, u32[]{:S(2)}) async-start(bf16[16,32,256]{2,1,0:T(8,128)(2,1)} %shard_map.111), calls=%async_computation | async-start | bytes 524288 | tf_op jit(solution)/shard_map/all_to_all | solution.py:291
  24.6 18.2 %copy-start = (bf16[256,1,256]{2,0,1:T(8,128)(2,1)S(1)}, bf16[256,1,256]{2,0,1:T(8,128)(2,1)}, u32[]{:S(2)}) copy-start(bf16[256,1,256]{2,0,1:T(8,128)(2,1)} %param.11) | copy-start | bytes 393220
  24.6 18.1 %copy-start.1 = (bf16[2,1,128,128]{3,2,1,0:T(8,128)(2,1)S(1)}, bf16[2,1,128,128]{3,2,1,0:T(8,128)(2,1)}, u32[]{:S(2)}) copy-start(bf16[2,1,128,128]{3,2,1,0:T(8,128)(2,1)} %inv_ref.5) | copy-start | bytes 196612
  24.6 18.1 %copy-start.4 = (f32[1,256]{1,0:T(1,128)S(1)}, f32[1,256]{1,0:T(1,128)}, u32[]{:S(2)}) copy-start(f32[1,256]{1,0:T(1,128)} %rate_ref.5) | copy-start | bytes 3076
  25.4 17.4 %copy-start.3 = (f32[1,256]{1,0:T(1,128)S(1)}, f32[1,256]{1,0:T(1,128)}, u32[]{:S(2)}) copy-start(f32[1,256]{1,0:T(1,128)} %gate_ref.5) | copy-start | bytes 3076
  44.1 8.0 %collective-permute-start = (bf16[272,512]{1,0:T(8,128)(2,1)S(1)}, bf16[272,512]{1,0:T(8,128)(2,1)S(1)}, u32[]{:S(2)}, u32[]{:S(2)}) collective-permute-start(bf16[272,512]{1,0:T(8,128)(2,1)S(1)} %get-tuple-element.30.own_ref), channel_id=1, source_target_pairs={{0,16},{16,0},{1,17},{17,1},{2,18},{18,2},{3,19},{19,3},{4,20},{20... | collective-permute-start | bytes 835592 | tf_op jit(solution)/shard_map/ppermute | solution.py:311
  46.1 25.9 %all-to-all-start.1 = ((bf16[16,2,16,256]{3,2,1,0:T(8,128)(2,1)}), bf16[16,2,16,256]{3,2,1,0:T(8,128)(2,1)S(1)}, u32[]{:S(2)}, u32[]{:S(2)}) async-start(bf16[16,2,16,256]{3,2,1,0:T(8,128)(2,1)} %bitcast.15), calls=%async_computation.1 | async-start | bytes 524288 | tf_op jit(solution)/shard_map/all_to_all | solution.py:291
  67.0 5.1 %copy-start.2 = (bf16[256,1,256]{2,0,1:T(8,128)(2,1)S(1)}, bf16[256,1,256]{2,0,1:T(8,128)(2,1)}, u32[]{:S(2)}) copy-start(bf16[256,1,256]{2,0,1:T(8,128)(2,1)} %param.10) | copy-start | bytes 393220
  68.1 10.4 %collective-permute-start.3 = (bf16[272,256]{1,0:T(8,128)(2,1)S(1)}, bf16[272,256]{1,0:T(8,128)(2,1)S(1)}, u32[]{:S(2)}, u32[]{:S(2)}) collective-permute-start(bf16[272,256]{1,0:T(8,128)(2,1)S(1)} %get-tuple-element.31), channel_id=1, source_target_pairs={{384,0},{385,1},{386,2},{387,3},{388,4},{389,5},{390,6},{391,7},{3... | collective-permute-start | bytes 417800 | tf_op jit(solution)/shard_map/ppermute | solution.py:320
  69.4 9.1 %collective-permute-start.2 = (bf16[272,256]{1,0:T(8,128)(2,1)S(1)}, bf16[272,256]{1,0:T(8,128)(2,1)S(1)}, u32[]{:S(2)}, u32[]{:S(2)}) collective-permute-start(bf16[272,256]{1,0:T(8,128)(2,1)S(1)} %get-tuple-element.31), channel_id=1, source_target_pairs={{256,0},{384,128},{257,1},{385,129},{258,2},{386,130},{259,3},{387... | collective-permute-start | bytes 417800 | tf_op jit(solution)/shard_map/ppermute | solution.py:320
  70.7 7.8 %collective-permute-start.1 = (bf16[272,256]{1,0:T(8,128)(2,1)S(1)}, bf16[272,256]{1,0:T(8,128)(2,1)S(1)}, u32[]{:S(2)}, u32[]{:S(2)}) collective-permute-start(bf16[272,256]{1,0:T(8,128)(2,1)S(1)} %get-tuple-element.31), channel_id=1, source_target_pairs={{128,0},{256,128},{384,256},{129,1},{257,129},{385,257},{130,2},{2... | collective-permute-start | bytes 417800 | tf_op jit(solution)/shard_map/ppermute | solution.py:320

commit v7 on v6

--- a/solution.py
+++ b/solution.py
@@ -190,7 +190,7 @@
 
 
 def final_kernel(place_ref, halves_ref, end_ref, other_ref, kq_ref, grad_ref, gate_ref, rate_ref, inv_ref, wt_ref,
-                 lg_ref, state_ref, nv_ref, ct_ref, sum_ref, gk_ref, gv_ref, total_ref):
+                 lg_ref, state_ref, nv_ref, ct_ref, sum_ref, gq_ref, out_ref, gv_ref):
     key_t = head_rows(kq_ref, 0)
     query_t = head_rows(kq_ref, 1)
     state_grad = state_after(place_ref, halves_ref, end_ref, other_ref)
@@ -210,7 +210,8 @@
         gv_ref[span, :] = gv
         write_t = (-nt(state_ref[:, g].reshape(K, V), rounded)).astype(BF16)
         gk = (ct_ref[:, span] + away * nt(high, nv_ref[span, :]) + (rate * into) * nn(write_t, inverse)).astype(BF16)
-        gk_ref[:, :, span] = gk.reshape(16, 16, N)
+        out_ref[:, 16 * g : 16 * g + 16, :] = gq_ref[:, :, span]
+        out_ref[:, 32 + 16 * g : 48 + 16 * g, :] = gk.reshape(16, 16, N)
         total += jnp.sum(jnp.square(gk.astype(F32)), keepdims=True) + jnp.sum(
             jnp.square(gv.astype(F32)), keepdims=True
         )
@@ -221,7 +222,12 @@
                 + nn(in_t, grad_ref[span, :])
                 - nn2(wt_ref[:, span], value_grad)
             )
-    total_ref[...] = jnp.broadcast_to(total[None], (32, 1, 128))
+    high = total.astype(BF16).astype(F32)
+    middle = (total - high).astype(BF16).astype(F32)
+    low = total - high - middle
+    rows = lax.broadcasted_iota(jnp.int32, (16, N), 0)
+    pieces = jnp.where(rows == 0, high, jnp.where(rows == 1, middle, jnp.where(rows == 2, low, 0.0)))
+    out_ref[:, 64:, :] = jnp.broadcast_to(pieces.astype(BF16)[None], (16, 16, N))
 
 
 def join_kernel(key_ref, query_ref, out_ref, done):
@@ -241,31 +247,21 @@
         join_kernel,
         out_shape=shape((16, 32, 2 * N)),
         in_specs=[spec, spec],
-        out_specs=spec,
+        out_specs=pl.BlockSpec(memory_space=pltpu.VMEM),
         scratch_shapes=[pltpu.SemaphoreType.DMA((2,))],
     )(keys, queries)
 
 
-def send_kernel(gq_ref, gk_ref, parts_ref, out_ref):
-    total = jnp.sum(parts_ref[...], axis=0)
-    high = total.astype(BF16).astype(F32)
-    middle = (total - high).astype(BF16).astype(F32)
-    low = total - high - middle
-    rows = lax.broadcasted_iota(jnp.int32, (16, N), 0)
-    pieces = jnp.where(rows == 0, high, jnp.where(rows == 1, middle, jnp.where(rows == 2, low, 0.0)))
-    for at, ref in ((0, gq_ref), (32, gk_ref)):
-        out_ref[:, at : at + 16, :] = ref[:, :, :N]
-        out_ref[:, at + 16 : at + 32, :] = ref[:, :, N:]
-    out_ref[:, 64:, :] = jnp.broadcast_to(pieces.astype(BF16)[None], (16, 16, N))
-
-
-def receive_kernel(back_ref, gq_ref, gk_ref, square_ref):
+def spread_kernel(back_ref, out_ref):
+    pieces = jnp.sum(back_ref[:, 64:, :].astype(F32), axis=0)
+    total = jnp.sum(pieces, axis=0, keepdims=True)
+    out_ref[...] = jnp.broadcast_to(total[None], (32, 1, 128))
+
+
+def receive_kernel(back_ref, gq_ref, gk_ref):
     for at, ref in ((0, gq_ref), (32, gk_ref)):
         ref[:, :, :N] = back_ref[:, at : at + 16, :]
         ref[:, :, N:] = back_ref[:, at + 16 : at + 32, :]
-    pieces = jnp.sum(back_ref[:, 64:, :].astype(F32), axis=0)
-    total = jnp.sum(pieces, axis=0, keepdims=True)
-    square_ref[...] = total[:, :1] * (1.0 / (8192 * 16 * (2 * K + V)))
 
 
 def call(kernel, outs, args, flops, scratch=(), scalars=0):
@@ -328,29 +324,26 @@
     later, fresh = lax.optimization_barrier((later, fresh))
     last = jnp.concatenate([later[2][:K, HALF:], end_b], axis=1)
     halves = lax.all_gather(jnp.concatenate([later[0], later[1], last], axis=0), "c")
-    gk, grad_value, total = call(
+    sent, grad_value = call(
         final_kernel,
-        [shape((16, 16, 2 * N)), shape((2 * N, V)), shape((32, 1, 128), F32)],
+        [shape((16, 80, N)), shape((2 * N, V))],
         (
             place, halves, end, chip_other, *basics, written_t, local_grad, state_heads, fresh, score_term,
-            query_sum,
+            query_sum, gq,
         ),
         4 * 10**8,
         scalars=1,
     )
-    parts = lax.all_to_all(total, SEQ, 0, 0, tiled=True)
-    (sent,) = call(send_kernel, [shape((16, 80, N))], (gq, gk, parts), 10**6)
-    grad_query, grad_key, grad_square = call(
-        receive_kernel,
-        [shape((16, 16, 2 * N)), shape((16, 16, 2 * N)), shape((1, 1), F32)],
-        (to_heads(sent),),
-        10**6,
-    )
+    back = to_heads(sent)
+    (spread,) = call(spread_kernel, [shape((32, 1, 128), F32)], (back,), 10**6)
+    parts = lax.all_to_all(spread, SEQ, 0, 0, tiled=True)
+    grad_square = jnp.sum(parts[:, 0, 0]) / (8192 * 16 * (2 * K + V))
+    grad_query, grad_key = call(receive_kernel, [shape((16, 16, 2 * N))] * 2, (back,), 10**6)
     return (
         jnp.transpose(grad_query, (2, 0, 1)),
         jnp.transpose(grad_key, (2, 0, 1)),
         grad_value.reshape(2 * N, 1, V),
-        grad_square.reshape(()),
+        grad_square,
     )
 
 

time: 133 us -> 130 us (0.977)
  the two profiles are of different devices: /device:TPU:64 before, /device:TPU:1 now
where the time goes in v7:
time: 130 us; the launch traced here: 129 us
  starting transfers between devices  47.4 us (36%)
  blocking collectives  44.8 us (34%)
  waiting for transfers between devices  22.2 us (17%)
  Pallas kernels  10.6 us (8%)
  between operations  2.6 us (2%)
    all_to_all x1, blocking collectives, to_heads(): return lax.all_to_all(array, 'key', 0, 0, tiled=True)  26.4 us
    all_to_all x2, starting transfers between devices, to_heads(): return lax.all_to_all(array, 'key', 0, 0, tiled=True)  21.4 us
    all_to_all x1, starting transfers between devices, local(): parts = lax.all_to_all(spread, SEQ, 0, 0, tiled=True)  14.1 us
    all_gather x1, blocking collectives, local(): lax.all_gather(now, 'y')  12.7 us
    all_to_all x2, waiting for transfers between devices, to_heads(): return lax.all_to_all(array, 'key', 0, 0, tiled=True)  12.4 us
    pallas_call x7, Pallas kernels, call(): pl.pallas_call(kernel, out_shape=outs, in_specs=[smem] * scalars + [spec]...  8.92 us
    ppermute x1, starting transfers between devices, local(): chip_other = lax.ppermute(device_map, 'c', [(0, 1), (1, 0)])  8.09 us
    all_to_all x1, waiting for transfers between devices, local(): parts = lax.all_to_all(spread, SEQ, 0, 0, tiled=True)  6.2 us
  transfers between devices with their start and end apart: 7, of which 4 were waited for; matrix products, arithmetic and copies ran while one was open for 1% of the time, Pallas kernels for 3%

profile of v7, /device:TPU:1, one launch (start us, length us, event | category | flops | bytes accessed | tf_op | source)
XLA Modules:
  0.0 129.1 jit_solution(16913209992086685712)
XLA Ops:
  0.6 1.7 %shard_map.111 = bf16[16,32,256]{2,1,0:T(8,128)(2,1)} custom-call(bf16[16,16,256]{2,1,0:T(8,128)(2,1)} %bitcast.21, bf16[16,16,256]{2,1,0:T(8,128)(2,1)} %bitcast.22), custom_call_target="tpu_custom_call" | custom-call | tf_op jit(solution)/shard_map/pallas_call | solution.py:246
  2.3 15.9 %all-to-all-start = ((bf16[16,32,256]{2,1,0:T(8,128)(2,1)}), bf16[16,32,256]{2,1,0:T(8,128)(2,1)S(1)}, u32[]{:S(2)}, u32[]{:S(2)}) async-start(bf16[16,32,256]{2,1,0:T(8,128)(2,1)} %shard_map.111), calls=%async_computation | async-start | bytes 524288 | tf_op jit(solution)/shard_map/all_to_all | solution.py:287
  18.3 0.7 copy.14
  19.0 12.4 %all-to-all-done.kq_ref = bf16[16,32,256]{2,1,0:T(8,128)(2,1)S(1)} async-done(((bf16[16,32,256]{2,1,0:T(8,128)(2,1)}), bf16[16,32,256]{2,1,0:T(8,128)(2,1)S(1)}, u32[]{:S(2)}, u32[]{:S(2)}) %all-to-all-start) | async-done | bytes 262176 | tf_op jit(solution)/shard_map/all_to_all | solution.py:287
  31.4 1.3 %shard_map.112 = (bf16[272,512]{1,0:T(8,128)(2,1)S(1)}, bf16[256,256]{1,0:T(8,128)(2,1)S(1)}, f32[256,256]{1,0:T(8,128)S(1)}) custom-call(bf16[16,32,256]{2,1,0:T(8,128)(2,1)S(1)} %all-to-all-done.kq_ref, bf16[256,256]{1,0:T(8,128)(2,1)S(1)} %bitcast.17, f32[1,256]{1,0:T(1,128)S(1)} %copy-done.3, f32[1,256]{1,0:T(1,128)S(1)} %copy-done.4, ...), custom_call_target="tpu_custom_call" | custom-call | flops 100000000 | bytes 460800 | tf_op jit(solution)/shard_map/pallas_call | solution.py:271
  32.7 8.1 %collective-permute-start = (bf16[272,512]{1,0:T(8,128)(2,1)S(1)}, bf16[272,512]{1,0:T(8,128)(2,1)S(1)}, u32[]{:S(2)}, u32[]{:S(2)}) collective-permute-start(bf16[272,512]{1,0:T(8,128)(2,1)S(1)} %get-tuple-element.25.own_ref), channel_id=1, source_target_pairs={{0,16},{16,0},{1,17},{17,1},{2,18},{18,2},{3,19},{19,3},{4,20},{20... | collective-permute-start | bytes 835592 | tf_op jit(solution)/shard_map/ppermute | solution.py:307
  40.9 5.5 %all-to-all-start.1 = ((bf16[16,2,16,256]{3,2,1,0:T(8,128)(2,1)}), bf16[16,2,16,256]{3,2,1,0:T(8,128)(2,1)S(1)}, u32[]{:S(2)}, u32[]{:S(2)}) async-start(bf16[16,2,16,256]{3,2,1,0:T(8,128)(2,1)} %bitcast.14), calls=%async_computation.1 | async-start | bytes 524288 | tf_op jit(solution)/shard_map/all_to_all | solution.py:287
  46.4 0.8 shard_map.113
  47.2 12.7 %all-gather = bf16[1088,384]{1,0:T(8,128)(2,1)S(1)} all-gather(bf16[272,384]{1,0:T(8,128)(2,1)S(1)} %shard_map.113), channel_id=2, replica_groups=mesh['x'=4,'y'=4,'c'=2,'key'=16] {'y'}, dimensions={0}, use_global_device_ids=true | all-gather | bytes 1044480 | tf_op jit(solution)/shard_map/all_gather | solution.py:312
  60.0 1.2 shard_map.114
  61.2 1.3 %collective-permute-start.3 = (bf16[272,256]{1,0:T(8,128)(2,1)S(1)}, bf16[272,256]{1,0:T(8,128)(2,1)S(1)}, u32[]{:S(2)}, u32[]{:S(2)}) collective-permute-start(bf16[272,256]{1,0:T(8,128)(2,1)S(1)} %get-tuple-element.26), channel_id=1, source_target_pairs={{384,0},{385,1},{386,2},{387,3},{388,4},{389,5},{390,6},{391,7},{3... | collective-permute-start | bytes 417800 | tf_op jit(solution)/shard_map/ppermute | solution.py:316
  62.5 1.3 %collective-permute-start.2 = (bf16[272,256]{1,0:T(8,128)(2,1)S(1)}, bf16[272,256]{1,0:T(8,128)(2,1)S(1)}, u32[]{:S(2)}, u32[]{:S(2)}) collective-permute-start(bf16[272,256]{1,0:T(8,128)(2,1)S(1)} %get-tuple-element.26), channel_id=1, source_target_pairs={{256,0},{384,128},{257,1},{385,129},{258,2},{386,130},{259,3},{387... | collective-permute-start | bytes 417800 | tf_op jit(solution)/shard_map/ppermute | solution.py:316
  63.8 1.3 %collective-permute-start.1 = (bf16[272,256]{1,0:T(8,128)(2,1)S(1)}, bf16[272,256]{1,0:T(8,128)(2,1)S(1)}, u32[]{:S(2)}, u32[]{:S(2)}) collective-permute-start(bf16[272,256]{1,0:T(8,128)(2,1)S(1)} %get-tuple-element.26), channel_id=1, source_target_pairs={{128,0},{256,128},{384,256},{129,1},{257,129},{385,257},{130,2},{2... | collective-permute-start | bytes 417800 | tf_op jit(solution)/shard_map/ppermute | solution.py:316
  65.1 1.1 shard_map.115
  66.2 2.0 %collective-permute-done.3 = bf16[272,256]{1,0:T(8,128)(2,1)S(1)} collective-permute-done((bf16[272,256]{1,0:T(8,128)(2,1)S(1)}, bf16[272,256]{1,0:T(8,128)(2,1)S(1)}, u32[]{:S(2)}, u32[]{:S(2)}) %collective-permute-start.3) | collective-permute-done | bytes 139296 | tf_op jit(solution)/shard_map/ppermute | solution.py:316
  68.2 1.7 %collective-permute-done.2 = bf16[272,256]{1,0:T(8,128)(2,1)S(1)} collective-permute-done((bf16[272,256]{1,0:T(8,128)(2,1)S(1)}, bf16[272,256]{1,0:T(8,128)(2,1)S(1)}, u32[]{:S(2)}, u32[]{:S(2)}) %collective-permute-start.2) | collective-permute-done | bytes 139296 | tf_op jit(solution)/shard_map/ppermute | solution.py:316
  69.9 5.6 %all-gather.1 = bf16[1600,256]{1,0:T(8,128)(2,1)S(1)} all-gather(bf16[800,256]{1,0:T(8,128)(2,1)S(1)} %maximum_maximum_fusion), channel_id=3, replica_groups=mesh['x'=4,'y'=4,'c'=2,'key'=16] {'c'}, dimensions={0}, use_global_device_ids=true | all-gather | bytes 1228800 | tf_op jit(solution)/shard_map/all_gather | solution.py:326
  75.5 3.1 %shard_map.116 = (bf16[16,80,128]{2,1,0:T(8,128)(2,1)S(1)}, bf16[256,256]{1,0:T(8,128)(2,1)}) custom-call(s32[3]{0:T(128)S(1)} %pad_add_fusion.place_ref, bf16[2,800,256]{2,1,0:T(8,128)(2,1)S(1)} %bitcast.16, f32[264,256]{1,0:T(8,128)S(1)} %get-tuple-element.34.end_ref, bf16[272,512]{1,0:T(8,128)(2,1)S(1)} %collective-permute-done.other_ref, ...), custom_call_target="tpu_custom_call" | custom-call | flops 400000000 | bytes 3012620 | tf_op jit(solution)/shard_map/pallas_call | solution.py:271
  78.7 26.4 %all_to_all.20.back_ref = bf16[16,80,128]{2,1,0:T(8,128)(2,1)S(1)} all-to-all(bf16[16,80,128]{2,1,0:T(8,128)(2,1)S(1)} %get-tuple-element.40), channel_id=1, replica_groups=mesh['x'=4,'y'=4,'c'=2,'key'=16] {'key'}, dimensions={0} | all-to-all | bytes 655360 | tf_op jit(solution)/shard_map/all_to_all | solution.py:287
  105.1 0.6 shard_map.118
  105.7 14.1 %all-to-all-start.3 = ((f32[32,1,128]{2,1,0:T(1,128)}), f32[32,1,128]{2,1,0:T(1,128)S(1)}, u32[]{:S(2)}, u32[]{:S(2)}) async-start(f32[32,1,128]{2,1,0:T(1,128)} %shard_map.118), calls=%async_computation.3 | async-start | bytes 32768 | tf_op jit(solution)/shard_map/all_to_all | solution.py:339
  119.8 0.7 shard_map.117
  120.5 6.2 %all-to-all-done.3 = f32[32,1,128]{2,1,0:T(1,128)S(1)} async-done(((f32[32,1,128]{2,1,0:T(1,128)}), f32[32,1,128]{2,1,0:T(1,128)S(1)}, u32[]{:S(2)}, u32[]{:S(2)}) %all-to-all-start.3) | async-done | bytes 16416 | tf_op jit(solution)/shard_map/all_to_all | solution.py:339
  126.7 0.6 slice_reduce_fusion
  (18 shorter events, 0.2 us)
Async XLA Ops:
  2.3 15.9 %copy-start.5 = (bf16[2,16,16,256]{3,2,1,0:T(8,128)(2,1)S(1)}, bf16[2,16,16,256]{3,2,1,0:T(8,128)(2,1)}, u32[]{:S(2)}) copy-start(bf16[2,16,16,256]{3,2,1,0:T(8,128)(2,1)} %param.15) | copy-start | bytes 786436
  2.3 29.0 %all-to-all-start = ((bf16[16,32,256]{2,1,0:T(8,128)(2,1)}), bf16[16,32,256]{2,1,0:T(8,128)(2,1)S(1)}, u32[]{:S(2)}, u32[]{:S(2)}) async-start(bf16[16,32,256]{2,1,0:T(8,128)(2,1)} %shard_map.111), calls=%async_computation | async-start | bytes 524288 | tf_op jit(solution)/shard_map/all_to_all | solution.py:287
  18.2 13.1 %copy-start = (bf16[256,1,256]{2,0,1:T(8,128)(2,1)S(1)}, bf16[256,1,256]{2,0,1:T(8,128)(2,1)}, u32[]{:S(2)}) copy-start(bf16[256,1,256]{2,0,1:T(8,128)(2,1)} %param.11) | copy-start | bytes 393220
  18.3 13.1 %copy-start.1 = (bf16[2,1,128,128]{3,2,1,0:T(8,128)(2,1)S(1)}, bf16[2,1,128,128]{3,2,1,0:T(8,128)(2,1)}, u32[]{:S(2)}) copy-start(bf16[2,1,128,128]{3,2,1,0:T(8,128)(2,1)} %inv_ref.5) | copy-start | bytes 196612
  18.3 13.1 %copy-start.4 = (f32[1,256]{1,0:T(1,128)S(1)}, f32[1,256]{1,0:T(1,128)}, u32[]{:S(2)}) copy-start(f32[1,256]{1,0:T(1,128)} %rate_ref.5) | copy-start | bytes 3076
  19.0 12.4 %copy-start.3 = (f32[1,256]{1,0:T(1,128)S(1)}, f32[1,256]{1,0:T(1,128)}, u32[]{:S(2)}) copy-start(f32[1,256]{1,0:T(1,128)} %gate_ref.5) | copy-start | bytes 3076
  32.7 13.7 %collective-permute-start = (bf16[272,512]{1,0:T(8,128)(2,1)S(1)}, bf16[272,512]{1,0:T(8,128)(2,1)S(1)}, u32[]{:S(2)}, u32[]{:S(2)}) collective-permute-start(bf16[272,512]{1,0:T(8,128)(2,1)S(1)} %get-tuple-element.25.own_ref), channel_id=1, source_target_pairs={{0,16},{16,0},{1,17},{17,1},{2,18},{18,2},{3,19},{19,3},{4,20},{20... | collective-permute-start | bytes 835592 | tf_op jit(solution)/shard_map/ppermute | solution.py:307
  40.9 24.2 %all-to-all-start.1 = ((bf16[16,2,16,256]{3,2,1,0:T(8,128)(2,1)}), bf16[16,2,16,256]{3,2,1,0:T(8,128)(2,1)S(1)}, u32[]{:S(2)}, u32[]{:S(2)}) async-start(bf16[16,2,16,256]{3,2,1,0:T(8,128)(2,1)} %bitcast.14), calls=%async_computation.1 | async-start | bytes 524288 | tf_op jit(solution)/shard_map/all_to_all | solution.py:287
  60.0 5.1 %copy-start.2 = (bf16[256,1,256]{2,0,1:T(8,128)(2,1)S(1)}, bf16[256,1,256]{2,0,1:T(8,128)(2,1)}, u32[]{:S(2)}) copy-start(bf16[256,1,256]{2,0,1:T(8,128)(2,1)} %param.10) | copy-start | bytes 393220
  61.2 7.0 %collective-permute-start.3 = (bf16[272,256]{1,0:T(8,128)(2,1)S(1)}, bf16[272,256]{1,0:T(8,128)(2,1)S(1)}, u32[]{:S(2)}, u32[]{:S(2)}) collective-permute-start(bf16[272,256]{1,0:T(8,128)(2,1)S(1)} %get-tuple-element.26), channel_id=1, source_target_pairs={{384,0},{385,1},{386,2},{387,3},{388,4},{389,5},{390,6},{391,7},{3... | collective-permute-start | bytes 417800 | tf_op jit(solution)/shard_map/ppermute | solution.py:316
  62.5 7.4 %collective-permute-start.2 = (bf16[272,256]{1,0:T(8,128)(2,1)S(1)}, bf16[272,256]{1,0:T(8,128)(2,1)S(1)}, u32[]{:S(2)}, u32[]{:S(2)}) collective-permute-start(bf16[272,256]{1,0:T(8,128)(2,1)S(1)} %get-tuple-element.26), channel_id=1, source_target_pairs={{256,0},{384,128},{257,1},{385,129},{258,2},{386,130},{259,3},{387... | collective-permute-start | bytes 417800 | tf_op jit(solution)/shard_map/ppermute | solution.py:316
  63.8 6.1 %collective-permute-start.1 = (bf16[272,256]{1,0:T(8,128)(2,1)S(1)}, bf16[272,256]{1,0:T(8,128)(2,1)S(1)}, u32[]{:S(2)}, u32[]{:S(2)}) collective-permute-start(bf16[272,256]{1,0:T(8,128)(2,1)S(1)} %get-tuple-element.26), channel_id=1, source_target_pairs={{128,0},{256,128},{384,256},{129,1},{257,129},{385,257},{130,2},{2... | collective-permute-start | bytes 417800 | tf_op jit(solution)/shard_map/ppermute | solution.py:316
  105.7 21.0 %all-to-all-start.3 = ((f32[32,1,128]{2,1,0:T(1,128)}), f32[32,1,128]{2,1,0:T(1,128)S(1)}, u32[]{:S(2)}, u32[]{:S(2)}) async-start(f32[32,1,128]{2,1,0:T(1,128)} %shard_map.118), calls=%async_computation.3 | async-start | bytes 32768 | tf_op jit(solution)/shard_map/all_to_all | solution.py:339

commit v8 on v6

--- a/solution.py
+++ b/solution.py
@@ -241,7 +241,7 @@
         join_kernel,
         out_shape=shape((16, 32, 2 * N)),
         in_specs=[spec, spec],
-        out_specs=spec,
+        out_specs=pl.BlockSpec(memory_space=pltpu.VMEM),
         scratch_shapes=[pltpu.SemaphoreType.DMA((2,))],
     )(keys, queries)
 

time: 133 us -> 125 us (0.940)
  Pallas kernels: 17.3 us -> 9.94 us
    pallas_call x1, Pallas kernels: 9.06 us -> 1.69 us  [join(): pl.pallas_call(join_kernel, out_shape=shape((16, 32, 2 * N)), in_specs=[s...]
where the time goes in v8:
time: 125 us
  blocking collectives  63.5 us (51%)
  starting transfers between devices  26.7 us (21%)
  waiting for transfers between devices  22.8 us (18%)
  Pallas kernels  9.94 us (8%)
    all_to_all x1, blocking collectives, to_heads(): return lax.all_to_all(array, 'key', 0, 0, tiled=True)  32.6 us
    all_to_all x2, starting transfers between devices, to_heads(): return lax.all_to_all(array, 'key', 0, 0, tiled=True)  20.9 us
    all_to_all x2, waiting for transfers between devices, to_heads(): return lax.all_to_all(array, 'key', 0, 0, tiled=True)  17.4 us
    all_to_all x1, blocking collectives, local(): parts = lax.all_to_all(total, SEQ, 0, 0, tiled=True)  14.6 us
    all_gather x1, blocking collectives, local(): lax.all_gather(now, 'y')  14 us
    pallas_call x7, Pallas kernels, call(): pl.pallas_call(kernel, out_shape=outs, in_specs=[smem] * scalars + [spec]...  8.25 us
    ppermute x3, waiting for transfers between devices, local(): lax.ppermute(plane_half, 'x', [(s, s - d) for s in range(d, 4)])  5.42 us
    ppermute x3, starting transfers between devices, local(): lax.ppermute(plane_half, 'x', [(s, s - d) for s in range(d, 4)])  3.88 us
  transfers between devices with their start and end apart: 6, of which 2 were waited for; matrix products, arithmetic and copies ran while one was open for 1% of the time, Pallas kernels for 2%

profile of v8, /device:TPU:64, one launch (start us, length us, event | category | flops | bytes accessed | tf_op | source)
XLA Modules:
  0.0 124.7 jit_solution(15311708450824598294)
XLA Ops:
  0.6 1.7 %shard_map.111 = bf16[16,32,256]{2,1,0:T(8,128)(2,1)} custom-call(bf16[16,16,256]{2,1,0:T(8,128)(2,1)} %bitcast.22, bf16[16,16,256]{2,1,0:T(8,128)(2,1)} %bitcast.23), custom_call_target="tpu_custom_call" | custom-call | tf_op jit(solution)/shard_map/pallas_call | solution.py:240
  2.3 0.0 copy-start.5
  2.3 14.9 %all-to-all-start = ((bf16[16,32,256]{2,1,0:T(8,128)(2,1)}), bf16[16,32,256]{2,1,0:T(8,128)(2,1)S(1)}, u32[]{:S(2)}, u32[]{:S(2)}) async-start(bf16[16,32,256]{2,1,0:T(8,128)(2,1)} %shard_map.111), calls=%async_computation | async-start | bytes 524288 | tf_op jit(solution)/shard_map/all_to_all | solution.py:291
  17.2 0.0 copy-start
  17.3 0.7 copy.14
  18.0 17.4 %all-to-all-done.kq_ref = bf16[16,32,256]{2,1,0:T(8,128)(2,1)S(1)} async-done(((bf16[16,32,256]{2,1,0:T(8,128)(2,1)}), bf16[16,32,256]{2,1,0:T(8,128)(2,1)S(1)}, u32[]{:S(2)}, u32[]{:S(2)}) %all-to-all-start) | async-done | bytes 262176 | tf_op jit(solution)/shard_map/all_to_all | solution.py:291
  35.4 1.3 %shard_map.112 = (bf16[272,512]{1,0:T(8,128)(2,1)S(1)}, bf16[256,256]{1,0:T(8,128)(2,1)S(1)}, f32[256,256]{1,0:T(8,128)S(1)}) custom-call(bf16[16,32,256]{2,1,0:T(8,128)(2,1)S(1)} %all-to-all-done.kq_ref, bf16[256,256]{1,0:T(8,128)(2,1)S(1)} %bitcast.18, f32[1,256]{1,0:T(1,128)S(1)} %copy-done.3, f32[1,256]{1,0:T(1,128)S(1)} %copy-done.4, ...), custom_call_target="tpu_custom_call" | custom-call | flops 100000000 | bytes 460800 | tf_op jit(solution)/shard_map/pallas_call | solution.py:275
  36.7 1.9 %collective-permute-start = (bf16[272,512]{1,0:T(8,128)(2,1)S(1)}, bf16[272,512]{1,0:T(8,128)(2,1)S(1)}, u32[]{:S(2)}, u32[]{:S(2)}) collective-permute-start(bf16[272,512]{1,0:T(8,128)(2,1)S(1)} %get-tuple-element.30.own_ref), channel_id=1, source_target_pairs={{0,16},{16,0},{1,17},{17,1},{2,18},{18,2},{3,19},{19,3},{4,20},{20... | collective-permute-start | bytes 835592 | tf_op jit(solution)/shard_map/ppermute | solution.py:311
  38.7 0.1 pad_add_fusion.place_ref
  38.8 6.0 %all-to-all-start.1 = ((bf16[16,2,16,256]{3,2,1,0:T(8,128)(2,1)}), bf16[16,2,16,256]{3,2,1,0:T(8,128)(2,1)S(1)}, u32[]{:S(2)}, u32[]{:S(2)}) async-start(bf16[16,2,16,256]{3,2,1,0:T(8,128)(2,1)} %bitcast.15), calls=%async_computation.1 | async-start | bytes 524288 | tf_op jit(solution)/shard_map/all_to_all | solution.py:291
  44.8 0.8 shard_map.114
  45.6 14.0 %all-gather = bf16[1088,384]{1,0:T(8,128)(2,1)S(1)} all-gather(bf16[272,384]{1,0:T(8,128)(2,1)S(1)} %shard_map.114), channel_id=2, replica_groups=mesh['x'=4,'y'=4,'c'=2,'key'=16] {'y'}, dimensions={0}, use_global_device_ids=true | all-gather | bytes 1044480 | tf_op jit(solution)/shard_map/all_gather | solution.py:316
  59.6 1.2 shard_map.115
  60.8 1.3 %collective-permute-start.3 = (bf16[272,256]{1,0:T(8,128)(2,1)S(1)}, bf16[272,256]{1,0:T(8,128)(2,1)S(1)}, u32[]{:S(2)}, u32[]{:S(2)}) collective-permute-start(bf16[272,256]{1,0:T(8,128)(2,1)S(1)} %get-tuple-element.31), channel_id=1, source_target_pairs={{384,0},{385,1},{386,2},{387,3},{388,4},{389,5},{390,6},{391,7},{3... | collective-permute-start | bytes 417800 | tf_op jit(solution)/shard_map/ppermute | solution.py:320
  62.1 1.3 %collective-permute-start.2 = (bf16[272,256]{1,0:T(8,128)(2,1)S(1)}, bf16[272,256]{1,0:T(8,128)(2,1)S(1)}, u32[]{:S(2)}, u32[]{:S(2)}) collective-permute-start(bf16[272,256]{1,0:T(8,128)(2,1)S(1)} %get-tuple-element.31), channel_id=1, source_target_pairs={{256,0},{384,128},{257,1},{385,129},{258,2},{386,130},{259,3},{387... | collective-permute-start | bytes 417800 | tf_op jit(solution)/shard_map/ppermute | solution.py:320
  63.4 1.3 %collective-permute-start.1 = (bf16[272,256]{1,0:T(8,128)(2,1)S(1)}, bf16[272,256]{1,0:T(8,128)(2,1)S(1)}, u32[]{:S(2)}, u32[]{:S(2)}) collective-permute-start(bf16[272,256]{1,0:T(8,128)(2,1)S(1)} %get-tuple-element.31), channel_id=1, source_target_pairs={{128,0},{256,128},{384,256},{129,1},{257,129},{385,257},{130,2},{2... | collective-permute-start | bytes 417800 | tf_op jit(solution)/shard_map/ppermute | solution.py:320
  64.7 1.1 shard_map.113
  65.8 5.4 %collective-permute-done.3 = bf16[272,256]{1,0:T(8,128)(2,1)S(1)} collective-permute-done((bf16[272,256]{1,0:T(8,128)(2,1)S(1)}, bf16[272,256]{1,0:T(8,128)(2,1)S(1)}, u32[]{:S(2)}, u32[]{:S(2)}) %collective-permute-start.3) | collective-permute-done | bytes 139296 | tf_op jit(solution)/shard_map/ppermute | solution.py:320
  71.3 2.4 %all-gather.1 = bf16[1600,256]{1,0:T(8,128)(2,1)S(1)} all-gather(bf16[800,256]{1,0:T(8,128)(2,1)S(1)} %maximum_maximum_fusion), channel_id=3, replica_groups=mesh['x'=4,'y'=4,'c'=2,'key'=16] {'c'}, dimensions={0}, use_global_device_ids=true | all-gather | bytes 1228800 | tf_op jit(solution)/shard_map/all_gather | solution.py:330
  73.7 3.0 %shard_map.116 = (bf16[16,16,256]{2,1,0:T(8,128)(2,1)S(1)}, bf16[256,256]{1,0:T(8,128)(2,1)}, f32[32,1,128]{2,1,0:T(1,128)S(1)}) custom-call(s32[3]{0:T(128)S(1)} %pad_add_fusion.place_ref, bf16[2,800,256]{2,1,0:T(8,128)(2,1)S(1)} %bitcast.17, f32[264,256]{1,0:T(8,128)S(1)} %get-tuple-element.37.end_ref, ...), custom_call_target="tpu_custom_call" | custom-call | flops 400000000 | bytes 2881548 | tf_op jit(solution)/shard_map/pallas_call | solution.py:275
  76.7 14.6 %all_to_all.20.parts_ref = f32[32,1,128]{2,1,0:T(1,128)S(1)} all-to-all(f32[32,1,128]{2,1,0:T(1,128)S(1)} %get-tuple-element.43), channel_id=1, replica_groups=mesh['x'=4,'y'=4,'c'=2,'key'=16] {'x','y','c'}, dimensions={0} | all-to-all | bytes 32768 | tf_op jit(solution)/shard_map/all_to_all | solution.py:341
  91.2 0.1 shard_map.117
  91.3 32.6 %all_to_all.21.back_ref = bf16[16,80,128]{2,1,0:T(8,128)(2,1)S(1)} all-to-all(bf16[16,80,128]{2,1,0:T(8,128)(2,1)S(1)} %shard_map.117), channel_id=1, replica_groups=mesh['x'=4,'y'=4,'c'=2,'key'=16] {'key'}, dimensions={0} | all-to-all | bytes 655360 | tf_op jit(solution)/shard_map/all_to_all | solution.py:291
  123.9 0.7 shard_map.118
  (16 shorter events, 0.1 us)
Async XLA Ops:
  2.3 14.9 %copy-start.5 = (bf16[2,16,16,256]{3,2,1,0:T(8,128)(2,1)S(1)}, bf16[2,16,16,256]{3,2,1,0:T(8,128)(2,1)}, u32[]{:S(2)}) copy-start(bf16[2,16,16,256]{3,2,1,0:T(8,128)(2,1)} %param.15) | copy-start | bytes 786436
  2.3 33.1 %all-to-all-start = ((bf16[16,32,256]{2,1,0:T(8,128)(2,1)}), bf16[16,32,256]{2,1,0:T(8,128)(2,1)S(1)}, u32[]{:S(2)}, u32[]{:S(2)}) async-start(bf16[16,32,256]{2,1,0:T(8,128)(2,1)} %shard_map.111), calls=%async_computation | async-start | bytes 524288 | tf_op jit(solution)/shard_map/all_to_all | solution.py:291
  17.2 18.2 %copy-start = (bf16[256,1,256]{2,0,1:T(8,128)(2,1)S(1)}, bf16[256,1,256]{2,0,1:T(8,128)(2,1)}, u32[]{:S(2)}) copy-start(bf16[256,1,256]{2,0,1:T(8,128)(2,1)} %param.11) | copy-start | bytes 393220
  17.3 18.1 %copy-start.1 = (bf16[2,1,128,128]{3,2,1,0:T(8,128)(2,1)S(1)}, bf16[2,1,128,128]{3,2,1,0:T(8,128)(2,1)}, u32[]{:S(2)}) copy-start(bf16[2,1,128,128]{3,2,1,0:T(8,128)(2,1)} %inv_ref.5) | copy-start | bytes 196612
  17.3 18.1 %copy-start.4 = (f32[1,256]{1,0:T(1,128)S(1)}, f32[1,256]{1,0:T(1,128)}, u32[]{:S(2)}) copy-start(f32[1,256]{1,0:T(1,128)} %rate_ref.5) | copy-start | bytes 3076
  18.0 17.4 %copy-start.3 = (f32[1,256]{1,0:T(1,128)S(1)}, f32[1,256]{1,0:T(1,128)}, u32[]{:S(2)}) copy-start(f32[1,256]{1,0:T(1,128)} %gate_ref.5) | copy-start | bytes 3076
  36.7 8.0 %collective-permute-start = (bf16[272,512]{1,0:T(8,128)(2,1)S(1)}, bf16[272,512]{1,0:T(8,128)(2,1)S(1)}, u32[]{:S(2)}, u32[]{:S(2)}) collective-permute-start(bf16[272,512]{1,0:T(8,128)(2,1)S(1)} %get-tuple-element.30.own_ref), channel_id=1, source_target_pairs={{0,16},{16,0},{1,17},{17,1},{2,18},{18,2},{3,19},{19,3},{4,20},{20... | collective-permute-start | bytes 835592 | tf_op jit(solution)/shard_map/ppermute | solution.py:311
  38.8 25.9 %all-to-all-start.1 = ((bf16[16,2,16,256]{3,2,1,0:T(8,128)(2,1)}), bf16[16,2,16,256]{3,2,1,0:T(8,128)(2,1)S(1)}, u32[]{:S(2)}, u32[]{:S(2)}) async-start(bf16[16,2,16,256]{3,2,1,0:T(8,128)(2,1)} %bitcast.15), calls=%async_computation.1 | async-start | bytes 524288 | tf_op jit(solution)/shard_map/all_to_all | solution.py:291
  59.6 5.1 %copy-start.2 = (bf16[256,1,256]{2,0,1:T(8,128)(2,1)S(1)}, bf16[256,1,256]{2,0,1:T(8,128)(2,1)}, u32[]{:S(2)}) copy-start(bf16[256,1,256]{2,0,1:T(8,128)(2,1)} %param.10) | copy-start | bytes 393220
  60.8 10.4 %collective-permute-start.3 = (bf16[272,256]{1,0:T(8,128)(2,1)S(1)}, bf16[272,256]{1,0:T(8,128)(2,1)S(1)}, u32[]{:S(2)}, u32[]{:S(2)}) collective-permute-start(bf16[272,256]{1,0:T(8,128)(2,1)S(1)} %get-tuple-element.31), channel_id=1, source_target_pairs={{384,0},{385,1},{386,2},{387,3},{388,4},{389,5},{390,6},{391,7},{3... | collective-permute-start | bytes 417800 | tf_op jit(solution)/shard_map/ppermute | solution.py:320
  62.1 9.1 %collective-permute-start.2 = (bf16[272,256]{1,0:T(8,128)(2,1)S(1)}, bf16[272,256]{1,0:T(8,128)(2,1)S(1)}, u32[]{:S(2)}, u32[]{:S(2)}) collective-permute-start(bf16[272,256]{1,0:T(8,128)(2,1)S(1)} %get-tuple-element.31), channel_id=1, source_target_pairs={{256,0},{384,128},{257,1},{385,129},{258,2},{386,130},{259,3},{387... | collective-permute-start | bytes 417800 | tf_op jit(solution)/shard_map/ppermute | solution.py:320
  63.4 7.8 %collective-permute-start.1 = (bf16[272,256]{1,0:T(8,128)(2,1)S(1)}, bf16[272,256]{1,0:T(8,128)(2,1)S(1)}, u32[]{:S(2)}, u32[]{:S(2)}) collective-permute-start(bf16[272,256]{1,0:T(8,128)(2,1)S(1)} %get-tuple-element.31), channel_id=1, source_target_pairs={{128,0},{256,128},{384,256},{129,1},{257,129},{385,257},{130,2},{2... | collective-permute-start | bytes 417800 | tf_op jit(solution)/shard_map/ppermute | solution.py:320

commit v9 on v6

--- a/solution.py
+++ b/solution.py
@@ -102,7 +102,7 @@
     return kq_ref[:, 16 * which : 16 * which + 16, :].reshape(K, 2 * N)
 
 
-def local_map_kernel(kq_ref, grad_ref, gate_ref, rate_ref, inv_ref, map_ref, wt_ref, lg_ref):
+def local_map_kernel(kq_ref, grad_ref, gate_ref, rate_ref, inv_ref, map_ref, wt_ref, lg_ref, later_m_ref, later_b_ref):
     key_t = head_rows(kq_ref, 0)
     query_t = head_rows(kq_ref, 1)
     maps = []
@@ -124,6 +124,8 @@
         offset = nn(in_t, grad) - nn2(wt, lg)
         maps.append((jnp.exp(gamma_end), nt(wt, out_t), offset))
     pack(map_ref, compose(*maps))
+    later_m_ref[...] = maps[1][1].astype(BF16)
+    later_b_ref[...] = maps[1][2]
 
 
 def pair_kernel(place_ref, own_ref, other_ref, map_ref):
@@ -137,7 +139,7 @@
     pack(map_ref, compose(choose(upper, other, own), choose(upper, own, other)))
 
 
-def plane_kernel(place_ref, chips_ref, send_ref, end_ref, end_b_ref):
+def plane_kernel(place_ref, chips_ref, send_ref, send_b_ref, end_ref, end_b_ref):
     suffix = unpack(chips_ref[3])
     end = (jnp.ones((1, 1), F32), jnp.zeros((K, K), F32), jnp.zeros((K, HALF), F32))
     for j in (2, 1, 0):
@@ -148,6 +150,7 @@
     send_ref[:K, :HALF] = m_half.astype(BF16)
     send_ref[:K, HALF:] = b.astype(BF16)
     send_ref[K:, :] = decay_rows(decay, 2 * HALF)
+    send_b_ref[...] = b.astype(BF16)
     decay, m, b = end
     end_ref[:K, :] = m
     end_ref[K:, :] = jnp.broadcast_to(decay, (8, K))
@@ -184,15 +187,15 @@
         low, high = (halves_ref[i, ROWS * d : ROWS * (d + 1), :] for i in range(2))
         m = jnp.concatenate([low[:K, :HALF], high[:K, :HALF]], axis=1)
         b = jnp.concatenate([low[:K, HALF:], high[:K, HALF:]], axis=1).astype(F32)
-        state = apply((decay_from(low[K:]), m, b), state)
+        ahead = apply((decay_from(low[K:]), m, b), state)
+        state = jnp.where(place_ref[2] == 1, state, ahead) if d == 1 else ahead
     state = apply((end_ref[K : K + 1, :1], end_ref[:K, :], end_b), state)
     return jnp.where(place_ref[0] == 0, apply(unpack(other_ref[...]), state), state)
 
 
-def final_kernel(place_ref, halves_ref, end_ref, other_ref, kq_ref, grad_ref, gate_ref, rate_ref, inv_ref, wt_ref,
-                 lg_ref, state_ref, nv_ref, ct_ref, sum_ref, gk_ref, gv_ref, total_ref):
+def final_kernel(place_ref, halves_ref, end_ref, other_ref, later_m_ref, later_b_ref, kq_ref, gate_ref, rate_ref,
+                 inv_ref, lg_ref, state_ref, nv_ref, ct_ref, sum_ref, gk_ref, gv_ref, total_ref):
     key_t = head_rows(kq_ref, 0)
-    query_t = head_rows(kq_ref, 1)
     state_grad = state_after(place_ref, halves_ref, end_ref, other_ref)
     total = sum_ref[:1, :1]
     for g in (1, 0):
@@ -215,23 +218,21 @@
             jnp.square(gv.astype(F32)), keepdims=True
         )
         if g == 1:
-            in_t = (query_t[:, span] * into).astype(BF16)
-            state_grad = (
-                jnp.exp(gamma_end) * state_grad
-                + nn(in_t, grad_ref[span, :])
-                - nn2(wt_ref[:, span], value_grad)
-            )
+            state_grad = apply((jnp.exp(gamma_end), later_m_ref[...], later_b_ref[...]), state_grad)
     total_ref[...] = jnp.broadcast_to(total[None], (32, 1, 128))
 
 
-def join_kernel(key_ref, query_ref, out_ref, done):
-    copies = [
-        pltpu.make_async_copy(ref, out_ref.at[:, pl.ds(16 * i, 16), :], done.at[i])
-        for i, ref in enumerate((key_ref, query_ref))
+def join_kernel(key_ref, query_ref, out_ref, held, done):
+    inward = [pltpu.make_async_copy(ref, held.at[i], done.at[i]) for i, ref in enumerate((key_ref, query_ref))]
+    outward = [
+        pltpu.make_async_copy(held.at[i], out_ref.at[:, pl.ds(16 * i, 16), :], done.at[2 + i]) for i in range(2)
     ]
-    for copy in copies:
+    for copy in inward:
         copy.start()
-    for copy in copies:
+    for first, second in zip(inward, outward):
+        first.wait()
+        second.start()
+    for copy in outward:
         copy.wait()
 
 
@@ -242,7 +243,7 @@
         out_shape=shape((16, 32, 2 * N)),
         in_specs=[spec, spec],
         out_specs=spec,
-        scratch_shapes=[pltpu.SemaphoreType.DMA((2,))],
+        scratch_shapes=[pltpu.VMEM((2, 16, 16, 2 * N), BF16), pltpu.SemaphoreType.DMA((4,))],
     )(keys, queries)
 
 
@@ -303,21 +304,25 @@
     square = shape((K, V), F32)
     basics = (kq, grad, log_gates, write_rate, group_inverse)
 
-    device_map, written_t, local_grad = call(
-        local_map_kernel, [shape((K + PAD, K + V)), shape((K, 2 * N)), square], basics, 10**8
+    device_map, written_t, local_grad, later_m, later_b = call(
+        local_map_kernel,
+        [shape((K + PAD, K + V)), shape((K, 2 * N)), square, shape((K, K)), square],
+        basics,
+        10**8,
     )
     state_blocks, device_map = lax.optimization_barrier((jnp.transpose(states, (1, 0, 2, 3)), device_map))
     state_heads = to_heads(state_blocks)
     chip_other = lax.ppermute(device_map, "c", [(0, 1), (1, 0)])
     (now,) = call(pair_kernel, [chip_map], (place, device_map, chip_other), HIDING, scalars=1)
-    plane_half, end, end_b = call(
+    plane_half, plane_b, end, end_b = call(
         plane_kernel,
-        [shape((ROWS, 2 * HALF)), shape((K + 8, K), F32), shape((K, HALF))],
+        [shape((ROWS, 2 * HALF)), shape((K, HALF)), shape((K + 8, K), F32), shape((K, HALF))],
         (place, lax.all_gather(now, "y")),
         10**8,
         scalars=1,
     )
-    later = [lax.ppermute(plane_half, "x", [(s, s - d) for s in range(d, 4)]) for d in (1, 2, 3)]
+    later = [lax.ppermute(plane_half, "x", pairs) for pairs in ([(1, 0), (2, 1), (3, 2)], [(2, 0)])]
+    later += [lax.ppermute(plane_b, "x", pairs) for pairs in ([(3, 1)], [(3, 0)])]
 
     gq, fresh, score_term, query_sum = call(
         ahead_kernel,
@@ -326,14 +331,14 @@
         2 * 10**8,
     )
     later, fresh = lax.optimization_barrier((later, fresh))
-    last = jnp.concatenate([later[2][:K, HALF:], end_b], axis=1)
+    last = jnp.concatenate([later[2] + later[3], end_b], axis=1)
     halves = lax.all_gather(jnp.concatenate([later[0], later[1], last], axis=0), "c")
     gk, grad_value, total = call(
         final_kernel,
         [shape((16, 16, 2 * N)), shape((2 * N, V)), shape((32, 1, 128), F32)],
         (
-            place, halves, end, chip_other, *basics, written_t, local_grad, state_heads, fresh, score_term,
-            query_sum,
+            place, halves, end, chip_other, later_m, later_b, kq, log_gates, write_rate, group_inverse, local_grad,
+            state_heads, fresh, score_term, query_sum,
         ),
         4 * 10**8,
         scalars=1,

time: 133 us -> 125 us (0.940)
  Pallas kernels: 17.3 us -> 9.67 us
    pallas_call x1, Pallas kernels: 9.06 us -> 1.67 us  [join(): pl.pallas_call(join_kernel, out_shape=shape((16, 32, 2 * N)), in_specs=[s...]
    ppermute x3 -> x4, starting transfers between devices: 3.88 us -> 4.54 us  [the longest x2 2.58 us: local(): lax.ppermute(plane_half, 'x', pairs)]
    ppermute x3 -> x4, waiting for transfers between devices: 5.42 us -> 5.77 us  [the longest x2 5.76 us: local(): lax.ppermute(plane_b, 'x', pairs)]
  transfers between devices with their start and end apart: 6 -> 7, of which waited for: 2 -> 2; matrix products, arithmetic and copies ran while one was open for 1% -> 1% of each run, Pallas kernels for 2% -> 2%
where the time goes in v9:
time: 125 us; the launch traced here: 124 us
  blocking collectives  62.4 us (50%)
  starting transfers between devices  27.4 us (22%)
  waiting for transfers between devices  23.2 us (19%)
  Pallas kernels  9.67 us (8%)
    all_to_all x1, blocking collectives, to_heads(): return lax.all_to_all(array, 'key', 0, 0, tiled=True)  32.6 us
    all_to_all x2, starting transfers between devices, to_heads(): return lax.all_to_all(array, 'key', 0, 0, tiled=True)  20.9 us
    all_to_all x2, waiting for transfers between devices, to_heads(): return lax.all_to_all(array, 'key', 0, 0, tiled=True)  17.4 us
    all_gather x1, blocking collectives, local(): lax.all_gather(now, 'y')  14 us
    all_to_all x1, blocking collectives, local(): parts = lax.all_to_all(total, SEQ, 0, 0, tiled=True)  13.5 us
    pallas_call x7, Pallas kernels, call(): pl.pallas_call(kernel, out_shape=outs, in_specs=[smem] * scalars + [spec]...  8 us
    ppermute x2, waiting for transfers between devices, local(): lax.ppermute(plane_b, 'x', pairs)  5.76 us
    ppermute x2, starting transfers between devices, local(): lax.ppermute(plane_half, 'x', pairs)  2.58 us
  transfers between devices with their start and end apart: 7, of which 2 were waited for; matrix products, arithmetic and copies ran while one was open for 1% of the time, Pallas kernels for 2%

profile of v9, /device:TPU:64, one launch (start us, length us, event | category | flops | bytes accessed | tf_op | source)
XLA Modules:
  0.0 124.3 jit_solution(4773372408750100776)
XLA Ops:
  0.6 1.7 %shard_map.111 = bf16[16,32,256]{2,1,0:T(8,128)(2,1)} custom-call(bf16[16,16,256]{2,1,0:T(8,128)(2,1)} %bitcast.21, bf16[16,16,256]{2,1,0:T(8,128)(2,1)} %bitcast.22), custom_call_target="tpu_custom_call" | custom-call | tf_op jit(solution)/shard_map/pallas_call | solution.py:241
  2.3 0.0 copy-start.5
  2.3 14.9 %all-to-all-start = ((bf16[16,32,256]{2,1,0:T(8,128)(2,1)}), bf16[16,32,256]{2,1,0:T(8,128)(2,1)S(1)}, u32[]{:S(2)}, u32[]{:S(2)}) async-start(bf16[16,32,256]{2,1,0:T(8,128)(2,1)} %shard_map.111), calls=%async_computation | async-start | bytes 524288 | tf_op jit(solution)/shard_map/all_to_all | solution.py:292
  17.3 0.7 copy.14
  18.0 17.4 %all-to-all-done.kq_ref = bf16[16,32,256]{2,1,0:T(8,128)(2,1)S(1)} async-done(((bf16[16,32,256]{2,1,0:T(8,128)(2,1)}), bf16[16,32,256]{2,1,0:T(8,128)(2,1)S(1)}, u32[]{:S(2)}, u32[]{:S(2)}) %all-to-all-start) | async-done | bytes 262176 | tf_op jit(solution)/shard_map/all_to_all | solution.py:292
  35.4 1.3 %shard_map.112 = (bf16[272,512]{1,0:T(8,128)(2,1)S(1)}, bf16[256,256]{1,0:T(8,128)(2,1)S(1)}, f32[256,256]{1,0:T(8,128)S(1)}, bf16[256,256]{1,0:T(8,128)(2,1)S(1)}, f32[256,256]{1,0:T(8,128)S(1)}) custom-call(bf16[16,32,256]{2,1,0:T(8,128)(2,1)S(1)} %all-to-all-done.kq_ref, bf16[256,256]{1,0:T(8,128)(2,1)S(1)} %bitcast.18, f32[1,256]{1,0:T(1,128)S(1)} %copy-done.3, ...), custom_call_target="tpu_custom_call" | custom-call | flops 100000000 | bytes 460800 | tf_op jit(solution)/shard_map/pallas_call | solution.py:276
  36.7 1.9 %collective-permute-start = (bf16[272,512]{1,0:T(8,128)(2,1)S(1)}, bf16[272,512]{1,0:T(8,128)(2,1)S(1)}, u32[]{:S(2)}, u32[]{:S(2)}) collective-permute-start(bf16[272,512]{1,0:T(8,128)(2,1)S(1)} %get-tuple-element.34.own_ref), channel_id=1, source_target_pairs={{0,16},{16,0},{1,17},{17,1},{2,18},{18,2},{3,19},{19,3},{4,20},{20... | collective-permute-start | bytes 835592 | tf_op jit(solution)/shard_map/ppermute | solution.py:315
  38.7 0.1 pad_add_fusion.place_ref
  38.7 6.0 %all-to-all-start.1 = ((bf16[16,2,16,256]{3,2,1,0:T(8,128)(2,1)}), bf16[16,2,16,256]{3,2,1,0:T(8,128)(2,1)S(1)}, u32[]{:S(2)}, u32[]{:S(2)}) async-start(bf16[16,2,16,256]{3,2,1,0:T(8,128)(2,1)} %bitcast.15), calls=%async_computation.1 | async-start | bytes 524288 | tf_op jit(solution)/shard_map/all_to_all | solution.py:292
  44.7 0.8 shard_map.114
  45.6 14.0 %all-gather = bf16[1088,384]{1,0:T(8,128)(2,1)S(1)} all-gather(bf16[272,384]{1,0:T(8,128)(2,1)S(1)} %shard_map.114), channel_id=2, replica_groups=mesh['x'=4,'y'=4,'c'=2,'key'=16] {'y'}, dimensions={0}, use_global_device_ids=true | all-gather | bytes 1044480 | tf_op jit(solution)/shard_map/all_gather | solution.py:320
  59.6 1.2 shard_map.115
  60.8 1.3 %collective-permute-start.2 = (bf16[272,256]{1,0:T(8,128)(2,1)S(1)}, bf16[272,256]{1,0:T(8,128)(2,1)S(1)}, u32[]{:S(2)}, u32[]{:S(2)}) collective-permute-start(bf16[272,256]{1,0:T(8,128)(2,1)S(1)} %get-tuple-element.35), channel_id=1, source_target_pairs={{256,0},{257,1},{258,2},{259,3},{260,4},{261,5},{262,6},{263,7},{2... | collective-permute-start | bytes 417800 | tf_op jit(solution)/shard_map/ppermute | solution.py:324
  62.1 1.3 %collective-permute-start.1 = (bf16[272,256]{1,0:T(8,128)(2,1)S(1)}, bf16[272,256]{1,0:T(8,128)(2,1)S(1)}, u32[]{:S(2)}, u32[]{:S(2)}) collective-permute-start(bf16[272,256]{1,0:T(8,128)(2,1)S(1)} %get-tuple-element.35), channel_id=1, source_target_pairs={{128,0},{256,128},{384,256},{129,1},{257,129},{385,257},{130,2},{2... | collective-permute-start | bytes 417800 | tf_op jit(solution)/shard_map/ppermute | solution.py:324
  63.4 1.3 %collective-permute-start.4 = (bf16[256,128]{1,0:T(8,128)(2,1)S(1)}, bf16[256,128]{1,0:T(8,128)(2,1)S(1)}, u32[]{:S(2)}, u32[]{:S(2)}) collective-permute-start(bf16[256,128]{1,0:T(8,128)(2,1)S(1)} %get-tuple-element.36), channel_id=1, source_target_pairs={{384,0},{385,1},{386,2},{387,3},{388,4},{389,5},{390,6},{391,7},{3... | collective-permute-start | bytes 196616 | tf_op jit(solution)/shard_map/ppermute | solution.py:325
  64.7 0.7 collective-permute-start.3
  65.3 1.1 shard_map.113
  66.5 5.8 %collective-permute-done.4 = bf16[256,128]{1,0:T(8,128)(2,1)S(1)} collective-permute-done((bf16[256,128]{1,0:T(8,128)(2,1)S(1)}, bf16[256,128]{1,0:T(8,128)(2,1)S(1)}, u32[]{:S(2)}, u32[]{:S(2)}) %collective-permute-start.4) | collective-permute-done | bytes 65568 | tf_op jit(solution)/shard_map/ppermute | solution.py:325
  72.3 2.4 %all-gather.1 = bf16[1600,256]{1,0:T(8,128)(2,1)S(1)} all-gather(bf16[800,256]{1,0:T(8,128)(2,1)S(1)} %maximum_maximum_fusion), channel_id=3, replica_groups=mesh['x'=4,'y'=4,'c'=2,'key'=16] {'c'}, dimensions={0}, use_global_device_ids=true | all-gather | bytes 1228800 | tf_op jit(solution)/shard_map/all_gather | solution.py:335
  74.7 2.8 %shard_map.116 = (bf16[16,16,256]{2,1,0:T(8,128)(2,1)S(1)}, bf16[256,256]{1,0:T(8,128)(2,1)}, f32[32,1,128]{2,1,0:T(1,128)S(1)}) custom-call(s32[3]{0:T(128)S(1)} %pad_add_fusion.place_ref, bf16[2,800,256]{2,1,0:T(8,128)(2,1)S(1)} %bitcast.17, f32[264,256]{1,0:T(8,128)S(1)} %get-tuple-element.43.end_ref, ...), custom_call_target="tpu_custom_call" | custom-call | flops 400000000 | bytes 3012620 | tf_op jit(solution)/shard_map/pallas_call | solution.py:276
  77.5 13.5 %all_to_all.20.parts_ref = f32[32,1,128]{2,1,0:T(1,128)S(1)} all-to-all(f32[32,1,128]{2,1,0:T(1,128)S(1)} %get-tuple-element.51), channel_id=1, replica_groups=mesh['x'=4,'y'=4,'c'=2,'key'=16] {'x','y','c'}, dimensions={0} | all-to-all | bytes 32768 | tf_op jit(solution)/shard_map/all_to_all | solution.py:346
  90.9 0.1 shard_map.117
  91.0 32.6 %all_to_all.21.back_ref = bf16[16,80,128]{2,1,0:T(8,128)(2,1)S(1)} all-to-all(bf16[16,80,128]{2,1,0:T(8,128)(2,1)S(1)} %shard_map.117), channel_id=1, replica_groups=mesh['x'=4,'y'=4,'c'=2,'key'=16] {'key'}, dimensions={0} | all-to-all | bytes 655360 | tf_op jit(solution)/shard_map/all_to_all | solution.py:292
  123.6 0.7 shard_map.118
  (18 shorter events, 0.1 us)
Async XLA Ops:
  2.3 14.9 %copy-start.5 = (bf16[2,16,16,256]{3,2,1,0:T(8,128)(2,1)S(1)}, bf16[2,16,16,256]{3,2,1,0:T(8,128)(2,1)}, u32[]{:S(2)}) copy-start(bf16[2,16,16,256]{3,2,1,0:T(8,128)(2,1)} %param.15) | copy-start | bytes 786436
  2.3 33.1 %all-to-all-start = ((bf16[16,32,256]{2,1,0:T(8,128)(2,1)}), bf16[16,32,256]{2,1,0:T(8,128)(2,1)S(1)}, u32[]{:S(2)}, u32[]{:S(2)}) async-start(bf16[16,32,256]{2,1,0:T(8,128)(2,1)} %shard_map.111), calls=%async_computation | async-start | bytes 524288 | tf_op jit(solution)/shard_map/all_to_all | solution.py:292
  17.2 18.2 %copy-start = (bf16[2,1,128,128]{3,2,1,0:T(8,128)(2,1)S(1)}, bf16[2,1,128,128]{3,2,1,0:T(8,128)(2,1)}, u32[]{:S(2)}) copy-start(bf16[2,1,128,128]{3,2,1,0:T(8,128)(2,1)} %inv_ref.5) | copy-start | bytes 196612
  17.2 18.1 %copy-start.1 = (bf16[256,1,256]{2,0,1:T(8,128)(2,1)S(1)}, bf16[256,1,256]{2,0,1:T(8,128)(2,1)}, u32[]{:S(2)}) copy-start(bf16[256,1,256]{2,0,1:T(8,128)(2,1)} %param.11) | copy-start | bytes 393220
  17.2 18.1 %copy-start.4 = (f32[1,256]{1,0:T(1,128)S(1)}, f32[1,256]{1,0:T(1,128)}, u32[]{:S(2)}) copy-start(f32[1,256]{1,0:T(1,128)} %rate_ref.5) | copy-start | bytes 3076
  18.0 17.4 %copy-start.3 = (f32[1,256]{1,0:T(1,128)S(1)}, f32[1,256]{1,0:T(1,128)}, u32[]{:S(2)}) copy-start(f32[1,256]{1,0:T(1,128)} %gate_ref.5) | copy-start | bytes 3076
  36.7 8.0 %collective-permute-start = (bf16[272,512]{1,0:T(8,128)(2,1)S(1)}, bf16[272,512]{1,0:T(8,128)(2,1)S(1)}, u32[]{:S(2)}, u32[]{:S(2)}) collective-permute-start(bf16[272,512]{1,0:T(8,128)(2,1)S(1)} %get-tuple-element.34.own_ref), channel_id=1, source_target_pairs={{0,16},{16,0},{1,17},{17,1},{2,18},{18,2},{3,19},{19,3},{4,20},{20... | collective-permute-start | bytes 835592 | tf_op jit(solution)/shard_map/ppermute | solution.py:315
  38.7 26.6 %all-to-all-start.1 = ((bf16[16,2,16,256]{3,2,1,0:T(8,128)(2,1)}), bf16[16,2,16,256]{3,2,1,0:T(8,128)(2,1)S(1)}, u32[]{:S(2)}, u32[]{:S(2)}) async-start(bf16[16,2,16,256]{3,2,1,0:T(8,128)(2,1)} %bitcast.15), calls=%async_computation.1 | async-start | bytes 524288 | tf_op jit(solution)/shard_map/all_to_all | solution.py:292
  59.6 5.8 %copy-start.2 = (bf16[256,1,256]{2,0,1:T(8,128)(2,1)S(1)}, bf16[256,1,256]{2,0,1:T(8,128)(2,1)}, u32[]{:S(2)}) copy-start(bf16[256,1,256]{2,0,1:T(8,128)(2,1)} %param.10) | copy-start | bytes 393220
  60.8 11.5 %collective-permute-start.2 = (bf16[272,256]{1,0:T(8,128)(2,1)S(1)}, bf16[272,256]{1,0:T(8,128)(2,1)S(1)}, u32[]{:S(2)}, u32[]{:S(2)}) collective-permute-start(bf16[272,256]{1,0:T(8,128)(2,1)S(1)} %get-tuple-element.35), channel_id=1, source_target_pairs={{256,0},{257,1},{258,2},{259,3},{260,4},{261,5},{262,6},{263,7},{2... | collective-permute-start | bytes 417800 | tf_op jit(solution)/shard_map/ppermute | solution.py:324
  62.1 10.2 %collective-permute-start.1 = (bf16[272,256]{1,0:T(8,128)(2,1)S(1)}, bf16[272,256]{1,0:T(8,128)(2,1)S(1)}, u32[]{:S(2)}, u32[]{:S(2)}) collective-permute-start(bf16[272,256]{1,0:T(8,128)(2,1)S(1)} %get-tuple-element.35), channel_id=1, source_target_pairs={{128,0},{256,128},{384,256},{129,1},{257,129},{385,257},{130,2},{2... | collective-permute-start | bytes 417800 | tf_op jit(solution)/shard_map/ppermute | solution.py:324
  63.4 8.9 %collective-permute-start.4 = (bf16[256,128]{1,0:T(8,128)(2,1)S(1)}, bf16[256,128]{1,0:T(8,128)(2,1)S(1)}, u32[]{:S(2)}, u32[]{:S(2)}) collective-permute-start(bf16[256,128]{1,0:T(8,128)(2,1)S(1)} %get-tuple-element.36), channel_id=1, source_target_pairs={{384,0},{385,1},{386,2},{387,3},{388,4},{389,5},{390,6},{391,7},{3... | collective-permute-start | bytes 196616 | tf_op jit(solution)/shard_map/ppermute | solution.py:325
  64.7 7.6 %collective-permute-start.3 = (bf16[256,128]{1,0:T(8,128)(2,1)S(1)}, bf16[256,128]{1,0:T(8,128)(2,1)S(1)}, u32[]{:S(2)}, u32[]{:S(2)}) collective-permute-start(bf16[256,128]{1,0:T(8,128)(2,1)S(1)} %get-tuple-element.36), channel_id=1, source_target_pairs={{384,128},{385,129},{386,130},{387,131},{388,132},{389,133},{390,1... | collective-permute-start | bytes 196616 | tf_op jit(solution)/shard_map/ppermute | solution.py:325

commit v10 on v9

--- a/solution.py
+++ b/solution.py
@@ -184,7 +184,7 @@
     state = jnp.concatenate([low[:, :HALF], high[:, :HALF]], axis=1)
     end_b = jnp.concatenate([low[:, HALF:], high[:, HALF:]], axis=1)
     for d in (1, 0):
-        low, high = (halves_ref[i, ROWS * d : ROWS * (d + 1), :] for i in range(2))
+        low, high = (halves_ref[i, ROWS * (1 - d) : ROWS * (2 - d), :] for i in range(2))
         m = jnp.concatenate([low[:K, :HALF], high[:K, :HALF]], axis=1)
         b = jnp.concatenate([low[:K, HALF:], high[:K, HALF:]], axis=1).astype(F32)
         ahead = apply((decay_from(low[K:]), m, b), state)
@@ -321,7 +321,8 @@
         10**8,
         scalars=1,
     )
-    later = [lax.ppermute(plane_half, "x", pairs) for pairs in ([(1, 0), (2, 1), (3, 2)], [(2, 0)])]
+    two_ahead = lax.ppermute(plane_half, "x", [(2, 0)])
+    later = [two_ahead, lax.ppermute(plane_half, "x", [(1, 0), (2, 1), (3, 2)])]
     later += [lax.ppermute(plane_b, "x", pairs) for pairs in ([(3, 1)], [(3, 0)])]
 
     gq, fresh, score_term, query_sum = call(

time: 125 us -> 124 us (level)
  no operation moved by 1% of the time
where the time goes in v10:
time: 124 us
  blocking collectives  62.8 us (51%)
  starting transfers between devices  27.4 us (22%)
  waiting for transfers between devices  22.2 us (18%)
  Pallas kernels  9.67 us (8%)
    all_to_all x1, blocking collectives, to_heads(): return lax.all_to_all(array, 'key', 0, 0, tiled=True)  32.6 us
    all_to_all x2, starting transfers between devices, to_heads(): return lax.all_to_all(array, 'key', 0, 0, tiled=True)  20.9 us
    all_to_all x2, waiting for transfers between devices, to_heads(): return lax.all_to_all(array, 'key', 0, 0, tiled=True)  17.4 us
    all_gather x1, blocking collectives, local(): lax.all_gather(now, 'y')  14 us
    all_to_all x1, blocking collectives, local(): parts = lax.all_to_all(total, SEQ, 0, 0, tiled=True)  13.8 us
    pallas_call x7, Pallas kernels, call(): pl.pallas_call(kernel, out_shape=outs, in_specs=[smem] * scalars + [spec]...  8 us
    ppermute x2, waiting for transfers between devices, local(): lax.ppermute(plane_b, 'x', pairs)  4.79 us
  transfers between devices with their start and end apart: 7, of which 2 were waited for; matrix products, arithmetic and copies ran while one was open for 1% of the time, Pallas kernels for 2%

profile of v10, /device:TPU:64, one launch (start us, length us, event | category | flops | bytes accessed | tf_op | source)
XLA Modules:
  0.0 123.7 jit_solution(8009085724526076238)
XLA Ops:
  0.6 1.7 %shard_map.111 = bf16[16,32,256]{2,1,0:T(8,128)(2,1)} custom-call(bf16[16,16,256]{2,1,0:T(8,128)(2,1)} %bitcast.21, bf16[16,16,256]{2,1,0:T(8,128)(2,1)} %bitcast.22), custom_call_target="tpu_custom_call" | custom-call | tf_op jit(solution)/shard_map/pallas_call | solution.py:241
  2.3 14.9 %all-to-all-start = ((bf16[16,32,256]{2,1,0:T(8,128)(2,1)}), bf16[16,32,256]{2,1,0:T(8,128)(2,1)S(1)}, u32[]{:S(2)}, u32[]{:S(2)}) async-start(bf16[16,32,256]{2,1,0:T(8,128)(2,1)} %shard_map.111), calls=%async_computation | async-start | bytes 524288 | tf_op jit(solution)/shard_map/all_to_all | solution.py:292
  17.2 0.0 copy-start.4
  17.3 0.7 copy.14
  18.0 17.4 %all-to-all-done.kq_ref = bf16[16,32,256]{2,1,0:T(8,128)(2,1)S(1)} async-done(((bf16[16,32,256]{2,1,0:T(8,128)(2,1)}), bf16[16,32,256]{2,1,0:T(8,128)(2,1)S(1)}, u32[]{:S(2)}, u32[]{:S(2)}) %all-to-all-start) | async-done | bytes 262176 | tf_op jit(solution)/shard_map/all_to_all | solution.py:292
  35.4 1.3 %shard_map.112 = (bf16[272,512]{1,0:T(8,128)(2,1)S(1)}, bf16[256,256]{1,0:T(8,128)(2,1)S(1)}, f32[256,256]{1,0:T(8,128)S(1)}, bf16[256,256]{1,0:T(8,128)(2,1)S(1)}, f32[256,256]{1,0:T(8,128)S(1)}) custom-call(bf16[16,32,256]{2,1,0:T(8,128)(2,1)S(1)} %all-to-all-done.kq_ref, bf16[256,256]{1,0:T(8,128)(2,1)S(1)} %bitcast.18, f32[1,256]{1,0:T(1,128)S(1)} %copy-done.3, ...), custom_call_target="tpu_custom_call" | custom-call | flops 100000000 | bytes 460800 | tf_op jit(solution)/shard_map/pallas_call | solution.py:276
  36.7 1.9 %collective-permute-start = (bf16[272,512]{1,0:T(8,128)(2,1)S(1)}, bf16[272,512]{1,0:T(8,128)(2,1)S(1)}, u32[]{:S(2)}, u32[]{:S(2)}) collective-permute-start(bf16[272,512]{1,0:T(8,128)(2,1)S(1)} %get-tuple-element.34.own_ref), channel_id=1, source_target_pairs={{0,16},{16,0},{1,17},{17,1},{2,18},{18,2},{3,19},{19,3},{4,20},{20... | collective-permute-start | bytes 835592 | tf_op jit(solution)/shard_map/ppermute | solution.py:315
  38.7 0.1 pad_add_fusion.place_ref
  38.7 6.0 %all-to-all-start.1 = ((bf16[16,2,16,256]{3,2,1,0:T(8,128)(2,1)}), bf16[16,2,16,256]{3,2,1,0:T(8,128)(2,1)S(1)}, u32[]{:S(2)}, u32[]{:S(2)}) async-start(bf16[16,2,16,256]{3,2,1,0:T(8,128)(2,1)} %bitcast.15), calls=%async_computation.1 | async-start | bytes 524288 | tf_op jit(solution)/shard_map/all_to_all | solution.py:292
  44.7 0.8 shard_map.114
  45.6 14.0 %all-gather = bf16[1088,384]{1,0:T(8,128)(2,1)S(1)} all-gather(bf16[272,384]{1,0:T(8,128)(2,1)S(1)} %shard_map.114), channel_id=2, replica_groups=mesh['x'=4,'y'=4,'c'=2,'key'=16] {'y'}, dimensions={0}, use_global_device_ids=true | all-gather | bytes 1044480 | tf_op jit(solution)/shard_map/all_gather | solution.py:320
  59.6 1.2 shard_map.115
  60.8 1.3 %collective-permute-start.2 = (bf16[272,256]{1,0:T(8,128)(2,1)S(1)}, bf16[272,256]{1,0:T(8,128)(2,1)S(1)}, u32[]{:S(2)}, u32[]{:S(2)}) collective-permute-start(bf16[272,256]{1,0:T(8,128)(2,1)S(1)} %get-tuple-element.35), channel_id=1, source_target_pairs={{128,0},{256,128},{384,256},{129,1},{257,129},{385,257},{130,2},{2... | collective-permute-start | bytes 417800 | tf_op jit(solution)/shard_map/ppermute | solution.py:325
  62.1 1.3 %collective-permute-start.1 = (bf16[272,256]{1,0:T(8,128)(2,1)S(1)}, bf16[272,256]{1,0:T(8,128)(2,1)S(1)}, u32[]{:S(2)}, u32[]{:S(2)}) collective-permute-start(bf16[272,256]{1,0:T(8,128)(2,1)S(1)} %get-tuple-element.35), channel_id=1, source_target_pairs={{256,0},{257,1},{258,2},{259,3},{260,4},{261,5},{262,6},{263,7},{2... | collective-permute-start | bytes 417800 | tf_op jit(solution)/shard_map/ppermute | solution.py:324
  63.4 1.3 %collective-permute-start.4 = (bf16[256,128]{1,0:T(8,128)(2,1)S(1)}, bf16[256,128]{1,0:T(8,128)(2,1)S(1)}, u32[]{:S(2)}, u32[]{:S(2)}) collective-permute-start(bf16[256,128]{1,0:T(8,128)(2,1)S(1)} %get-tuple-element.36), channel_id=1, source_target_pairs={{384,0},{385,1},{386,2},{387,3},{388,4},{389,5},{390,6},{391,7},{3... | collective-permute-start | bytes 196616 | tf_op jit(solution)/shard_map/ppermute | solution.py:326
  64.7 0.7 collective-permute-start.3
  65.3 1.1 shard_map.113
  66.5 4.8 %collective-permute-done.4 = bf16[256,128]{1,0:T(8,128)(2,1)S(1)} collective-permute-done((bf16[256,128]{1,0:T(8,128)(2,1)S(1)}, bf16[256,128]{1,0:T(8,128)(2,1)S(1)}, u32[]{:S(2)}, u32[]{:S(2)}) %collective-permute-start.4) | collective-permute-done | bytes 65568 | tf_op jit(solution)/shard_map/ppermute | solution.py:326
  71.3 2.4 %all-gather.1 = bf16[1600,256]{1,0:T(8,128)(2,1)S(1)} all-gather(bf16[800,256]{1,0:T(8,128)(2,1)S(1)} %maximum_maximum_fusion), channel_id=3, replica_groups=mesh['x'=4,'y'=4,'c'=2,'key'=16] {'c'}, dimensions={0}, use_global_device_ids=true | all-gather | bytes 1228800 | tf_op jit(solution)/shard_map/all_gather | solution.py:336
  73.7 2.8 %shard_map.116 = (bf16[16,16,256]{2,1,0:T(8,128)(2,1)S(1)}, bf16[256,256]{1,0:T(8,128)(2,1)}, f32[32,1,128]{2,1,0:T(1,128)S(1)}) custom-call(s32[3]{0:T(128)S(1)} %pad_add_fusion.place_ref, bf16[2,800,256]{2,1,0:T(8,128)(2,1)S(1)} %bitcast.17, f32[264,256]{1,0:T(8,128)S(1)} %get-tuple-element.43.end_ref, ...), custom_call_target="tpu_custom_call" | custom-call | flops 400000000 | bytes 3012620 | tf_op jit(solution)/shard_map/pallas_call | solution.py:276
  76.5 13.8 %all_to_all.20.parts_ref = f32[32,1,128]{2,1,0:T(1,128)S(1)} all-to-all(f32[32,1,128]{2,1,0:T(1,128)S(1)} %get-tuple-element.51), channel_id=1, replica_groups=mesh['x'=4,'y'=4,'c'=2,'key'=16] {'x','y','c'}, dimensions={0} | all-to-all | bytes 32768 | tf_op jit(solution)/shard_map/all_to_all | solution.py:347
  90.3 0.1 shard_map.117
  90.4 32.6 %all_to_all.21.back_ref = bf16[16,80,128]{2,1,0:T(8,128)(2,1)S(1)} all-to-all(bf16[16,80,128]{2,1,0:T(8,128)(2,1)S(1)} %shard_map.117), channel_id=1, replica_groups=mesh['x'=4,'y'=4,'c'=2,'key'=16] {'key'}, dimensions={0} | all-to-all | bytes 655360 | tf_op jit(solution)/shard_map/all_to_all | solution.py:292
  122.9 0.7 shard_map.118
  (18 shorter events, 0.1 us)
Async XLA Ops:
  2.3 14.9 %copy-start.5 = (bf16[2,16,16,256]{3,2,1,0:T(8,128)(2,1)S(1)}, bf16[2,16,16,256]{3,2,1,0:T(8,128)(2,1)}, u32[]{:S(2)}) copy-start(bf16[2,16,16,256]{3,2,1,0:T(8,128)(2,1)} %param.15) | copy-start | bytes 786436
  2.3 33.1 %all-to-all-start = ((bf16[16,32,256]{2,1,0:T(8,128)(2,1)}), bf16[16,32,256]{2,1,0:T(8,128)(2,1)S(1)}, u32[]{:S(2)}, u32[]{:S(2)}) async-start(bf16[16,32,256]{2,1,0:T(8,128)(2,1)} %shard_map.111), calls=%async_computation | async-start | bytes 524288 | tf_op jit(solution)/shard_map/all_to_all | solution.py:292
  17.2 18.2 %copy-start = (bf16[2,1,128,128]{3,2,1,0:T(8,128)(2,1)S(1)}, bf16[2,1,128,128]{3,2,1,0:T(8,128)(2,1)}, u32[]{:S(2)}) copy-start(bf16[2,1,128,128]{3,2,1,0:T(8,128)(2,1)} %inv_ref.5) | copy-start | bytes 196612
  17.2 18.1 %copy-start.1 = (bf16[256,1,256]{2,0,1:T(8,128)(2,1)S(1)}, bf16[256,1,256]{2,0,1:T(8,128)(2,1)}, u32[]{:S(2)}) copy-start(bf16[256,1,256]{2,0,1:T(8,128)(2,1)} %param.11) | copy-start | bytes 393220
  17.2 18.1 %copy-start.4 = (f32[1,256]{1,0:T(1,128)S(1)}, f32[1,256]{1,0:T(1,128)}, u32[]{:S(2)}) copy-start(f32[1,256]{1,0:T(1,128)} %rate_ref.5) | copy-start | bytes 3076
  18.0 17.4 %copy-start.3 = (f32[1,256]{1,0:T(1,128)S(1)}, f32[1,256]{1,0:T(1,128)}, u32[]{:S(2)}) copy-start(f32[1,256]{1,0:T(1,128)} %gate_ref.5) | copy-start | bytes 3076
  36.7 8.0 %collective-permute-start = (bf16[272,512]{1,0:T(8,128)(2,1)S(1)}, bf16[272,512]{1,0:T(8,128)(2,1)S(1)}, u32[]{:S(2)}, u32[]{:S(2)}) collective-permute-start(bf16[272,512]{1,0:T(8,128)(2,1)S(1)} %get-tuple-element.34.own_ref), channel_id=1, source_target_pairs={{0,16},{16,0},{1,17},{17,1},{2,18},{18,2},{3,19},{19,3},{4,20},{20... | collective-permute-start | bytes 835592 | tf_op jit(solution)/shard_map/ppermute | solution.py:315
  38.7 26.6 %all-to-all-start.1 = ((bf16[16,2,16,256]{3,2,1,0:T(8,128)(2,1)}), bf16[16,2,16,256]{3,2,1,0:T(8,128)(2,1)S(1)}, u32[]{:S(2)}, u32[]{:S(2)}) async-start(bf16[16,2,16,256]{3,2,1,0:T(8,128)(2,1)} %bitcast.15), calls=%async_computation.1 | async-start | bytes 524288 | tf_op jit(solution)/shard_map/all_to_all | solution.py:292
  59.6 5.8 %copy-start.2 = (bf16[256,1,256]{2,0,1:T(8,128)(2,1)S(1)}, bf16[256,1,256]{2,0,1:T(8,128)(2,1)}, u32[]{:S(2)}) copy-start(bf16[256,1,256]{2,0,1:T(8,128)(2,1)} %param.10) | copy-start | bytes 393220
  60.8 10.5 %collective-permute-start.2 = (bf16[272,256]{1,0:T(8,128)(2,1)S(1)}, bf16[272,256]{1,0:T(8,128)(2,1)S(1)}, u32[]{:S(2)}, u32[]{:S(2)}) collective-permute-start(bf16[272,256]{1,0:T(8,128)(2,1)S(1)} %get-tuple-element.35), channel_id=1, source_target_pairs={{128,0},{256,128},{384,256},{129,1},{257,129},{385,257},{130,2},{2... | collective-permute-start | bytes 417800 | tf_op jit(solution)/shard_map/ppermute | solution.py:325
  62.1 9.2 %collective-permute-start.1 = (bf16[272,256]{1,0:T(8,128)(2,1)S(1)}, bf16[272,256]{1,0:T(8,128)(2,1)S(1)}, u32[]{:S(2)}, u32[]{:S(2)}) collective-permute-start(bf16[272,256]{1,0:T(8,128)(2,1)S(1)} %get-tuple-element.35), channel_id=1, source_target_pairs={{256,0},{257,1},{258,2},{259,3},{260,4},{261,5},{262,6},{263,7},{2... | collective-permute-start | bytes 417800 | tf_op jit(solution)/shard_map/ppermute | solution.py:324
  63.4 7.9 %collective-permute-start.4 = (bf16[256,128]{1,0:T(8,128)(2,1)S(1)}, bf16[256,128]{1,0:T(8,128)(2,1)S(1)}, u32[]{:S(2)}, u32[]{:S(2)}) collective-permute-start(bf16[256,128]{1,0:T(8,128)(2,1)S(1)} %get-tuple-element.36), channel_id=1, source_target_pairs={{384,0},{385,1},{386,2},{387,3},{388,4},{389,5},{390,6},{391,7},{3... | collective-permute-start | bytes 196616 | tf_op jit(solution)/shard_map/ppermute | solution.py:326
  64.7 6.6 %collective-permute-start.3 = (bf16[256,128]{1,0:T(8,128)(2,1)S(1)}, bf16[256,128]{1,0:T(8,128)(2,1)S(1)}, u32[]{:S(2)}, u32[]{:S(2)}) collective-permute-start(bf16[256,128]{1,0:T(8,128)(2,1)S(1)} %get-tuple-element.36), channel_id=1, source_target_pairs={{384,128},{385,129},{386,130},{387,131},{388,132},{389,133},{390,1... | collective-permute-start | bytes 196616 | tf_op jit(solution)/shard_map/ppermute | solution.py:326
